TPU v7x, 32 devices: a whole 2x2x4 slice. The times are simulated.
32 devices in a mesh: phase: 8 (over z, y), sect: 4 (over x, core).
Axes of the slice: x: 2, y: 2, z: 4, core: 2. Of those that a mesh axis runs over, the one named last changes fastest.
Arguments:
- activations: bfloat16 [1024, 32768], P('phase', 'sect'), may hold values from 0 to 2
- block_tiles: bfloat16 [8, 512, 8, 4096], P('phase', 'sect'), may hold values from -0.25 to 0.25
- sources: int32 [8, 512, 8], P('phase', 'sect'), may hold values from 0 to 511, all different within a row
- layer_bias: float32 [8], P('phase'), may hold values from -0.6 to -0.2
Outputs:
- next_acts: bfloat16 [1024, 32768], P('phase', 'sect')
Inputs may be any that keep to these rules, and one draw needn't show every extreme that they name: `sources`: each row of 8 entries names distinct input blocks.
All inputs are finite; a program needn't handle non-finite values.
Results may differ from a plain program's by a relative error of at most 0.0055.
Values may be sent and summed in bfloat16 or wider, within the bound.
No kernel may reach another device: no remote copies, remote signals or barrier semaphores. Data moves between devices by JAX's collectives and lax.ppermute only.
A program may use at most 128 MiB of HBM per device.

v0:
```python
import jax
import jax.numpy as jnp
from jax import lax
from jax.sharding import PartitionSpec as P

BLK = 64


def from_behind(array, axis, by):
    size = lax.axis_size(axis)
    return lax.ppermute(array, axis, [(i, (i + by) % size) for i in range(size)])


def contract_picked(picked, block_tiles, sources):
    row_count = picked.shape[0]
    weights = block_tiles[0].reshape(sources.shape[1], sources.shape[2], BLK, BLK)
    summed = jnp.einsum("rjki,jkio->rjo", picked, weights, preferred_element_type=jnp.float32)
    return summed.reshape(row_count, -1)


def block_products(gathered, block_tiles, sources):
    row_count = gathered.shape[0]
    blocks = gathered.reshape(row_count, -1, BLK)
    picked = jnp.take(blocks, sources[0], axis=1)
    return contract_picked(picked, block_tiles, sources)


def activate(summed, layer_bias):
    return jax.nn.relu(summed + layer_bias[0]).astype(jnp.bfloat16)


def apply_layer(quarter, block_tiles, sources, layer_bias):
    gathered = lax.all_gather(quarter, "sect", axis=1, tiled=True)
    summed = block_products(gathered, block_tiles, sources)
    return activate(summed, layer_bias)


def per_device(activations, block_tiles, sources, layer_bias):
    quarter = activations
    result = apply_layer(quarter, block_tiles, sources, layer_bias)
    spread = lax.all_gather(result, "sect", axis=1, tiled=True)
    moved = from_behind(spread, "phase", 1)
    result = activate(block_products(moved, block_tiles, sources), layer_bias)
    quarter = from_behind(result, "phase", 1)
    return quarter


def solution(mesh):
    in_specs = (
        P("phase", "sect"),
        P("phase", "sect", None, None),
        P("phase", "sect", None),
        P("phase"),
    )
    out_specs = P("phase", "sect")
    return jax.shard_map(
        per_device, mesh=mesh, in_specs=in_specs, out_specs=out_specs, check_vma=False
    )
```

profile of v0, /device:TPU:0, one launch (start us, length us, event | category | flops | bytes accessed | tf_op | source)
XLA Modules:
  0.0 439.8 jit_solution(7372058034644755928)
XLA Ops:
  6.5 0.0 all-gather.3.cloned.1.call-start
  6.5 4.1 copy.13
  10.6 0.0 all-gather.3.cloned.1.call-update
  10.6 0.0 all-gather.5.cloned.1.call-start
  11.3 0.7 compare_and_fusion
  12.0 0.1 copy.11
  12.1 0.7 compare_select_fusion
  12.8 0.1 copy.14
  12.9 0.1 reshape.45
  13.0 12.8 %copy.15 = bf16[1,128,8,4096]{1,3,2,0:T(8,128)(2,1)} copy(bf16[1,128,8,4096]{3,2,1,0:T(8,128)(2,1)} %param.7) | data formatting | bytes 16777216 | tf_op args[1]
  25.8 29.2 %copy.16 = bf16[128,8,64,64]{2,3,1,0:T(8,128)(2,1)} copy(bf16[128,8,64,64]{0,3,2,1:T(8,128)(2,1)} %bitcast.47) | data formatting | bytes 16777216 | tf_op jit(solution)/shard_map/reshape;squeeze | solution.py:16
  55.0 16.7 %all-gather.3.cloned.1.call-done = bf16[128,32768]{0,1:T(8,128)(2,1)} async-done(((bf16[128,8192]{0,1:T(8,128)(2,1)}), bf16[128,32768]{0,1:T(8,128)(2,1)}) %all-gather.3.cloned.1.call-update) | async-done | bytes 8388624 | tf_op jit(solution)/shard_map/all_gather | solution.py:33
  71.8 16.8 %gather_fusion = bf16[1024,128,64]{1,2,0:T(8,128)(2,1)} fusion(bf16[128,512,64]{0,2,1:T(8,128)(2,1)} %bitcast.44, s32[1024]{0:T(1024)S(1)} %broadcast_clamp_fusion), kind=kCustom, calls=%fused_computation.clone | custom fusion | bytes 33558528 | tf_op jit(solution)/shard_map/jit(_take)/gather | solution.py:24
  88.6 15.3 %fusion.13 = bf16[128,128,64]{1,2,0:T(8,128)(2,1)} fusion(bf16[128,8,64,64]{2,3,1,0:T(8,128)(2,1)} %copy.16, bf16[128,8,128,64]{2,3,1,0:T(8,128)(2,1)} %bitcast.46, pred[128,8]{1,0:T(8,128)(4,1)S(1)} %copy.11, f32[]{:T(128)} %bitcast.42), kind=kOutput, calls=%fused_computation.17 | convolution fusion | flops 1085276160 | bytes 27264004 | tf_op jit(solution)/shard_map/rjki,jkio->rjo/dot_general | solution.py:17
  103.9 0.0 all-gather.5.cloned.1.call-update
  104.0 58.4 %all-gather.5.cloned.1.call-done = bf16[128,32768]{0,1:T(8,128)(2,1)} async-done(((bf16[128,8192]{0,1:T(8,128)(2,1)}), bf16[128,32768]{0,1:T(8,128)(2,1)}) %all-gather.5.cloned.1.call-update) | async-done | bytes 8388624 | tf_op jit(solution)/shard_map/all_gather | solution.py:41
  162.4 1.5 collective-permute-start
  163.9 184.2 %collective-permute-done = bf16[128,32768]{0,1:T(8,128)(2,1)} collective-permute-done((bf16[128,32768]{0,1:T(8,128)(2,1)}, bf16[128,32768]{0,1:T(8,128)(2,1)}, u32[]{:S(2)}, u32[]{:S(2)}) %collective-permute-start) | collective-permute-done | bytes 8388640 | tf_op jit(solution)/shard_map/ppermute | solution.py:11
  348.0 16.8 %gather_fusion.1 = bf16[1024,128,64]{1,2,0:T(8,128)(2,1)} fusion(bf16[128,512,64]{0,2,1:T(8,128)(2,1)} %bitcast.10, s32[1024]{0:T(1024)S(1)} %broadcast_clamp_fusion), kind=kCustom, calls=%fused_computation.1.clone | custom fusion | bytes 33558528 | tf_op jit(solution)/shard_map/jit(_take)/gather | solution.py:24
  364.9 14.0 %fusion.11 = bf16[128,128,64]{1,2,0:T(8,128)(2,1)S(1)} fusion(bf16[128,8,64,64]{2,3,1,0:T(8,128)(2,1)} %copy.16, bf16[128,8,128,64]{2,3,1,0:T(8,128)(2,1)} %bitcast.45, pred[128,8]{1,0:T(8,128)(4,1)S(1)} %copy.11, f32[]{:T(128)} %bitcast.43), kind=kOutput, calls=%fused_computation.14 | convolution fusion | flops 1085276160 | bytes 27264004 | tf_op jit(solution)/shard_map/rjki,jkio->rjo/dot_general | solution.py:17
  378.9 2.9 copy.19
  381.8 0.0 collective-permute-start.1
  381.8 49.9 %collective-permute-done.1 = bf16[128,8192]{1,0:T(8,128)(2,1)S(1)} collective-permute-done((bf16[128,8192]{1,0:T(8,128)(2,1)}, bf16[128,8192]{1,0:T(8,128)(2,1)S(1)}, u32[]{:S(2)}, u32[]{:S(2)}) %collective-permute-start.1) | collective-permute-done | bytes 2097184 | tf_op jit(solution)/shard_map/ppermute | solution.py:11
  431.7 1.3 copy.24
  (1 shorter events, 0.0 us)
Async XLA Ops:
  6.5 65.2 %all-gather.3.cloned.1.call-start = ((), (), s32[]{:S(2)}) async-start(), calls=%async_computation | async-start | bytes 10485760 | tf_op jit(solution)/shard_map/all_gather | solution.py:33
  10.6 151.8 %all-gather.5.cloned.1.call-start = ((), (), s32[]{:S(2)}) async-start(), calls=%async_computation.1 | async-start | bytes 10485760 | tf_op jit(solution)/shard_map/all_gather | solution.py:41
  162.4 185.6 %collective-permute-start = (bf16[128,32768]{0,1:T(8,128)(2,1)}, bf16[128,32768]{0,1:T(8,128)(2,1)}, u32[]{:S(2)}, u32[]{:S(2)}) collective-permute-start(bf16[128,32768]{0,1:T(8,128)(2,1)} %all-gather.5.cloned.1.call-done), channel_id=1, source_target_pairs={{0,4},{4,8},{8,12},{12,16},{16,20},{20,24},{24,28},{28,0},{1,5},{5... | collective-permute-start | bytes 25165832 | tf_op jit(solution)/shard_map/ppermute | solution.py:11
  381.8 49.9 %collective-permute-start.1 = (bf16[128,8192]{1,0:T(8,128)(2,1)}, bf16[128,8192]{1,0:T(8,128)(2,1)S(1)}, u32[]{:S(2)}, u32[]{:S(2)}) collective-permute-start(bf16[128,8192]{1,0:T(8,128)(2,1)} %copy.19), channel_id=1, source_target_pairs={{0,4},{4,8},{8,12},{12,16},{16,20},{20,24},{24,28},{28,0},{1,5},{5... | collective-permute-start | bytes 6291464 | tf_op jit(solution)/shard_map/ppermute | solution.py:11
Sparse Core Ops, SparseCore 0:
  10.7 60.9 all-gather.2
  104.1 58.2 all-gather.4
where the time goes:
time: 440 us
  waiting for transfers between devices  309 us (70%)
  local copies, waits for them, and re-layouts  84.2 us (19%)
  matrix products  29.4 us (7%)
  between operations  14.1 us (3%)
    ppermute x2, waiting for transfers between devices, from_behind(): lax.ppermute(array, axis, [(i, (i + by) % size) for i in range(size)])  234 us
    all_gather x1, waiting for transfers between devices, per_device(): spread = lax.all_gather(result, 'sect', axis=1, tiled=True)  58.4 us
    gather x2, local copies, waits for them, and re-layouts, block_products(): picked = jnp.take(blocks, sources[0], axis=1)  33.6 us
    dot_general x2, matrix products, contract_picked(): jnp.einsum('rjki,jkio->rjo', picked, weights, preferred_element_type=jnp....  29.4 us
    another operation x1, local copies, waits for them, and re-layouts, contract_picked(): block_tiles[0].reshape(sources.shape[1], sources.shape[2], BLK, BLK)  29.2 us
    unnamed x3, local copies, waits for them, and re-layouts  18.1 us
    all_gather x1, waiting for transfers between devices, apply_layer(): gathered = lax.all_gather(quarter, 'sect', axis=1, tiled=True)  16.7 us
  transfers between devices with their start and end apart: 4, of which 4 were waited for; matrix products, arithmetic and copies ran while one was open for 10% of the time, Pallas kernels for 0%

commit v1 on v0

v1 whole, which is shorter than its diff:
```python
import functools

import jax
import jax.numpy as jnp
from jax import lax
from jax.experimental import pallas as pl
from jax.experimental.pallas import tpu as pltpu
from jax.sharding import PartitionSpec as P

BLK = 64
LANES = 128
WIDE = 4
CHUNKS = (32, 32, 32, 32)
MIB = 1 << 20


def arrange_body(groups, tiles_ref, out_ref, order_ref):
    fanin = tiles_ref.shape[1]
    depth = fanin * BLK
    half = depth // 2

    @pl.when(pl.program_id(0) == 0)
    def _():
        row = lax.broadcasted_iota(jnp.int32, (depth, depth), 0)
        column = lax.broadcasted_iota(jnp.int32, (depth, depth), 1)
        neuron = row % BLK
        origin = (neuron % 2) * half + (neuron // 2) * fanin + row // BLK
        order_ref[...] = jnp.where(column == origin, 1.0, 0.0).astype(jnp.bfloat16)

    low = lax.broadcasted_iota(jnp.int32, (half, LANES), 1) < BLK
    for group in range(groups):
        stacked = []
        for member in range(WIDE):
            flat = tiles_ref[group * WIDE + member].astype(jnp.float32)
            stacked.append(jnp.concatenate([flat[:, t * LANES:(t + 1) * LANES] for t in range(half // fanin)], axis=0))
        even, odd = [], []
        for pair in range(WIDE // 2):
            first, second = stacked[2 * pair], stacked[2 * pair + 1]
            even.append(jnp.where(low, first, pltpu.roll(second, BLK, axis=1)).astype(jnp.bfloat16))
            odd.append(jnp.where(low, pltpu.roll(first, BLK, axis=1), second).astype(jnp.bfloat16))
        mixed = jnp.concatenate([jnp.concatenate(even, axis=1), jnp.concatenate(odd, axis=1)], axis=0)
        out_ref[group] = jnp.dot(order_ref[...], mixed, preferred_element_type=jnp.float32).astype(jnp.bfloat16)


def arrange_weights(block_tiles):
    _, blocks, fanin, flat = block_tiles.shape
    groups = 4
    depth = fanin * BLK
    tiles = block_tiles.reshape(blocks, fanin, flat)
    return pl.pallas_call(
        functools.partial(arrange_body, groups),
        grid=(blocks // (WIDE * groups),),
        in_specs=[pl.BlockSpec((WIDE * groups, fanin, flat), lambda i: (i, 0, 0))],
        out_specs=pl.BlockSpec((groups, depth, WIDE * BLK), lambda i: (i, 0, 0)),
        out_shape=jax.ShapeDtypeStruct((blocks // WIDE, depth, WIDE * BLK), jnp.bfloat16),
        scratch_shapes=[pltpu.VMEM((depth, depth), jnp.bfloat16)],
        compiler_params=pltpu.CompilerParams(vmem_limit_bytes=24 * MIB),
        cost_estimate=pl.CostEstimate(flops=2 * blocks * depth * depth * BLK, bytes_accessed=4 * blocks * depth * BLK, transcendentals=0),
        name="arrange_weights",
    )(tiles)


def layer_body(groups, parts, place_ref, bias_ref, *refs):
    part_refs, (weight_ref, out_ref, tile_ref, lhs_ref) = refs[:parts], refs[parts:]
    rows, columns = part_refs[0].shape
    per_part = columns // LANES
    turned = parts * per_part
    step = pl.program_id(0)
    fanin = weight_ref.shape[1] // BLK

    @pl.when(step == 0)
    def _():
        for part, ref in enumerate(part_refs):
            for t in range(per_part):
                tile = ref[:, t * LANES:(t + 1) * LANES]
                tile_ref[part * per_part + t] = tile
                tile_ref[turned + part * per_part + t] = jnp.concatenate([tile[:, BLK:], tile[:, :BLK]], axis=1)

    low = lax.broadcasted_iota(jnp.int32, (rows, LANES), 1) < BLK
    bias = bias_ref[0]
    for group in range(groups):
        stacked = []
        for member in range(WIDE):
            base = ((step * groups + group) * WIDE + member) * fanin
            picked = []
            for k in range(0, fanin, 2):
                left = tile_ref[place_ref[base + k]]
                right = tile_ref[place_ref[base + k + 1]]
                picked.append(jnp.where(low, left, right))
            stacked.append(jnp.concatenate(picked, axis=1))
        lhs = jnp.concatenate(stacked, axis=0)
        sums = jnp.dot(lhs, weight_ref[group], preferred_element_type=jnp.float32)
        for pair in range(WIDE // 2):
            lanes = slice(pair * LANES, (pair + 1) * LANES)
            first = sums[2 * pair * rows:(2 * pair + 1) * rows, lanes]
            second = sums[(2 * pair + 1) * rows:(2 * pair + 2) * rows, lanes]
            result = jnp.maximum(jnp.where(low, first, second) + bias, 0.0)
            start = (group * (WIDE // 2) + pair) * LANES
            out_ref[:, start:start + LANES] = result.astype(jnp.bfloat16)


def apply_layer(parts, weights, places, layer_bias):
    rows, columns = parts[0].shape
    total, depth, width = weights.shape
    groups = 4
    tiles = len(parts) * columns // LANES
    whole = pl.BlockSpec((rows, columns), lambda i: (0, 0), pipeline_mode=pl.Buffered(1))
    return pl.pallas_call(
        functools.partial(layer_body, groups, len(parts)),
        grid=(total // groups,),
        in_specs=[pl.BlockSpec(memory_space=pltpu.SMEM), pl.BlockSpec(memory_space=pltpu.SMEM)]
        + [whole] * len(parts)
        + [pl.BlockSpec((groups, depth, width), lambda i: (i, 0, 0))],
        out_specs=pl.BlockSpec((rows, groups * width), lambda i: (0, i)),
        out_shape=jax.ShapeDtypeStruct((rows, total * width), jnp.bfloat16),
        scratch_shapes=[pltpu.VMEM((2 * tiles, rows, LANES), jnp.bfloat16), pltpu.VMEM((WIDE * rows, depth), jnp.bfloat16)],
        compiler_params=pltpu.CompilerParams(vmem_limit_bytes=24 * MIB),
        cost_estimate=pl.CostEstimate(
            flops=2 * rows * total * depth * width,
            bytes_accessed=2 * total * depth * width + 2 * rows * columns * (len(parts) + 1),
            transcendentals=0,
        ),
        name="apply_layer",
    )(places, layer_bias, *parts, weights)


def from_behind(array, axis, by):
    size = lax.axis_size(axis)
    return lax.ppermute(array, axis, [(i, (i + by) % size) for i in range(size)])


def swapped(array, axis, bit):
    return lax.ppermute(array, axis, [(i, i ^ bit) for i in range(lax.axis_size(axis))])


def distances(size):
    held, bit = [0], size // 2
    while bit:
        held, bit = held + [d ^ bit for d in held], bit // 2
    return held


def gather_parts(part):
    held, bit = [part], lax.axis_size("sect") // 2
    while bit:
        held, bit = held + [swapped(h, "sect", bit) for h in held], bit // 2
    return held


def block_places(sources, per_part):
    size = lax.axis_size("sect")
    me = lax.axis_index("sect")
    order = distances(size)
    distance = (sources // per_part) ^ me
    slot = jnp.zeros_like(distance)
    for position, d in enumerate(order):
        slot = jnp.where(distance == d, position, slot)
    inside = sources % per_part
    tile = slot * (per_part // 2) + inside // 2
    position = lax.broadcasted_iota(jnp.int32, sources.shape, sources.ndim - 1)
    return (tile + jnp.where(inside % 2 == position % 2, 0, size * per_part // 2)).reshape(-1)


def per_device(activations, block_tiles, sources, layer_bias):
    places = block_places(sources[0], activations.shape[1] // BLK)
    starts = [sum(CHUNKS[:c]) for c in range(len(CHUNKS))]
    weights = arrange_weights(block_tiles)
    chunks = [activations[s:s + r] for s, r in zip(starts, CHUNKS)]
    for tick in range(2):
        gathered = [gather_parts(chunk) for chunk in chunks]
        hidden = [apply_layer(parts, weights, places, layer_bias) for parts in gathered]
        chunks = [from_behind(h, "phase", 1) for h in hidden]
    return jnp.concatenate(chunks, axis=0)


def solution(mesh):
    in_specs = (
        P("phase", "sect"),
        P("phase", "sect", None, None),
        P("phase", "sect", None),
        P("phase"),
    )
    out_specs = P("phase", "sect")
    return jax.shard_map(
        per_device, mesh=mesh, in_specs=in_specs, out_specs=out_specs, check_vma=False
    )
```

time: 440 us -> 189 us (0.43)
  waiting for transfers between devices: 309 us -> 111 us
  local copies, waits for them, and re-layouts: 84.2 us -> 6.13 us
  Pallas kernels: 0 us -> 43.6 us
  matrix products: 29.4 us -> 0 us
  starting transfers between devices: 1.52 us -> 25.3 us
  between operations: 14.1 us -> 0.83 us
    ppermute x2 -> x8, waiting for transfers between devices: 234 us -> 59.9 us  [from_behind(): lax.ppermute(array, axis, [(i, (i + by) % size) for i in range(size)])]
    all_gather x2 -> x0, waiting for transfers between devices: 75.2 us -> none  [the longest x1 58.4 us: per_device(): spread = lax.all_gather(result, 'sect', axis=1, tiled=True)]
    ppermute x0 -> x24, waiting for transfers between devices: none -> 51.2 us  [swapped(): lax.ppermute(array, axis, [(i, i ^ bit) for i in range(lax.axis_size(axis...]
    pallas_call x0 -> x9, Pallas kernels: none -> 43.6 us  [the longest x8 36.6 us: apply_layer(): pl.pallas_call(functools.partial(layer_body, groups, len(parts)), grid=(t...]
    gather x2 -> x0, local copies, waits for them, and re-layouts: 33.6 us -> none  [block_products(): picked = jnp.take(blocks, sources[0], axis=1)]
    dot_general x2 -> x0, matrix products: 29.4 us -> none  [contract_picked(): jnp.einsum('rjki,jkio->rjo', picked, weights, preferred_element_type=jnp....]
    another operation x1 -> x0, local copies, waits for them, and re-layouts: 29.2 us -> none  [contract_picked(): block_tiles[0].reshape(sources.shape[1], sources.shape[2], BLK, BLK)]
    ppermute x0 -> x24, starting transfers between devices: none -> 14.7 us  [swapped(): lax.ppermute(array, axis, [(i, i ^ bit) for i in range(lax.axis_size(axis...]
  transfers between devices with their start and end apart: 4 -> 32, of which waited for: 4 -> 13; matrix products, arithmetic and copies ran while one was open for 10% -> 0% of each run, Pallas kernels for 0% -> 23%
where the time goes in v1:
time: 189 us
  waiting for transfers between devices  111 us (59%)
  Pallas kernels  43.6 us (23%)
  starting transfers between devices  25.3 us (13%)
  local copies, waits for them, and re-layouts  6.13 us (3%)
    ppermute x8, waiting for transfers between devices, from_behind(): lax.ppermute(array, axis, [(i, (i + by) % size) for i in range(size)])  59.9 us
    ppermute x24, waiting for transfers between devices, swapped(): lax.ppermute(array, axis, [(i, i ^ bit) for i in range(lax.axis_size(axis...  51.2 us
    pallas_call x8, Pallas kernels, apply_layer(): pl.pallas_call(functools.partial(layer_body, groups, len(parts)), grid=(t...  36.6 us
    ppermute x24, starting transfers between devices, swapped(): lax.ppermute(array, axis, [(i, i ^ bit) for i in range(lax.axis_size(axis...  14.7 us
    ppermute x8, starting transfers between devices, from_behind(): lax.ppermute(array, axis, [(i, (i + by) % size) for i in range(size)])  10.6 us
    pallas_call x1, Pallas kernels, arrange_weights(): pl.pallas_call(functools.partial(arrange_body, groups), grid=(blocks // (...  6.94 us
    unnamed x9, local copies, waits for them, and re-layouts  4.28 us
  transfers between devices with their start and end apart: 32, of which 13 were waited for; matrix products, arithmetic and copies ran while one was open for 0% of the time, Pallas kernels for 23%

profile of v1, /device:TPU:0, one launch (start us, length us, event | category | flops | bytes accessed | tf_op | source)
XLA Modules:
  0.0 188.5 jit_solution(4487201141767359331)
XLA Ops:
  0.0 1.7 fusion.7
  1.7 3.0 %collective-permute-start = (bf16[32,8192]{1,0:T(8,128)(2,1)S(1)}, bf16[32,8192]{1,0:T(8,128)(2,1)}, u32[]{:S(2)}, u32[]{:S(2)}) collective-permute-start(bf16[32,8192]{1,0:T(8,128)(2,1)S(1)} %get-tuple-element.5.refs_0_), channel_id=1, source_target_pairs={{0,2},{1,3},{2,0},{3,1},{4,6},{5,7},{6,4},{7,5},{8,10},{9,11},{10,... | collective-permute-start | bytes 1572872 | tf_op jit(solution)/shard_map/ppermute | solution.py:133
  4.7 0.0 collective-permute-start.1
  4.7 0.2 collective-permute-start.8
  4.8 0.4 collective-permute-start.9
  5.2 1.7 collective-permute-start.16
  6.9 10.6 %collective-permute-done.refs_1_ = bf16[32,8192]{1,0:T(8,128)(2,1)} collective-permute-done((bf16[32,8192]{1,0:T(8,128)(2,1)S(1)}, bf16[32,8192]{1,0:T(8,128)(2,1)}, u32[]{:S(2)}, u32[]{:S(2)}) %collective-permute-start) | collective-permute-done | bytes 524320 | tf_op jit(solution)/shard_map/ppermute | solution.py:133
  17.5 2.1 %collective-permute-start.24 = (bf16[32,8192]{1,0:T(8,128)(2,1)S(1)}, bf16[32,8192]{1,0:T(8,128)(2,1)S(1)}, u32[]{:S(2)}, u32[]{:S(2)}) collective-permute-start(bf16[32,8192]{1,0:T(8,128)(2,1)S(1)} %get-tuple-element.7.refs_0_), channel_id=1, source_target_pairs={{0,2},{1,3},{2,0},{3,1},{4,6},{5,7},{6,4},{7,5},{8,10},{9,11},{10,... | collective-permute-start | bytes 1572872 | tf_op jit(solution)/shard_map/ppermute | solution.py:133
  19.6 0.8 copy-done.1
  20.4 0.0 collective-permute-start.2
  20.4 0.1 select_n.58
  20.5 0.1 copy.5
  20.6 0.1 squeeze.3
  20.7 8.1 %collective-permute-done.8.refs_1_ = bf16[32,8192]{1,0:T(8,128)(2,1)} collective-permute-done((bf16[32,8192]{1,0:T(8,128)(2,1)S(1)}, bf16[32,8192]{1,0:T(8,128)(2,1)}, u32[]{:S(2)}, u32[]{:S(2)}) %collective-permute-start.8) | collective-permute-done | bytes 524320 | tf_op jit(solution)/shard_map/ppermute | solution.py:133
  28.8 3.4 %copy-done = bf16[1,128,8,4096]{3,2,1,0:T(8,128)(2,1)S(1)} copy-done((bf16[1,128,8,4096]{3,2,1,0:T(8,128)(2,1)S(1)}, bf16[1,128,8,4096]{3,2,1,0:T(8,128)(2,1)}, u32[]{:S(2)}) %copy-start) | copy-done | bytes 8388632
  32.2 6.9 %arrange_weights.1.refs_4_ = bf16[32,512,256]{2,1,0:T(8,128)(2,1)S(1)} custom-call(bf16[128,8,4096]{2,1,0:T(8,128)(2,1)S(1)} %bitcast.1), custom_call_target="tpu_custom_call" | custom-call | flops 4294967296 | bytes 16777216 | tf_op jit(solution)/shard_map/arrange_weights/pallas_call | solution.py:50
  39.1 0.0 collective-permute-done.9.refs_2_
  39.1 0.6 collective-permute-start.17
  39.7 0.2 collective-permute-done.16.refs_1_
  39.9 10.4 %collective-permute-done.24.refs_1_ = bf16[32,8192]{1,0:T(8,128)(2,1)S(1)} collective-permute-done((bf16[32,8192]{1,0:T(8,128)(2,1)S(1)}, bf16[32,8192]{1,0:T(8,128)(2,1)S(1)}, u32[]{:S(2)}, u32[]{:S(2)}) %collective-permute-start.24) | collective-permute-done | bytes 524320 | tf_op jit(solution)/shard_map/ppermute | solution.py:133
  50.3 0.5 collective-permute-start.26
  51.5 5.1 %apply_layer.8 = bf16[32,8192]{1,0:T(8,128)(2,1)S(1)} custom-call(s32[1024]{0:T(1024)S(1)} %fusion.2.place_ref, f32[1]{0:T(128)S(6)} %copy.6.bias_ref, bf16[32,8192]{1,0:T(8,128)(2,1)S(1)} %get-tuple-element.5.refs_0_, bf16[32,8192]{1,0:T(8,128)(2,1)} %collective-permute-done.refs_1_, bf16[32,8192]{1,0:T(8,128)(2,1)S(1)} %copy-done.2, ...), custom_call_target="tpu_custom_call" | custom-call | flops 268435456 | bytes 11010048 | tf_op jit(solution)/shard_map/apply_layer/pallas_call | solution.py:108
  56.6 0.0 collective-permute-done.10.refs_3_
  56.6 1.8 collective-permute-start.3
  58.4 5.1 %apply_layer.10 = bf16[32,8192]{1,0:T(8,128)(2,1)S(1)} custom-call(s32[1024]{0:T(1024)S(1)} %fusion.2.place_ref, f32[1]{0:T(128)S(6)} %copy.6.bias_ref, bf16[32,8192]{1,0:T(8,128)(2,1)S(1)} %get-tuple-element.6.refs_0_, bf16[32,8192]{1,0:T(8,128)(2,1)} %collective-permute-done.8.refs_1_, bf16[32,8192]{1,0:T(8,128)(2,1)} %collective-permute-done.9.refs_2_, ...), custom_call_target="tpu_custom_call" | custom-call | flops 268435456 | bytes 11010048 | tf_op jit(solution)/shard_map/apply_layer/pallas_call | solution.py:108
  63.5 0.0 collective-permute-done.17.refs_2_
  63.5 1.6 collective-permute-start.11
  65.1 0.0 collective-permute-done.18.refs_3_
  65.1 4.4 %apply_layer.12 = bf16[32,8192]{1,0:T(8,128)(2,1)S(1)} custom-call(s32[1024]{0:T(1024)S(1)} %fusion.2.place_ref, f32[1]{0:T(128)S(6)} %copy.6.bias_ref, bf16[32,8192]{1,0:T(8,128)(2,1)S(1)} %get-tuple-element.8.refs_0_, bf16[32,8192]{1,0:T(8,128)(2,1)S(1)} %collective-permute-done.16.refs_1_, bf16[32,8192]{1,0:T(8,128)(2,1)S(1)} %collective-permute-done.17.refs_2_, ...), custom_call_target="tpu_custom_call" | custom-call | flops 268435456 | bytes 11010048 | tf_op jit(solution)/shard_map/apply_layer/pallas_call | solution.py:108
  69.5 1.6 collective-permute-start.19
  71.1 0.0 collective-permute-done.25.refs_2_
  71.1 0.0 collective-permute-done.26.refs_3_
  71.1 4.4 %apply_layer.14 = bf16[32,8192]{1,0:T(8,128)(2,1)S(1)} custom-call(s32[1024]{0:T(1024)S(1)} %fusion.2.place_ref, f32[1]{0:T(128)S(6)} %copy.6.bias_ref, bf16[32,8192]{1,0:T(8,128)(2,1)S(1)} %get-tuple-element.7.refs_0_, bf16[32,8192]{1,0:T(8,128)(2,1)S(1)} %collective-permute-done.24.refs_1_, bf16[32,8192]{1,0:T(8,128)(2,1)S(1)} %collective-permute-done.25.refs_2_, ...), custom_call_target="tpu_custom_call" | custom-call | flops 268435456 | bytes 11010048 | tf_op jit(solution)/shard_map/apply_layer/pallas_call | solution.py:108
  75.5 1.6 collective-permute-start.27
  77.1 0.0 collective-permute-done.3.refs_0_
  77.1 1.5 collective-permute-start.4
  78.5 0.0 collective-permute-start.5
  78.5 6.9 %collective-permute-done.11.refs_0_ = bf16[32,8192]{1,0:T(8,128)(2,1)S(1)} collective-permute-done((bf16[32,8192]{1,0:T(8,128)(2,1)S(1)}, bf16[32,8192]{1,0:T(8,128)(2,1)S(1)}, u32[]{:S(2)}, u32[]{:S(2)}) %collective-permute-start.11) | collective-permute-done | bytes 524320 | tf_op jit(solution)/shard_map/ppermute | solution.py:129
  85.4 1.7 collective-permute-start.12
  87.1 9.6 %collective-permute-done.19.refs_0_ = bf16[32,8192]{1,0:T(8,128)(2,1)S(1)} collective-permute-done((bf16[32,8192]{1,0:T(8,128)(2,1)S(1)}, bf16[32,8192]{1,0:T(8,128)(2,1)S(1)}, u32[]{:S(2)}, u32[]{:S(2)}) %collective-permute-start.19) | collective-permute-done | bytes 524320 | tf_op jit(solution)/shard_map/ppermute | solution.py:129
  96.7 0.0 collective-permute-start.13
  96.7 10.6 %collective-permute-done.27.refs_0_ = bf16[32,8192]{1,0:T(8,128)(2,1)S(1)} collective-permute-done((bf16[32,8192]{1,0:T(8,128)(2,1)S(1)}, bf16[32,8192]{1,0:T(8,128)(2,1)S(1)}, u32[]{:S(2)}, u32[]{:S(2)}) %collective-permute-start.27) | collective-permute-done | bytes 524320 | tf_op jit(solution)/shard_map/ppermute | solution.py:129
  107.3 1.5 collective-permute-start.20
  108.8 0.0 collective-permute-done.4.refs_1_
  108.8 0.5 collective-permute-start.28
  109.3 0.0 collective-permute-done.5.refs_2_
  109.3 0.5 collective-permute-start.14
  109.8 0.1 collective-permute-start.21
  109.9 12.2 %collective-permute-done.20.refs_1_ = bf16[32,8192]{1,0:T(8,128)(2,1)S(1)} collective-permute-done((bf16[32,8192]{1,0:T(8,128)(2,1)S(1)}, bf16[32,8192]{1,0:T(8,128)(2,1)S(1)}, u32[]{:S(2)}, u32[]{:S(2)}) %collective-permute-start.20) | collective-permute-done | bytes 524320 | tf_op jit(solution)/shard_map/ppermute | solution.py:133
  122.1 9.7 %collective-permute-done.28.refs_1_ = bf16[32,8192]{1,0:T(8,128)(2,1)S(1)} collective-permute-done((bf16[32,8192]{1,0:T(8,128)(2,1)S(1)}, bf16[32,8192]{1,0:T(8,128)(2,1)S(1)}, u32[]{:S(2)}, u32[]{:S(2)}) %collective-permute-start.28) | collective-permute-done | bytes 524320 | tf_op jit(solution)/shard_map/ppermute | solution.py:133
  131.8 0.5 collective-permute-start.30
  132.3 4.4 %apply_layer.9 = bf16[32,8192]{1,0:T(8,128)(2,1)S(1)} custom-call(s32[1024]{0:T(1024)S(1)} %fusion.2.place_ref, f32[1]{0:T(128)S(6)} %copy.6.bias_ref, bf16[32,8192]{1,0:T(8,128)(2,1)S(1)} %collective-permute-done.3.refs_0_, bf16[32,8192]{1,0:T(8,128)(2,1)S(1)} %collective-permute-done.4.refs_1_, bf16[32,8192]{1,0:T(8,128)(2,1)S(1)} %collective-permute-done.5.refs_2_, ...), custom_call_target="tpu_custom_call" | custom-call | flops 268435456 | bytes 11010048 | tf_op jit(solution)/shard_map/apply_layer/pallas_call | solution.py:108
  136.7 0.1 collective-permute-start.7
  136.8 4.4 %apply_layer.11 = bf16[32,8192]{1,0:T(8,128)(2,1)S(1)} custom-call(s32[1024]{0:T(1024)S(1)} %fusion.2.place_ref, f32[1]{0:T(128)S(6)} %copy.6.bias_ref, bf16[32,8192]{1,0:T(8,128)(2,1)S(1)} %collective-permute-done.11.refs_0_, bf16[32,8192]{1,0:T(8,128)(2,1)S(1)} %collective-permute-done.12.refs_1_, bf16[32,8192]{1,0:T(8,128)(2,1)S(1)} %collective-permute-done.13.refs_2_, ...), custom_call_target="tpu_custom_call" | custom-call | flops 268435456 | bytes 11010048 | tf_op jit(solution)/shard_map/apply_layer/pallas_call | solution.py:108
  141.3 0.9 collective-permute-start.15
  142.1 4.4 %apply_layer.13 = bf16[32,8192]{1,0:T(8,128)(2,1)S(1)} custom-call(s32[1024]{0:T(1024)S(1)} %fusion.2.place_ref, f32[1]{0:T(128)S(6)} %copy.6.bias_ref, bf16[32,8192]{1,0:T(8,128)(2,1)S(1)} %collective-permute-done.19.refs_0_, bf16[32,8192]{1,0:T(8,128)(2,1)S(1)} %collective-permute-done.20.refs_1_, bf16[32,8192]{1,0:T(8,128)(2,1)S(1)} %collective-permute-done.21.refs_2_, ...), custom_call_target="tpu_custom_call" | custom-call | flops 268435456 | bytes 11010048 | tf_op jit(solution)/shard_map/apply_layer/pallas_call | solution.py:108
  146.5 0.7 collective-permute-start.23
  147.2 4.4 %apply_layer.15 = bf16[32,8192]{1,0:T(8,128)(2,1)S(1)} custom-call(s32[1024]{0:T(1024)S(1)} %fusion.2.place_ref, f32[1]{0:T(128)S(6)} %copy.6.bias_ref, bf16[32,8192]{1,0:T(8,128)(2,1)S(1)} %collective-permute-done.27.refs_0_, bf16[32,8192]{1,0:T(8,128)(2,1)S(1)} %collective-permute-done.28.refs_1_, bf16[32,8192]{1,0:T(8,128)(2,1)S(1)} %collective-permute-done.29.refs_2_, ...), custom_call_target="tpu_custom_call" | custom-call | flops 268435456 | bytes 11010048 | tf_op jit(solution)/shard_map/apply_layer/pallas_call | solution.py:108
  151.6 2.5 %collective-permute-start.31 = (bf16[32,8192]{1,0:T(8,128)(2,1)S(1)}, bf16[32,8192]{1,0:T(8,128)(2,1)S(1)}, u32[]{:S(2)}, u32[]{:S(2)}) collective-permute-start(bf16[32,8192]{1,0:T(8,128)(2,1)S(1)} %apply_layer.15), channel_id=1, source_target_pairs={{0,4},{4,8},{8,12},{12,16},{16,20},{20,24},{24,28},{28,0},{1,5},{5... | collective-permute-start | bytes 1572872 | tf_op jit(solution)/shard_map/ppermute | solution.py:129
  154.1 0.1 collective-permute-done.7
  154.3 11.2 %collective-permute-done.15 = bf16[32,8192]{1,0:T(8,128)(2,1)S(1)} collective-permute-done((bf16[32,8192]{1,0:T(8,128)(2,1)S(1)}, bf16[32,8192]{1,0:T(8,128)(2,1)S(1)}, u32[]{:S(2)}, u32[]{:S(2)}) %collective-permute-start.15) | collective-permute-done | bytes 524320 | tf_op jit(solution)/shard_map/ppermute | solution.py:129
  165.5 11.2 %collective-permute-done.23 = bf16[32,8192]{1,0:T(8,128)(2,1)S(1)} collective-permute-done((bf16[32,8192]{1,0:T(8,128)(2,1)S(1)}, bf16[32,8192]{1,0:T(8,128)(2,1)S(1)}, u32[]{:S(2)}, u32[]{:S(2)}) %collective-permute-start.23) | collective-permute-done | bytes 524320 | tf_op jit(solution)/shard_map/ppermute | solution.py:129
  176.7 10.3 %collective-permute-done.31 = bf16[32,8192]{1,0:T(8,128)(2,1)S(1)} collective-permute-done((bf16[32,8192]{1,0:T(8,128)(2,1)S(1)}, bf16[32,8192]{1,0:T(8,128)(2,1)S(1)}, u32[]{:S(2)}, u32[]{:S(2)}) %collective-permute-start.31) | collective-permute-done | bytes 524320 | tf_op jit(solution)/shard_map/ppermute | solution.py:129
  187.0 1.5 pad_maximum_fusion
  (26 shorter events, 0.1 us)
Async XLA Ops:
  0.0 20.5 %copy-start.3 = (s32[1,128,8]{1,2,0:T(8,128)S(1)}, s32[1,128,8]{1,2,0:T(8,128)}, u32[]{:S(2)}) copy-start(s32[1,128,8]{1,2,0:T(8,128)} %param.6) | copy-start | bytes 12292
  1.7 15.9 %collective-permute-start = (bf16[32,8192]{1,0:T(8,128)(2,1)S(1)}, bf16[32,8192]{1,0:T(8,128)(2,1)}, u32[]{:S(2)}, u32[]{:S(2)}) collective-permute-start(bf16[32,8192]{1,0:T(8,128)(2,1)S(1)} %get-tuple-element.5.refs_0_), channel_id=1, source_target_pairs={{0,2},{1,3},{2,0},{3,1},{4,6},{5,7},{6,4},{7,5},{8,10},{9,11},{10,... | collective-permute-start | bytes 1572872 | tf_op jit(solution)/shard_map/ppermute | solution.py:133
  4.7 14.9 %collective-permute-start.1 = (bf16[32,8192]{1,0:T(8,128)(2,1)S(1)}, bf16[32,8192]{1,0:T(8,128)(2,1)S(1)}, u32[]{:S(2)}, u32[]{:S(2)}) collective-permute-start(bf16[32,8192]{1,0:T(8,128)(2,1)S(1)} %get-tuple-element.5.refs_0_), channel_id=1, source_target_pairs={{0,1},{1,0},{2,3},{3,2},{4,5},{5,4},{6,7},{7,6},{8,9},{9,8},{10,11... | collective-permute-start | bytes 1572872 | tf_op jit(solution)/shard_map/ppermute | solution.py:133
  4.7 24.1 %collective-permute-start.8 = (bf16[32,8192]{1,0:T(8,128)(2,1)S(1)}, bf16[32,8192]{1,0:T(8,128)(2,1)}, u32[]{:S(2)}, u32[]{:S(2)}) collective-permute-start(bf16[32,8192]{1,0:T(8,128)(2,1)S(1)} %get-tuple-element.6.refs_0_), channel_id=1, source_target_pairs={{0,2},{1,3},{2,0},{3,1},{4,6},{5,7},{6,4},{7,5},{8,10},{9,11},{10,... | collective-permute-start | bytes 1572872 | tf_op jit(solution)/shard_map/ppermute | solution.py:133
  4.8 34.3 %collective-permute-start.9 = (bf16[32,8192]{1,0:T(8,128)(2,1)S(1)}, bf16[32,8192]{1,0:T(8,128)(2,1)}, u32[]{:S(2)}, u32[]{:S(2)}) collective-permute-start(bf16[32,8192]{1,0:T(8,128)(2,1)S(1)} %get-tuple-element.6.refs_0_), channel_id=1, source_target_pairs={{0,1},{1,0},{2,3},{3,2},{4,5},{5,4},{6,7},{7,6},{8,9},{9,8},{10,11... | collective-permute-start | bytes 1572872 | tf_op jit(solution)/shard_map/ppermute | solution.py:133
  5.2 34.7 %collective-permute-start.16 = (bf16[32,8192]{1,0:T(8,128)(2,1)S(1)}, bf16[32,8192]{1,0:T(8,128)(2,1)S(1)}, u32[]{:S(2)}, u32[]{:S(2)}) collective-permute-start(bf16[32,8192]{1,0:T(8,128)(2,1)S(1)} %get-tuple-element.8.refs_0_), channel_id=1, source_target_pairs={{0,2},{1,3},{2,0},{3,1},{4,6},{5,7},{6,4},{7,5},{8,10},{9,11},{10,... | collective-permute-start | bytes 1572872 | tf_op jit(solution)/shard_map/ppermute | solution.py:133
  17.5 32.8 %collective-permute-start.24 = (bf16[32,8192]{1,0:T(8,128)(2,1)S(1)}, bf16[32,8192]{1,0:T(8,128)(2,1)S(1)}, u32[]{:S(2)}, u32[]{:S(2)}) collective-permute-start(bf16[32,8192]{1,0:T(8,128)(2,1)S(1)} %get-tuple-element.7.refs_0_), channel_id=1, source_target_pairs={{0,2},{1,3},{2,0},{3,1},{4,6},{5,7},{6,4},{7,5},{8,10},{9,11},{10,... | collective-permute-start | bytes 1572872 | tf_op jit(solution)/shard_map/ppermute | solution.py:133
  19.6 0.8 copy-start.1
  20.4 29.9 %collective-permute-start.2 = (bf16[32,8192]{1,0:T(8,128)(2,1)}, bf16[32,8192]{1,0:T(8,128)(2,1)}, u32[]{:S(2)}, u32[]{:S(2)}) collective-permute-start(bf16[32,8192]{1,0:T(8,128)(2,1)} %collective-permute-done.refs_1_), channel_id=1, source_target_pairs={{0,1},{1,0},{2,3},{3,2},{4,5},{5,4},{6,7},{7,6},{8,9},{9,8},{10,11... | collective-permute-start | bytes 1572872 | tf_op jit(solution)/shard_map/ppermute | solution.py:133
  28.8 27.8 %collective-permute-start.10 = (bf16[32,8192]{1,0:T(8,128)(2,1)}, bf16[32,8192]{1,0:T(8,128)(2,1)S(1)}, u32[]{:S(2)}, u32[]{:S(2)}) collective-permute-start(bf16[32,8192]{1,0:T(8,128)(2,1)} %collective-permute-done.8.refs_1_), channel_id=1, source_target_pairs={{0,1},{1,0},{2,3},{3,2},{4,5},{5,4},{6,7},{7,6},{8,9},{9,8},{10,11... | collective-permute-start | bytes 1572872 | tf_op jit(solution)/shard_map/ppermute | solution.py:133
  28.8 3.4 %copy-start = (bf16[1,128,8,4096]{3,2,1,0:T(8,128)(2,1)S(1)}, bf16[1,128,8,4096]{3,2,1,0:T(8,128)(2,1)}, u32[]{:S(2)}) copy-start(bf16[1,128,8,4096]{3,2,1,0:T(8,128)(2,1)} %param.5) | copy-start | bytes 25165828
  32.2 19.3 %copy-start.2 = (bf16[32,8192]{1,0:T(8,128)(2,1)S(1)}, bf16[32,8192]{1,0:T(8,128)(2,1)}, u32[]{:S(2)}) copy-start(bf16[32,8192]{1,0:T(8,128)(2,1)} %copy-done.1) | copy-start | bytes 1572868
  39.1 24.4 %collective-permute-start.17 = (bf16[32,8192]{1,0:T(8,128)(2,1)S(1)}, bf16[32,8192]{1,0:T(8,128)(2,1)S(1)}, u32[]{:S(2)}, u32[]{:S(2)}) collective-permute-start(bf16[32,8192]{1,0:T(8,128)(2,1)S(1)} %get-tuple-element.8.refs_0_), channel_id=1, source_target_pairs={{0,1},{1,0},{2,3},{3,2},{4,5},{5,4},{6,7},{7,6},{8,9},{9,8},{10,11... | collective-permute-start | bytes 1572872 | tf_op jit(solution)/shard_map/ppermute | solution.py:133
  39.9 31.2 %collective-permute-start.25 = (bf16[32,8192]{1,0:T(8,128)(2,1)S(1)}, bf16[32,8192]{1,0:T(8,128)(2,1)S(1)}, u32[]{:S(2)}, u32[]{:S(2)}) collective-permute-start(bf16[32,8192]{1,0:T(8,128)(2,1)S(1)} %get-tuple-element.7.refs_0_), channel_id=1, source_target_pairs={{0,1},{1,0},{2,3},{3,2},{4,5},{5,4},{6,7},{7,6},{8,9},{9,8},{10,11... | collective-permute-start | bytes 1572872 | tf_op jit(solution)/shard_map/ppermute | solution.py:133
  50.3 14.8 %collective-permute-start.18 = (bf16[32,8192]{1,0:T(8,128)(2,1)S(1)}, bf16[32,8192]{1,0:T(8,128)(2,1)S(1)}, u32[]{:S(2)}, u32[]{:S(2)}) collective-permute-start(bf16[32,8192]{1,0:T(8,128)(2,1)S(1)} %collective-permute-done.16.refs_1_), channel_id=1, source_target_pairs={{0,1},{1,0},{2,3},{3,2},{4,5},{5,4},{6,7},{7,6},{8,9},{9,8},{10,11... | collective-permute-start | bytes 1572872 | tf_op jit(solution)/shard_map/ppermute | solution.py:133
  50.3 20.8 %collective-permute-start.26 = (bf16[32,8192]{1,0:T(8,128)(2,1)S(1)}, bf16[32,8192]{1,0:T(8,128)(2,1)S(1)}, u32[]{:S(2)}, u32[]{:S(2)}) collective-permute-start(bf16[32,8192]{1,0:T(8,128)(2,1)S(1)} %collective-permute-done.24.refs_1_), channel_id=1, source_target_pairs={{0,1},{1,0},{2,3},{3,2},{4,5},{5,4},{6,7},{7,6},{8,9},{9,8},{10,11... | collective-permute-start | bytes 1572872 | tf_op jit(solution)/shard_map/ppermute | solution.py:133
  56.6 20.4 %collective-permute-start.3 = (bf16[32,8192]{1,0:T(8,128)(2,1)S(1)}, bf16[32,8192]{1,0:T(8,128)(2,1)S(1)}, u32[]{:S(2)}, u32[]{:S(2)}) collective-permute-start(bf16[32,8192]{1,0:T(8,128)(2,1)S(1)} %apply_layer.8), channel_id=1, source_target_pairs={{0,4},{4,8},{8,12},{12,16},{16,20},{20,24},{24,28},{28,0},{1,5},{5... | collective-permute-start | bytes 1572872 | tf_op jit(solution)/shard_map/ppermute | solution.py:129
  63.5 21.9 %collective-permute-start.11 = (bf16[32,8192]{1,0:T(8,128)(2,1)S(1)}, bf16[32,8192]{1,0:T(8,128)(2,1)S(1)}, u32[]{:S(2)}, u32[]{:S(2)}) collective-permute-start(bf16[32,8192]{1,0:T(8,128)(2,1)S(1)} %apply_layer.10), channel_id=1, source_target_pairs={{0,4},{4,8},{8,12},{12,16},{16,20},{20,24},{24,28},{28,0},{1,5},{5... | collective-permute-start | bytes 1572872 | tf_op jit(solution)/shard_map/ppermute | solution.py:129
  69.5 27.2 %collective-permute-start.19 = (bf16[32,8192]{1,0:T(8,128)(2,1)S(1)}, bf16[32,8192]{1,0:T(8,128)(2,1)S(1)}, u32[]{:S(2)}, u32[]{:S(2)}) collective-permute-start(bf16[32,8192]{1,0:T(8,128)(2,1)S(1)} %apply_layer.12), channel_id=1, source_target_pairs={{0,4},{4,8},{8,12},{12,16},{16,20},{20,24},{24,28},{28,0},{1,5},{5... | collective-permute-start | bytes 1572872 | tf_op jit(solution)/shard_map/ppermute | solution.py:129
  75.5 31.8 %collective-permute-start.27 = (bf16[32,8192]{1,0:T(8,128)(2,1)S(1)}, bf16[32,8192]{1,0:T(8,128)(2,1)S(1)}, u32[]{:S(2)}, u32[]{:S(2)}) collective-permute-start(bf16[32,8192]{1,0:T(8,128)(2,1)S(1)} %apply_layer.14), channel_id=1, source_target_pairs={{0,4},{4,8},{8,12},{12,16},{16,20},{20,24},{24,28},{28,0},{1,5},{5... | collective-permute-start | bytes 1572872 | tf_op jit(solution)/shard_map/ppermute | solution.py:129
  77.1 31.7 %collective-permute-start.4 = (bf16[32,8192]{1,0:T(8,128)(2,1)S(1)}, bf16[32,8192]{1,0:T(8,128)(2,1)S(1)}, u32[]{:S(2)}, u32[]{:S(2)}) collective-permute-start(bf16[32,8192]{1,0:T(8,128)(2,1)S(1)} %collective-permute-done.3.refs_0_), channel_id=1, source_target_pairs={{0,2},{1,3},{2,0},{3,1},{4,6},{5,7},{6,4},{7,5},{8,10},{9,11},{10,... | collective-permute-start | bytes 1572872 | tf_op jit(solution)/shard_map/ppermute | solution.py:133
  78.5 30.8 %collective-permute-start.5 = (bf16[32,8192]{1,0:T(8,128)(2,1)S(1)}, bf16[32,8192]{1,0:T(8,128)(2,1)S(1)}, u32[]{:S(2)}, u32[]{:S(2)}) collective-permute-start(bf16[32,8192]{1,0:T(8,128)(2,1)S(1)} %collective-permute-done.3.refs_0_), channel_id=1, source_target_pairs={{0,1},{1,0},{2,3},{3,2},{4,5},{5,4},{6,7},{7,6},{8,9},{9,8},{10,11... | collective-permute-start | bytes 1572872 | tf_op jit(solution)/shard_map/ppermute | solution.py:133
  85.4 23.9 %collective-permute-start.12 = (bf16[32,8192]{1,0:T(8,128)(2,1)S(1)}, bf16[32,8192]{1,0:T(8,128)(2,1)S(1)}, u32[]{:S(2)}, u32[]{:S(2)}) collective-permute-start(bf16[32,8192]{1,0:T(8,128)(2,1)S(1)} %collective-permute-done.11.refs_0_), channel_id=1, source_target_pairs={{0,2},{1,3},{2,0},{3,1},{4,6},{5,7},{6,4},{7,5},{8,10},{9,11},{10,... | collective-permute-start | bytes 1572872 | tf_op jit(solution)/shard_map/ppermute | solution.py:133
  96.7 13.1 %collective-permute-start.13 = (bf16[32,8192]{1,0:T(8,128)(2,1)S(1)}, bf16[32,8192]{1,0:T(8,128)(2,1)S(1)}, u32[]{:S(2)}, u32[]{:S(2)}) collective-permute-start(bf16[32,8192]{1,0:T(8,128)(2,1)S(1)} %collective-permute-done.11.refs_0_), channel_id=1, source_target_pairs={{0,1},{1,0},{2,3},{3,2},{4,5},{5,4},{6,7},{7,6},{8,9},{9,8},{10,11... | collective-permute-start | bytes 1572872 | tf_op jit(solution)/shard_map/ppermute | solution.py:133
  107.3 14.9 %collective-permute-start.20 = (bf16[32,8192]{1,0:T(8,128)(2,1)S(1)}, bf16[32,8192]{1,0:T(8,128)(2,1)S(1)}, u32[]{:S(2)}, u32[]{:S(2)}) collective-permute-start(bf16[32,8192]{1,0:T(8,128)(2,1)S(1)} %collective-permute-done.19.refs_0_), channel_id=1, source_target_pairs={{0,2},{1,3},{2,0},{3,1},{4,6},{5,7},{6,4},{7,5},{8,10},{9,11},{10,... | collective-permute-start | bytes 1572872 | tf_op jit(solution)/shard_map/ppermute | solution.py:133
  108.8 23.0 %collective-permute-start.28 = (bf16[32,8192]{1,0:T(8,128)(2,1)S(1)}, bf16[32,8192]{1,0:T(8,128)(2,1)S(1)}, u32[]{:S(2)}, u32[]{:S(2)}) collective-permute-start(bf16[32,8192]{1,0:T(8,128)(2,1)S(1)} %collective-permute-done.27.refs_0_), channel_id=1, source_target_pairs={{0,2},{1,3},{2,0},{3,1},{4,6},{5,7},{6,4},{7,5},{8,10},{9,11},{10,... | collective-permute-start | bytes 1572872 | tf_op jit(solution)/shard_map/ppermute | solution.py:133
  109.3 22.5 %collective-permute-start.6 = (bf16[32,8192]{1,0:T(8,128)(2,1)S(1)}, bf16[32,8192]{1,0:T(8,128)(2,1)S(1)}, u32[]{:S(2)}, u32[]{:S(2)}) collective-permute-start(bf16[32,8192]{1,0:T(8,128)(2,1)S(1)} %collective-permute-done.4.refs_1_), channel_id=1, source_target_pairs={{0,1},{1,0},{2,3},{3,2},{4,5},{5,4},{6,7},{7,6},{8,9},{9,8},{10,11... | collective-permute-start | bytes 1572872 | tf_op jit(solution)/shard_map/ppermute | solution.py:133
  109.3 27.4 %collective-permute-start.14 = (bf16[32,8192]{1,0:T(8,128)(2,1)S(1)}, bf16[32,8192]{1,0:T(8,128)(2,1)S(1)}, u32[]{:S(2)}, u32[]{:S(2)}) collective-permute-start(bf16[32,8192]{1,0:T(8,128)(2,1)S(1)} %collective-permute-done.12.refs_1_), channel_id=1, source_target_pairs={{0,1},{1,0},{2,3},{3,2},{4,5},{5,4},{6,7},{7,6},{8,9},{9,8},{10,11... | collective-permute-start | bytes 1572872 | tf_op jit(solution)/shard_map/ppermute | solution.py:133
  109.8 31.4 %collective-permute-start.21 = (bf16[32,8192]{1,0:T(8,128)(2,1)S(1)}, bf16[32,8192]{1,0:T(8,128)(2,1)S(1)}, u32[]{:S(2)}, u32[]{:S(2)}) collective-permute-start(bf16[32,8192]{1,0:T(8,128)(2,1)S(1)} %collective-permute-done.19.refs_0_), channel_id=1, source_target_pairs={{0,1},{1,0},{2,3},{3,2},{4,5},{5,4},{6,7},{7,6},{8,9},{9,8},{10,11... | collective-permute-start | bytes 1572872 | tf_op jit(solution)/shard_map/ppermute | solution.py:133
  122.1 20.0 %collective-permute-start.22 = (bf16[32,8192]{1,0:T(8,128)(2,1)S(1)}, bf16[32,8192]{1,0:T(8,128)(2,1)S(1)}, u32[]{:S(2)}, u32[]{:S(2)}) collective-permute-start(bf16[32,8192]{1,0:T(8,128)(2,1)S(1)} %collective-permute-done.20.refs_1_), channel_id=1, source_target_pairs={{0,1},{1,0},{2,3},{3,2},{4,5},{5,4},{6,7},{7,6},{8,9},{9,8},{10,11... | collective-permute-start | bytes 1572872 | tf_op jit(solution)/shard_map/ppermute | solution.py:133
  131.8 15.4 %collective-permute-start.29 = (bf16[32,8192]{1,0:T(8,128)(2,1)S(1)}, bf16[32,8192]{1,0:T(8,128)(2,1)S(1)}, u32[]{:S(2)}, u32[]{:S(2)}) collective-permute-start(bf16[32,8192]{1,0:T(8,128)(2,1)S(1)} %collective-permute-done.27.refs_0_), channel_id=1, source_target_pairs={{0,1},{1,0},{2,3},{3,2},{4,5},{5,4},{6,7},{7,6},{8,9},{9,8},{10,11... | collective-permute-start | bytes 1572872 | tf_op jit(solution)/shard_map/ppermute | solution.py:133
  131.8 15.4 %collective-permute-start.30 = (bf16[32,8192]{1,0:T(8,128)(2,1)S(1)}, bf16[32,8192]{1,0:T(8,128)(2,1)S(1)}, u32[]{:S(2)}, u32[]{:S(2)}) collective-permute-start(bf16[32,8192]{1,0:T(8,128)(2,1)S(1)} %collective-permute-done.28.refs_1_), channel_id=1, source_target_pairs={{0,1},{1,0},{2,3},{3,2},{4,5},{5,4},{6,7},{7,6},{8,9},{9,8},{10,11... | collective-permute-start | bytes 1572872 | tf_op jit(solution)/shard_map/ppermute | solution.py:133
  136.7 17.5 %collective-permute-start.7 = (bf16[32,8192]{1,0:T(8,128)(2,1)S(1)}, bf16[32,8192]{1,0:T(8,128)(2,1)S(1)}, u32[]{:S(2)}, u32[]{:S(2)}) collective-permute-start(bf16[32,8192]{1,0:T(8,128)(2,1)S(1)} %apply_layer.9), channel_id=1, source_target_pairs={{0,4},{4,8},{8,12},{12,16},{16,20},{20,24},{24,28},{28,0},{1,5},{5... | collective-permute-start | bytes 1572872 | tf_op jit(solution)/shard_map/ppermute | solution.py:129
  141.3 24.3 %collective-permute-start.15 = (bf16[32,8192]{1,0:T(8,128)(2,1)S(1)}, bf16[32,8192]{1,0:T(8,128)(2,1)S(1)}, u32[]{:S(2)}, u32[]{:S(2)}) collective-permute-start(bf16[32,8192]{1,0:T(8,128)(2,1)S(1)} %apply_layer.11), channel_id=1, source_target_pairs={{0,4},{4,8},{8,12},{12,16},{16,20},{20,24},{24,28},{28,0},{1,5},{5... | collective-permute-start | bytes 1572872 | tf_op jit(solution)/shard_map/ppermute | solution.py:129
  146.5 30.2 %collective-permute-start.23 = (bf16[32,8192]{1,0:T(8,128)(2,1)S(1)}, bf16[32,8192]{1,0:T(8,128)(2,1)S(1)}, u32[]{:S(2)}, u32[]{:S(2)}) collective-permute-start(bf16[32,8192]{1,0:T(8,128)(2,1)S(1)} %apply_layer.13), channel_id=1, source_target_pairs={{0,4},{4,8},{8,12},{12,16},{16,20},{20,24},{24,28},{28,0},{1,5},{5... | collective-permute-start | bytes 1572872 | tf_op jit(solution)/shard_map/ppermute | solution.py:129
  151.6 35.4 %collective-permute-start.31 = (bf16[32,8192]{1,0:T(8,128)(2,1)S(1)}, bf16[32,8192]{1,0:T(8,128)(2,1)S(1)}, u32[]{:S(2)}, u32[]{:S(2)}) collective-permute-start(bf16[32,8192]{1,0:T(8,128)(2,1)S(1)} %apply_layer.15), channel_id=1, source_target_pairs={{0,4},{4,8},{8,12},{12,16},{16,20},{20,24},{24,28},{28,0},{1,5},{5... | collective-permute-start | bytes 1572872 | tf_op jit(solution)/shard_map/ppermute | solution.py:129

commit v2 on v1

v2 whole, which is shorter than its diff:
```python
import functools

import jax
import jax.numpy as jnp
from jax import lax
from jax.experimental import pallas as pl
from jax.experimental.pallas import tpu as pltpu
from jax.sharding import PartitionSpec as P

BLK = 64
LANES = 128
WIDE = 4
STREAMS = 4
CHUNKS = (32, 32, 32, 32)
PIECES = 2
TOKEN = (8, LANES)
MIB = 1 << 20
ROOMY = 14 * MIB
TINY = pl.CostEstimate(flops=1, bytes_accessed=1, transcendentals=0)


def arrange_body(*refs):
    tile_refs, out_refs, (token_ref, order_ref) = refs[:STREAMS], refs[STREAMS + 1:2 * STREAMS + 1], refs[2 * STREAMS + 1:]
    fanin = tile_refs[0].shape[1]
    depth = fanin * BLK
    half = depth // 2

    @pl.when(pl.program_id(0) == 0)
    def _():
        row = lax.broadcasted_iota(jnp.int32, (depth, depth), 0)
        column = lax.broadcasted_iota(jnp.int32, (depth, depth), 1)
        neuron = row % BLK
        origin = (neuron % 2) * half + (neuron // 2) * fanin + row // BLK
        order_ref[...] = jnp.where(column == origin, 1.0, 0.0).astype(jnp.bfloat16)
        token_ref[...] = jnp.zeros_like(token_ref)

    low = lax.broadcasted_iota(jnp.int32, (half, LANES), 1) < BLK
    for tiles_ref, out_ref in zip(tile_refs, out_refs):
        stacked = []
        for member in range(WIDE):
            flat = tiles_ref[member].astype(jnp.float32)
            stacked.append(jnp.concatenate([flat[:, t * LANES:(t + 1) * LANES] for t in range(half // fanin)], axis=0))
        even, odd = [], []
        for pair in range(WIDE // 2):
            first, second = stacked[2 * pair], stacked[2 * pair + 1]
            even.append(jnp.where(low, first, pltpu.roll(second, BLK, axis=1)).astype(jnp.bfloat16))
            odd.append(jnp.where(low, pltpu.roll(first, BLK, axis=1), second).astype(jnp.bfloat16))
        mixed = jnp.concatenate([jnp.concatenate(even, axis=1), jnp.concatenate(odd, axis=1)], axis=0)
        out_ref[0] = jnp.dot(order_ref[...], mixed, preferred_element_type=jnp.float32).astype(jnp.bfloat16)


def arrange_weights(block_tiles, earlier):
    _, blocks, fanin, flat = block_tiles.shape
    steps = blocks // (WIDE * STREAMS)
    depth = fanin * BLK
    tiles = block_tiles.reshape(blocks, fanin, flat)
    return pl.pallas_call(
        arrange_body,
        grid=(steps,),
        in_specs=[pl.BlockSpec((WIDE, fanin, flat), lambda i, q=q: (STREAMS * i + q, 0, 0)) for q in range(STREAMS)]
        + [pl.BlockSpec(memory_space=pl.ANY)],
        out_specs=[pl.BlockSpec((1, depth, WIDE * BLK), lambda i: (i, 0, 0))] * STREAMS + [pl.BlockSpec(TOKEN, lambda i: (0, 0))],
        out_shape=[pltpu.VMEM((steps, depth, WIDE * BLK), jnp.bfloat16)] * STREAMS + [jax.ShapeDtypeStruct(TOKEN, jnp.float32)],
        scratch_shapes=[pltpu.VMEM((depth, depth), jnp.bfloat16)],
        compiler_params=pltpu.CompilerParams(vmem_limit_bytes=ROOMY),
        cost_estimate=TINY,
        name="arrange_weights",
    )(*[tiles] * STREAMS, earlier)


def layer_body(parts, waited, place_ref, bias_ref, *refs):
    pieces = sum(parts)
    piece_refs, weight_refs = refs[:pieces], refs[pieces:pieces + STREAMS]
    out_ref, tile_ref = refs[pieces + STREAMS + waited:]
    rows = out_ref.shape[0]
    turned = tile_ref.shape[0] // 2
    step = pl.program_id(0)
    fanin = weight_refs[0].shape[1] // BLK

    @pl.when(step == 0)
    def _():
        place = 0
        for ref in piece_refs:
            for t in range(ref.shape[1] // LANES):
                tile = ref[:, t * LANES:(t + 1) * LANES]
                tile_ref[place] = tile
                tile_ref[turned + place] = jnp.concatenate([tile[:, BLK:], tile[:, :BLK]], axis=1)
                place += 1

    low = lax.broadcasted_iota(jnp.int32, (rows, LANES), 1) < BLK
    bias = bias_ref[0]
    for q, weight_ref in enumerate(weight_refs):
        stacked = []
        for member in range(WIDE):
            base = ((step * STREAMS + q) * WIDE + member) * fanin
            picked = []
            for k in range(0, fanin, 2):
                left = tile_ref[place_ref[base + k]]
                right = tile_ref[place_ref[base + k + 1]]
                picked.append(jnp.where(low, left, right))
            stacked.append(jnp.concatenate(picked, axis=1))
        lhs = jnp.concatenate(stacked, axis=0)
        sums = jnp.dot(lhs, weight_ref[0], preferred_element_type=jnp.float32)
        for pair in range(WIDE // 2):
            lanes = slice(pair * LANES, (pair + 1) * LANES)
            first = sums[2 * pair * rows:(2 * pair + 1) * rows, lanes]
            second = sums[(2 * pair + 1) * rows:(2 * pair + 2) * rows, lanes]
            result = jnp.maximum(jnp.where(low, first, second) + bias, 0.0)
            start = (q * (WIDE // 2) + pair) * LANES
            out_ref[:, start:start + LANES] = result.astype(jnp.bfloat16)


def apply_layer(rows, parts, weights, places, layer_bias, earlier):
    pieces = [piece for part in parts for piece in part]
    columns = sum(array.shape[1] for array, _ in pieces)
    steps, depth, width = weights[0].shape
    in_specs = [pl.BlockSpec(memory_space=pltpu.SMEM), pl.BlockSpec(memory_space=pltpu.SMEM)]
    for array, block in pieces:
        in_specs.append(pl.BlockSpec((rows, array.shape[1]), lambda i, block=block: (block, 0), pipeline_mode=pl.Buffered(1)))
    in_specs += [pl.BlockSpec((1, depth, width), lambda i: (i, 0, 0))] * STREAMS
    in_specs += [pl.BlockSpec(memory_space=pl.ANY)] * len(earlier)
    return pl.pallas_call(
        functools.partial(layer_body, [len(part) for part in parts], len(earlier)),
        grid=(steps,),
        in_specs=in_specs,
        out_specs=pl.BlockSpec((rows, STREAMS * width), lambda i: (0, i)),
        out_shape=jax.ShapeDtypeStruct((rows, steps * STREAMS * width), jnp.bfloat16),
        scratch_shapes=[pltpu.VMEM((2 * columns // LANES, rows, LANES), jnp.bfloat16)],
        compiler_params=pltpu.CompilerParams(vmem_limit_bytes=ROOMY),
        cost_estimate=TINY,
        name="apply_layer",
    )(places, layer_bias, *[array for array, _ in pieces], *weights, *earlier)


def from_behind(array, axis, by):
    size = lax.axis_size(axis)
    return lax.ppermute(array, axis, [(i, (i + by) % size) for i in range(size)])


def swapped(array, axis, bit):
    return lax.ppermute(array, axis, [(i, i ^ bit) for i in range(lax.axis_size(axis))])


def distances(size):
    held, bit = [0], size // 2
    while bit:
        held, bit = held + [d ^ bit for d in held], bit // 2
    return held


def block_places(sources, per_part):
    size = lax.axis_size("sect")
    me = lax.axis_index("sect")
    order = distances(size)
    distance = (sources // per_part) ^ me
    slot = jnp.zeros_like(distance)
    for position, d in enumerate(order):
        slot = jnp.where(distance == d, position, slot)
    inside = sources % per_part
    tile = slot * (per_part // 2) + inside // 2
    position = lax.broadcasted_iota(jnp.int32, sources.shape, sources.ndim - 1)
    return (tile + jnp.where(inside % 2 == position % 2, 0, size * per_part // 2)).reshape(-1)


def nothing(*refs):
    del refs


def tie(array, *earlier):
    anywhere = pl.BlockSpec(memory_space=pl.ANY)
    return pl.pallas_call(
        nothing,
        in_specs=[anywhere] * (1 + len(earlier)),
        out_specs=anywhere,
        out_shape=jax.ShapeDtypeStruct(array.shape, array.dtype),
        input_output_aliases={0: 0},
        compiler_params=pltpu.CompilerParams(vmem_limit_bytes=MIB),
        cost_estimate=TINY,
        name="tie",
    )(array, *earlier)


def per_device(activations, block_tiles, sources, layer_bias):
    places = block_places(sources[0], activations.shape[1] // BLK)
    count = len(CHUNKS)
    starts = [sum(CHUNKS[:c]) for c in range(count)]
    size = lax.axis_size("sect")
    top, rest = size // 2, size // 4

    state = [activations[s:s + r] for s, r in zip(starts, CHUNKS)]
    far = [swapped(chunk, "sect", top) for chunk in state]
    near = swapped(activations, "sect", rest)
    *weights, token = arrange_weights(block_tiles, places)
    relayed, far_next, near_next, result = {}, {}, {}, {}
    latest = []

    def layer(c, own, far_part, near_part, pins):
        far_part = tie(far_part, *(latest[-1:] or [token]))
        pieces = PIECES if latest else 1
        wide = far_part.shape[1] // pieces
        across = [(swapped(far_part[:, p * wide:(p + 1) * wide], "sect", rest), 0) for p in range(pieces)]
        hidden = apply_layer(CHUNKS[c], [[own], [(far_part, 0)], [near_part], across], weights, places, layer_bias, latest[-1:] + pins)
        latest.append(hidden)
        return from_behind(hidden, "phase", 1)

    def first(c, pins):
        block = starts[c] // CHUNKS[c]
        relayed[c] = layer(c, (activations, block), far[c], (near, block), pins)

    def spread(c):
        relayed[c] = tie(relayed[c], latest[-1])
        far_next[c] = swapped(relayed[c], "sect", top)
        near_next[c] = swapped(relayed[c], "sect", rest)

    def second(c, pins):
        result[c] = layer(c, (relayed[c], 0), far_next[c], (near_next[c], 0), pins)

    first(0, [])
    for c in range(1, count):
        first(c, [near_next[c - 2]] if c > 1 else [])
        spread(c - 1)
    second(0, [near_next[count - 2]])
    spread(count - 1)
    for c in range(1, count):
        second(c, [near_next[count - 1]] if c == 1 else [result[c - 2]])
    return jnp.concatenate([result[c] for c in range(count)], axis=0)


def solution(mesh):
    in_specs = (
        P("phase", "sect"),
        P("phase", "sect", None, None),
        P("phase", "sect", None),
        P("phase"),
    )
    out_specs = P("phase", "sect")
    return jax.shard_map(
        per_device, mesh=mesh, in_specs=in_specs, out_specs=out_specs, check_vma=False
    )
```

time: 189 us -> 134 us (0.71)
  waiting for transfers between devices: 111 us -> 60.4 us
  starting transfers between devices: 25.3 us -> 22.5 us
    ppermute x24 -> x28, waiting for transfers between devices: 51.2 us -> 17.8 us  [swapped(): lax.ppermute(array, axis, [(i, i ^ bit) for i in range(lax.axis_size(axis...]
    ppermute x8, waiting for transfers between devices: 59.9 us -> 42.6 us  [from_behind(): lax.ppermute(array, axis, [(i, (i + by) % size) for i in range(size)])]
    ppermute x8, starting transfers between devices: 10.6 us -> 6.95 us  [from_behind(): lax.ppermute(array, axis, [(i, (i + by) % size) for i in range(size)])]
    pallas_call x9 -> x21, Pallas kernels: 43.6 us -> 42.2 us  [the longest x8 35.2 us: apply_layer(): pl.pallas_call(functools.partial(layer_body, [len(part) for part in parts...]
    ppermute x24 -> x28, starting transfers between devices: 14.7 us -> 15.5 us  [swapped(): lax.ppermute(array, axis, [(i, i ^ bit) for i in range(lax.axis_size(axis...]
    unnamed x9 -> x11, local copies, waits for them, and re-layouts: 4.28 us -> 3.49 us
  transfers between devices with their start and end apart: 32 -> 36, of which waited for: 13 -> 15; matrix products, arithmetic and copies ran while one was open for 0% -> 2% of each run, Pallas kernels for 23% -> 31%
where the time goes in v2:
time: 134 us
  waiting for transfers between devices  60.4 us (45%)
  Pallas kernels  42.2 us (31%)
  starting transfers between devices  22.5 us (17%)
  local copies, waits for them, and re-layouts  6.64 us (5%)
  other arithmetic  1.54 us (1%)
    ppermute x8, waiting for transfers between devices, from_behind(): lax.ppermute(array, axis, [(i, (i + by) % size) for i in range(size)])  42.6 us
    pallas_call x8, Pallas kernels, apply_layer(): pl.pallas_call(functools.partial(layer_body, [len(part) for part in parts...  35.2 us
    ppermute x28, waiting for transfers between devices, swapped(): lax.ppermute(array, axis, [(i, i ^ bit) for i in range(lax.axis_size(axis...  17.8 us
    ppermute x28, starting transfers between devices, swapped(): lax.ppermute(array, axis, [(i, i ^ bit) for i in range(lax.axis_size(axis...  15.5 us
    pallas_call x1, Pallas kernels, arrange_weights(): pl.pallas_call(arrange_body, grid=(steps,), in_specs=[pl.BlockSpec((WIDE,...  6.97 us
    ppermute x8, starting transfers between devices, from_behind(): lax.ppermute(array, axis, [(i, (i + by) % size) for i in range(size)])  6.95 us
    unnamed x11, local copies, waits for them, and re-layouts  3.49 us
    slice x1, local copies, waits for them, and re-layouts, per_device(): state = [activations[s:s + r] for s, r in zip(starts, CHUNKS)]  2.71 us
  transfers between devices with their start and end apart: 36, of which 15 were waited for; matrix products, arithmetic and copies ran while one was open for 2% of the time, Pallas kernels for 31%

profile of v2, /device:TPU:0, one launch (start us, length us, event | category | flops | bytes accessed | tf_op | source)
XLA Modules:
  0.0 134.2 jit_solution(13426873967886609032)
XLA Ops:
  0.0 0.5 collective-permute-start.1
  0.5 2.7 %fusion.7 = (bf16[32,8192]{1,0:T(8,128)(2,1)}, bf16[32,8192]{1,0:T(8,128)(2,1)}, bf16[32,8192]{1,0:T(8,128)(2,1)S(1)}, bf16[32,8192]{1,0:T(8,128)(2,1)}) fusion(bf16[128,8192]{1,0:T(8,128)(2,1)} %refs_0_.7), kind=kLoop, calls=%fused_computation.24 | loop fusion | bytes 4194304 | tf_op jit(solution)/shard_map/slice | solution.py:190
  3.2 2.5 %collective-permute-start = (bf16[32,8192]{1,0:T(8,128)(2,1)}, bf16[32,8192]{1,0:T(8,128)(2,1)S(1)}, u32[]{:S(2)}, u32[]{:S(2)}) collective-permute-start(bf16[32,8192]{1,0:T(8,128)(2,1)} %get-tuple-element.15), channel_id=1, source_target_pairs={{0,2},{1,3},{2,0},{3,1},{4,6},{5,7},{6,4},{7,5},{8,10},{9,11},{10,... | collective-permute-start | bytes 1572872 | tf_op jit(solution)/shard_map/ppermute | solution.py:141
  5.7 0.1 select_n.58
  5.8 0.1 copy.17
  5.9 0.1 squeeze.3
  6.0 0.0 copy-start
  6.0 3.4 %copy-done = bf16[1,128,8,4096]{3,2,1,0:T(8,128)(2,1)S(1)} copy-done((bf16[1,128,8,4096]{3,2,1,0:T(8,128)(2,1)S(1)}, bf16[1,128,8,4096]{3,2,1,0:T(8,128)(2,1)}, u32[]{:S(2)}) %copy-start) | copy-done | bytes 8388632
  9.4 7.0 %arrange_weights.1 = (bf16[8,512,256]{2,1,0:T(8,128)(2,1)S(1)}, bf16[8,512,256]{2,1,0:T(8,128)(2,1)S(1)}, bf16[8,512,256]{2,1,0:T(8,128)(2,1)S(1)}, bf16[8,512,256]{2,1,0:T(8,128)(2,1)S(1)}, f32[8,128]{1,0:T(8,128)S(1)}) custom-call(bf16[128,8,4096]{2,1,0:T(8,128)(2,1)S(1)} %bitcast.1, bf16[128,8,4096]{2,1,0:T(8,128)(2,1)S(1)} %bitcast.2, ...), custom_call_target="tpu_custom_call" | custom-call | flops 1 | bytes 1 | tf_op jit(solution)/shard_map/arrange_weights/pallas_call | solution.py:57
  16.4 2.1 %collective-permute-done.refs_0_ = bf16[32,8192]{1,0:T(8,128)(2,1)S(1)} collective-permute-done((bf16[32,8192]{1,0:T(8,128)(2,1)}, bf16[32,8192]{1,0:T(8,128)(2,1)S(1)}, u32[]{:S(2)}, u32[]{:S(2)}) %collective-permute-start) | collective-permute-done | bytes 524320 | tf_op jit(solution)/shard_map/ppermute | solution.py:141
  18.5 0.0 collective-permute-start.2
  18.5 1.7 %collective-permute-start.4 = (bf16[32,8192]{1,0:T(8,128)(2,1)S(1)}, bf16[32,8192]{1,0:T(8,128)(2,1)S(1)}, u32[]{:S(2)}, u32[]{:S(2)}) collective-permute-start(bf16[32,8192]{1,0:T(8,128)(2,1)S(1)} %copy-done.3), channel_id=1, source_target_pairs={{0,2},{1,3},{2,0},{3,1},{4,6},{5,7},{6,4},{7,5},{8,10},{9,11},{10,... | collective-permute-start | bytes 1572872 | tf_op jit(solution)/shard_map/ppermute | solution.py:141
  20.2 0.3 collective-permute-start.9
  21.2 0.0 collective-permute-done.1.refs_2_
  21.2 4.4 %apply_layer.8.refs_1_.refs_9_ = bf16[32,8192]{1,0:T(8,128)(2,1)S(1)} custom-call(s32[1024]{0:T(1024)S(1)} %fusion.2.refs_4_.place_ref, f32[1]{0:T(128)S(6)} %copy.30.bias_ref, bf16[128,8192]{1,0:T(8,128)(2,1)S(1)} %copy-done.1, bf16[32,8192]{1,0:T(8,128)(2,1)S(1)} %tie.12.refs_1_, bf16[128,8192]{1,0:T(8,128)(2,1)S(1)} %collective-permute-done.1.refs_2_, ...), custom_call_target="tpu_custom_call" | custom-call | flops 1 | bytes 1 | tf_op jit(solution)/shard_map/apply_layer/pallas_call | solution.py:122
  25.6 1.8 %collective-permute-start.3 = (bf16[32,8192]{1,0:T(8,128)(2,1)S(1)}, bf16[32,8192]{1,0:T(8,128)(2,1)S(1)}, u32[]{:S(2)}, u32[]{:S(2)}) collective-permute-start(bf16[32,8192]{1,0:T(8,128)(2,1)S(1)} %apply_layer.8.refs_1_.refs_9_), channel_id=1, source_target_pairs={{0,4},{4,8},{8,12},{12,16},{16,20},{20,24},{24,28},{28,0},{1,5},{5... | collective-permute-start | bytes 1572872 | tf_op jit(solution)/shard_map/ppermute | solution.py:137
  27.4 5.8 %collective-permute-done.4.refs_0_ = bf16[32,8192]{1,0:T(8,128)(2,1)S(1)} collective-permute-done((bf16[32,8192]{1,0:T(8,128)(2,1)S(1)}, bf16[32,8192]{1,0:T(8,128)(2,1)S(1)}, u32[]{:S(2)}, u32[]{:S(2)}) %collective-permute-start.4) | collective-permute-done | bytes 524320 | tf_op jit(solution)/shard_map/ppermute | solution.py:141
  33.2 0.1 collective-permute-start.5
  33.3 0.5 collective-permute-start.6
  33.8 1.7 %collective-permute-start.8 = (bf16[32,8192]{1,0:T(8,128)(2,1)S(1)}, bf16[32,8192]{1,0:T(8,128)(2,1)S(1)}, u32[]{:S(2)}, u32[]{:S(2)}) collective-permute-start(bf16[32,8192]{1,0:T(8,128)(2,1)S(1)} %get-tuple-element.17), channel_id=1, source_target_pairs={{0,2},{1,3},{2,0},{3,1},{4,6},{5,7},{6,4},{7,5},{8,10},{9,11},{10,... | collective-permute-start | bytes 1572872 | tf_op jit(solution)/shard_map/ppermute | solution.py:141
  35.6 4.4 %apply_layer.9.refs_1_.refs_9_ = bf16[32,8192]{1,0:T(8,128)(2,1)S(1)} custom-call(s32[1024]{0:T(1024)S(1)} %fusion.2.refs_4_.place_ref, f32[1]{0:T(128)S(6)} %copy.30.bias_ref, bf16[128,8192]{1,0:T(8,128)(2,1)S(1)} %copy-done.1, bf16[32,8192]{1,0:T(8,128)(2,1)S(1)} %tie.13.refs_1_, bf16[128,8192]{1,0:T(8,128)(2,1)S(1)} %collective-permute-done.1.refs_2_, ...), custom_call_target="tpu_custom_call" | custom-call | flops 1 | bytes 1 | tf_op jit(solution)/shard_map/apply_layer/pallas_call | solution.py:122
  40.0 1.6 %collective-permute-start.15 = (bf16[32,8192]{1,0:T(8,128)(2,1)S(1)}, bf16[32,8192]{1,0:T(8,128)(2,1)S(1)}, u32[]{:S(2)}, u32[]{:S(2)}) collective-permute-start(bf16[32,8192]{1,0:T(8,128)(2,1)S(1)} %apply_layer.9.refs_1_.refs_9_), channel_id=1, source_target_pairs={{0,4},{4,8},{8,12},{12,16},{16,20},{20,24},{24,28},{28,0},{1,5},{5... | collective-permute-start | bytes 1572872 | tf_op jit(solution)/shard_map/ppermute | solution.py:137
  41.5 2.9 %collective-permute-done.9.refs_0_ = bf16[32,8192]{1,0:T(8,128)(2,1)S(1)} collective-permute-done((bf16[32,8192]{1,0:T(8,128)(2,1)S(1)}, bf16[32,8192]{1,0:T(8,128)(2,1)S(1)}, u32[]{:S(2)}, u32[]{:S(2)}) %collective-permute-start.9) | collective-permute-done | bytes 524320 | tf_op jit(solution)/shard_map/ppermute | solution.py:141
  44.4 0.0 collective-permute-done.3.refs_0_
  44.5 0.6 collective-permute-start.10
  45.0 0.1 collective-permute-start.11
  45.1 1.6 %collective-permute-done.10.refs_3_ = bf16[32,4096]{1,0:T(8,128)(2,1)S(1)} collective-permute-done((bf16[32,4096]{1,0:T(8,128)(2,1)S(1)}, bf16[32,4096]{1,0:T(8,128)(2,1)S(1)}, u32[]{:S(2)}, u32[]{:S(2)}) %collective-permute-start.10) | collective-permute-done | bytes 262176 | tf_op jit(solution)/shard_map/ppermute | solution.py:141
  46.7 1.7 %collective-permute-start.7 = (bf16[32,8192]{1,0:T(8,128)(2,1)S(1)}, bf16[32,8192]{1,0:T(8,128)(2,1)S(1)}, u32[]{:S(2)}, u32[]{:S(2)}) collective-permute-start(bf16[32,8192]{1,0:T(8,128)(2,1)S(1)} %tie.14.refs_0_), channel_id=1, source_target_pairs={{0,2},{1,3},{2,0},{3,1},{4,6},{5,7},{6,4},{7,5},{8,10},{9,11},{10,... | collective-permute-start | bytes 1572872 | tf_op jit(solution)/shard_map/ppermute | solution.py:141
  48.5 0.0 collective-permute-done.11.refs_4_
  48.5 4.4 %apply_layer.10.refs_1_.refs_9_ = bf16[32,8192]{1,0:T(8,128)(2,1)S(1)} custom-call(s32[1024]{0:T(1024)S(1)} %fusion.2.refs_4_.place_ref, f32[1]{0:T(128)S(6)} %copy.30.bias_ref, bf16[128,8192]{1,0:T(8,128)(2,1)S(1)} %copy-done.1, bf16[32,8192]{1,0:T(8,128)(2,1)S(1)} %tie.15.refs_1_, bf16[128,8192]{1,0:T(8,128)(2,1)S(1)} %collective-permute-done.1.refs_2_, ...), custom_call_target="tpu_custom_call" | custom-call | flops 1 | bytes 1 | tf_op jit(solution)/shard_map/apply_layer/pallas_call | solution.py:122
  52.9 1.6 %collective-permute-start.19 = (bf16[32,8192]{1,0:T(8,128)(2,1)S(1)}, bf16[32,8192]{1,0:T(8,128)(2,1)S(1)}, u32[]{:S(2)}, u32[]{:S(2)}) collective-permute-start(bf16[32,8192]{1,0:T(8,128)(2,1)S(1)} %apply_layer.10.refs_1_.refs_9_), channel_id=1, source_target_pairs={{0,4},{4,8},{8,12},{12,16},{16,20},{20,24},{24,28},{28,0},{1,5},{5... | collective-permute-start | bytes 1572872 | tf_op jit(solution)/shard_map/ppermute | solution.py:137
  54.4 2.3 %collective-permute-done.15.refs_0_ = bf16[32,8192]{1,0:T(8,128)(2,1)S(1)} collective-permute-done((bf16[32,8192]{1,0:T(8,128)(2,1)S(1)}, bf16[32,8192]{1,0:T(8,128)(2,1)S(1)}, u32[]{:S(2)}, u32[]{:S(2)}) %collective-permute-start.15) | collective-permute-done | bytes 524320 | tf_op jit(solution)/shard_map/ppermute | solution.py:137
  56.8 0.6 collective-permute-start.13
  57.3 0.1 collective-permute-start.14
  57.4 1.6 %collective-permute-done.13.refs_3_ = bf16[32,4096]{1,0:T(8,128)(2,1)S(1)} collective-permute-done((bf16[32,4096]{1,0:T(8,128)(2,1)S(1)}, bf16[32,4096]{1,0:T(8,128)(2,1)S(1)}, u32[]{:S(2)}, u32[]{:S(2)}) %collective-permute-start.13) | collective-permute-done | bytes 262176 | tf_op jit(solution)/shard_map/ppermute | solution.py:141
  59.0 1.5 %collective-permute-start.22 = (bf16[32,8192]{1,0:T(8,128)(2,1)S(1)}, bf16[32,8192]{1,0:T(8,128)(2,1)S(1)}, u32[]{:S(2)}, u32[]{:S(2)}) collective-permute-start(bf16[32,8192]{1,0:T(8,128)(2,1)S(1)} %tie.17.refs_0_), channel_id=1, source_target_pairs={{0,2},{1,3},{2,0},{3,1},{4,6},{5,7},{6,4},{7,5},{8,10},{9,11},{10,... | collective-permute-start | bytes 1572872 | tf_op jit(solution)/shard_map/ppermute | solution.py:141
  60.5 4.4 %apply_layer.11.refs_1_.refs_9_ = bf16[32,8192]{1,0:T(8,128)(2,1)S(1)} custom-call(s32[1024]{0:T(1024)S(1)} %fusion.2.refs_4_.place_ref, f32[1]{0:T(128)S(6)} %copy.30.bias_ref, bf16[128,8192]{1,0:T(8,128)(2,1)S(1)} %copy-done.1, bf16[32,8192]{1,0:T(8,128)(2,1)S(1)} %tie.16.refs_1_, bf16[128,8192]{1,0:T(8,128)(2,1)S(1)} %collective-permute-done.1.refs_2_, ...), custom_call_target="tpu_custom_call" | custom-call | flops 1 | bytes 1 | tf_op jit(solution)/shard_map/apply_layer/pallas_call | solution.py:122
  64.9 0.1 collective-permute-start.25
  65.0 4.4 %collective-permute-done.19.refs_0_ = bf16[32,8192]{1,0:T(8,128)(2,1)S(1)} collective-permute-done((bf16[32,8192]{1,0:T(8,128)(2,1)S(1)}, bf16[32,8192]{1,0:T(8,128)(2,1)S(1)}, u32[]{:S(2)}, u32[]{:S(2)}) %collective-permute-start.19) | collective-permute-done | bytes 524320 | tf_op jit(solution)/shard_map/ppermute | solution.py:137
  69.5 0.6 collective-permute-start.17
  70.0 0.1 collective-permute-start.18
  70.1 1.6 %collective-permute-done.17.refs_3_ = bf16[32,4096]{1,0:T(8,128)(2,1)S(1)} collective-permute-done((bf16[32,4096]{1,0:T(8,128)(2,1)S(1)}, bf16[32,4096]{1,0:T(8,128)(2,1)S(1)}, u32[]{:S(2)}, u32[]{:S(2)}) %collective-permute-start.17) | collective-permute-done | bytes 262176 | tf_op jit(solution)/shard_map/ppermute | solution.py:141
  71.7 0.7 collective-permute-start.28
  72.4 4.4 %apply_layer.12.refs_1_.refs_9_ = bf16[32,8192]{1,0:T(8,128)(2,1)S(1)} custom-call(s32[1024]{0:T(1024)S(1)} %fusion.2.refs_4_.place_ref, f32[1]{0:T(128)S(6)} %copy.30.bias_ref, bf16[32,8192]{1,0:T(8,128)(2,1)S(1)} %tie.14.refs_0_, bf16[32,8192]{1,0:T(8,128)(2,1)S(1)} %tie.18.refs_1_, bf16[32,8192]{1,0:T(8,128)(2,1)S(1)} %collective-permute-done.12.refs_10_.refs_2_, ...), custom_call_target="tpu_custom_call" | custom-call | flops 1 | bytes 1 | tf_op jit(solution)/shard_map/apply_layer/pallas_call | solution.py:122
  76.8 4.5 %collective-permute-done.25.refs_0_ = bf16[32,8192]{1,0:T(8,128)(2,1)S(1)} collective-permute-done((bf16[32,8192]{1,0:T(8,128)(2,1)S(1)}, bf16[32,8192]{1,0:T(8,128)(2,1)S(1)}, u32[]{:S(2)}, u32[]{:S(2)}) %collective-permute-start.25) | collective-permute-done | bytes 524320 | tf_op jit(solution)/shard_map/ppermute | solution.py:137
  81.4 0.6 collective-permute-start.23
  81.9 0.1 collective-permute-start.24
  82.0 1.6 %collective-permute-done.23.refs_3_ = bf16[32,4096]{1,0:T(8,128)(2,1)S(1)} collective-permute-done((bf16[32,4096]{1,0:T(8,128)(2,1)S(1)}, bf16[32,4096]{1,0:T(8,128)(2,1)S(1)}, u32[]{:S(2)}, u32[]{:S(2)}) %collective-permute-start.23) | collective-permute-done | bytes 262176 | tf_op jit(solution)/shard_map/ppermute | solution.py:141
  83.6 0.6 collective-permute-start.32
  84.3 4.4 %apply_layer.13.refs_1_.refs_9_ = bf16[32,8192]{1,0:T(8,128)(2,1)S(1)} custom-call(s32[1024]{0:T(1024)S(1)} %fusion.2.refs_4_.place_ref, f32[1]{0:T(128)S(6)} %copy.30.bias_ref, bf16[32,8192]{1,0:T(8,128)(2,1)S(1)} %tie.17.refs_0_, bf16[32,8192]{1,0:T(8,128)(2,1)S(1)} %tie.20.refs_1_, bf16[32,8192]{1,0:T(8,128)(2,1)S(1)} %collective-permute-done.16.refs_10_.refs_2_, ...), custom_call_target="tpu_custom_call" | custom-call | flops 1 | bytes 1 | tf_op jit(solution)/shard_map/apply_layer/pallas_call | solution.py:122
  88.7 0.7 collective-permute-done.28.refs_0_
  89.4 0.1 collective-permute-start.29
  89.5 0.5 collective-permute-start.30
  90.0 1.8 %collective-permute-start.27 = (bf16[32,8192]{1,0:T(8,128)(2,1)S(1)}, bf16[32,8192]{1,0:T(8,128)(2,1)S(1)}, u32[]{:S(2)}, u32[]{:S(2)}) collective-permute-start(bf16[32,8192]{1,0:T(8,128)(2,1)S(1)} %apply_layer.13.refs_1_.refs_9_), channel_id=1, source_target_pairs={{0,4},{4,8},{8,12},{12,16},{16,20},{20,24},{24,28},{28,0},{1,5},{5... | collective-permute-start | bytes 1572872 | tf_op jit(solution)/shard_map/ppermute | solution.py:137
  91.8 7.7 %collective-permute-done.21.refs_10_ = bf16[32,8192]{1,0:T(8,128)(2,1)S(1)} collective-permute-done((bf16[32,8192]{1,0:T(8,128)(2,1)S(1)}, bf16[32,8192]{1,0:T(8,128)(2,1)S(1)}, u32[]{:S(2)}, u32[]{:S(2)}) %collective-permute-start.21) | collective-permute-done | bytes 524320 | tf_op jit(solution)/shard_map/ppermute | solution.py:137
  99.5 4.4 %apply_layer.14.refs_1_.refs_9_ = bf16[32,8192]{1,0:T(8,128)(2,1)S(1)} custom-call(s32[1024]{0:T(1024)S(1)} %fusion.2.refs_4_.place_ref, f32[1]{0:T(128)S(6)} %copy.30.bias_ref, bf16[32,8192]{1,0:T(8,128)(2,1)S(1)} %tie.19.refs_0_, bf16[32,8192]{1,0:T(8,128)(2,1)S(1)} %tie.22.refs_1_, bf16[32,8192]{1,0:T(8,128)(2,1)S(1)} %collective-permute-done.20.refs_10_.refs_2_, ...), custom_call_target="tpu_custom_call" | custom-call | flops 1 | bytes 1 | tf_op jit(solution)/shard_map/apply_layer/pallas_call | solution.py:122
  103.9 0.1 collective-permute-start.33
  104.0 0.5 collective-permute-start.34
  104.5 6.0 %collective-permute-done.27.refs_10_ = bf16[32,8192]{1,0:T(8,128)(2,1)S(1)} collective-permute-done((bf16[32,8192]{1,0:T(8,128)(2,1)S(1)}, bf16[32,8192]{1,0:T(8,128)(2,1)S(1)}, u32[]{:S(2)}, u32[]{:S(2)}) %collective-permute-start.27) | collective-permute-done | bytes 524320 | tf_op jit(solution)/shard_map/ppermute | solution.py:137
  110.5 4.4 %apply_layer.15 = bf16[32,8192]{1,0:T(8,128)(2,1)S(1)} custom-call(s32[1024]{0:T(1024)S(1)} %fusion.2.refs_4_.place_ref, f32[1]{0:T(128)S(6)} %copy.30.bias_ref, bf16[32,8192]{1,0:T(8,128)(2,1)S(1)} %tie.21.refs_0_, bf16[32,8192]{1,0:T(8,128)(2,1)S(1)} %tie.23.refs_1_, bf16[32,8192]{1,0:T(8,128)(2,1)S(1)} %collective-permute-done.26.refs_10_.refs_2_, ...), custom_call_target="tpu_custom_call" | custom-call | flops 1 | bytes 1 | tf_op jit(solution)/shard_map/apply_layer/pallas_call | solution.py:122
  114.9 0.1 collective-permute-start.35
  115.0 7.0 %collective-permute-done.31 = bf16[32,8192]{1,0:T(8,128)(2,1)S(1)} collective-permute-done((bf16[32,8192]{1,0:T(8,128)(2,1)S(1)}, bf16[32,8192]{1,0:T(8,128)(2,1)S(1)}, u32[]{:S(2)}, u32[]{:S(2)}) %collective-permute-start.31) | collective-permute-done | bytes 524320 | tf_op jit(solution)/shard_map/ppermute | solution.py:137
  122.0 10.7 %collective-permute-done.35 = bf16[32,8192]{1,0:T(8,128)(2,1)S(1)} collective-permute-done((bf16[32,8192]{1,0:T(8,128)(2,1)S(1)}, bf16[32,8192]{1,0:T(8,128)(2,1)S(1)}, u32[]{:S(2)}, u32[]{:S(2)}) %collective-permute-start.35) | collective-permute-done | bytes 524320 | tf_op jit(solution)/shard_map/ppermute | solution.py:137
  132.7 1.5 %pad_maximum_fusion = bf16[128,8192]{1,0:T(8,128)(2,1)} fusion(bf16[32,8192]{1,0:T(8,128)(2,1)S(1)} %collective-permute-done.35, bf16[32,8192]{1,0:T(8,128)(2,1)S(1)} %collective-permute-done.31, bf16[32,8192]{1,0:T(8,128)(2,1)S(1)} %collective-permute-done.27.refs_10_, bf16[32,8192]{1,0:T(8,128)(2,1)S(1)} %collective-permute-done.21.refs_10_), kind=kLoop, calls=%fused_computation | loop fusion | flops 8388608 | bytes 4194304 | tf_op jit(solution)/shard_map/concatenate | solution.py:226
  (55 shorter events, 0.4 us)
Async XLA Ops:
  0.0 5.8 %copy-start.4 = (s32[1,128,8]{1,2,0:T(8,128)S(1)}, s32[1,128,8]{1,2,0:T(8,128)}, u32[]{:S(2)}) copy-start(s32[1,128,8]{1,2,0:T(8,128)} %param.6) | copy-start | bytes 12292
  0.0 21.2 %collective-permute-start.1 = (bf16[128,8192]{1,0:T(8,128)(2,1)}, bf16[128,8192]{1,0:T(8,128)(2,1)S(1)}, u32[]{:S(2)}, u32[]{:S(2)}) collective-permute-start(bf16[128,8192]{1,0:T(8,128)(2,1)} %refs_0_.7), channel_id=1, source_target_pairs={{0,1},{1,0},{2,3},{3,2},{4,5},{5,4},{6,7},{7,6},{8,9},{9,8},{10,11... | collective-permute-start | bytes 6291464 | tf_op jit(solution)/shard_map/ppermute | solution.py:141
  3.2 15.3 %collective-permute-start = (bf16[32,8192]{1,0:T(8,128)(2,1)}, bf16[32,8192]{1,0:T(8,128)(2,1)S(1)}, u32[]{:S(2)}, u32[]{:S(2)}) collective-permute-start(bf16[32,8192]{1,0:T(8,128)(2,1)} %get-tuple-element.15), channel_id=1, source_target_pairs={{0,2},{1,3},{2,0},{3,1},{4,6},{5,7},{6,4},{7,5},{8,10},{9,11},{10,... | collective-permute-start | bytes 1572872 | tf_op jit(solution)/shard_map/ppermute | solution.py:141
  6.0 3.4 %copy-start = (bf16[1,128,8,4096]{3,2,1,0:T(8,128)(2,1)S(1)}, bf16[1,128,8,4096]{3,2,1,0:T(8,128)(2,1)}, u32[]{:S(2)}) copy-start(bf16[1,128,8,4096]{3,2,1,0:T(8,128)(2,1)} %param.5) | copy-start | bytes 25165828
  9.4 9.1 %copy-start.3 = (bf16[32,8192]{1,0:T(8,128)(2,1)S(1)}, bf16[32,8192]{1,0:T(8,128)(2,1)}, u32[]{:S(2)}) copy-start(bf16[32,8192]{1,0:T(8,128)(2,1)} %get-tuple-element.18) | copy-start | bytes 1572868
  9.4 10.8 %copy-start.2 = (bf16[32,8192]{1,0:T(8,128)(2,1)S(1)}, bf16[32,8192]{1,0:T(8,128)(2,1)}, u32[]{:S(2)}) copy-start(bf16[32,8192]{1,0:T(8,128)(2,1)} %get-tuple-element.16) | copy-start | bytes 1572868
  9.4 11.8 %copy-start.1 = (bf16[128,8192]{1,0:T(8,128)(2,1)S(1)}, bf16[128,8192]{1,0:T(8,128)(2,1)}, u32[]{:S(2)}) copy-start(bf16[128,8192]{1,0:T(8,128)(2,1)} %refs_0_.7) | copy-start | bytes 6291460
  18.5 2.7 %collective-permute-start.2 = (bf16[32,8192]{1,0:T(8,128)(2,1)S(1)}, bf16[32,8192]{1,0:T(8,128)(2,1)S(1)}, u32[]{:S(2)}, u32[]{:S(2)}) collective-permute-start(bf16[32,8192]{1,0:T(8,128)(2,1)S(1)} %tie.12.refs_1_), channel_id=1, source_target_pairs={{0,1},{1,0},{2,3},{3,2},{4,5},{5,4},{6,7},{7,6},{8,9},{9,8},{10,11... | collective-permute-start | bytes 1572872 | tf_op jit(solution)/shard_map/ppermute | solution.py:141
  18.5 14.7 %collective-permute-start.4 = (bf16[32,8192]{1,0:T(8,128)(2,1)S(1)}, bf16[32,8192]{1,0:T(8,128)(2,1)S(1)}, u32[]{:S(2)}, u32[]{:S(2)}) collective-permute-start(bf16[32,8192]{1,0:T(8,128)(2,1)S(1)} %copy-done.3), channel_id=1, source_target_pairs={{0,2},{1,3},{2,0},{3,1},{4,6},{5,7},{6,4},{7,5},{8,10},{9,11},{10,... | collective-permute-start | bytes 1572872 | tf_op jit(solution)/shard_map/ppermute | solution.py:141
  20.2 24.2 %collective-permute-start.9 = (bf16[32,8192]{1,0:T(8,128)(2,1)S(1)}, bf16[32,8192]{1,0:T(8,128)(2,1)S(1)}, u32[]{:S(2)}, u32[]{:S(2)}) collective-permute-start(bf16[32,8192]{1,0:T(8,128)(2,1)S(1)} %copy-done.2), channel_id=1, source_target_pairs={{0,2},{1,3},{2,0},{3,1},{4,6},{5,7},{6,4},{7,5},{8,10},{9,11},{10,... | collective-permute-start | bytes 1572872 | tf_op jit(solution)/shard_map/ppermute | solution.py:141
  25.6 18.8 %collective-permute-start.3 = (bf16[32,8192]{1,0:T(8,128)(2,1)S(1)}, bf16[32,8192]{1,0:T(8,128)(2,1)S(1)}, u32[]{:S(2)}, u32[]{:S(2)}) collective-permute-start(bf16[32,8192]{1,0:T(8,128)(2,1)S(1)} %apply_layer.8.refs_1_.refs_9_), channel_id=1, source_target_pairs={{0,4},{4,8},{8,12},{12,16},{16,20},{20,24},{24,28},{28,0},{1,5},{5... | collective-permute-start | bytes 1572872 | tf_op jit(solution)/shard_map/ppermute | solution.py:137
  33.2 2.3 %collective-permute-start.5 = (bf16[32,4096]{1,0:T(8,128)(2,1)S(1)}, bf16[32,4096]{1,0:T(8,128)(2,1)S(1)}, u32[]{:S(2)}, u32[]{:S(2)}) collective-permute-start(bf16[32,4096]{1,0:T(8,128)(2,1)S(1)} %get-tuple-element.32), channel_id=1, source_target_pairs={{0,1},{1,0},{2,3},{3,2},{4,5},{5,4},{6,7},{7,6},{8,9},{9,8},{10,11... | collective-permute-start | bytes 786440 | tf_op jit(solution)/shard_map/ppermute | solution.py:141
  33.3 2.2 %collective-permute-start.6 = (bf16[32,4096]{1,0:T(8,128)(2,1)S(1)}, bf16[32,4096]{1,0:T(8,128)(2,1)S(1)}, u32[]{:S(2)}, u32[]{:S(2)}) collective-permute-start(bf16[32,4096]{1,0:T(8,128)(2,1)S(1)} %get-tuple-element.31), channel_id=1, source_target_pairs={{0,1},{1,0},{2,3},{3,2},{4,5},{5,4},{6,7},{7,6},{8,9},{9,8},{10,11... | collective-permute-start | bytes 786440 | tf_op jit(solution)/shard_map/ppermute | solution.py:141
  33.8 22.9 %collective-permute-start.8 = (bf16[32,8192]{1,0:T(8,128)(2,1)S(1)}, bf16[32,8192]{1,0:T(8,128)(2,1)S(1)}, u32[]{:S(2)}, u32[]{:S(2)}) collective-permute-start(bf16[32,8192]{1,0:T(8,128)(2,1)S(1)} %get-tuple-element.17), channel_id=1, source_target_pairs={{0,2},{1,3},{2,0},{3,1},{4,6},{5,7},{6,4},{7,5},{8,10},{9,11},{10,... | collective-permute-start | bytes 1572872 | tf_op jit(solution)/shard_map/ppermute | solution.py:141
  40.0 16.7 %collective-permute-start.15 = (bf16[32,8192]{1,0:T(8,128)(2,1)S(1)}, bf16[32,8192]{1,0:T(8,128)(2,1)S(1)}, u32[]{:S(2)}, u32[]{:S(2)}) collective-permute-start(bf16[32,8192]{1,0:T(8,128)(2,1)S(1)} %apply_layer.9.refs_1_.refs_9_), channel_id=1, source_target_pairs={{0,4},{4,8},{8,12},{12,16},{16,20},{20,24},{24,28},{28,0},{1,5},{5... | collective-permute-start | bytes 1572872 | tf_op jit(solution)/shard_map/ppermute | solution.py:137
  44.4 4.0 %collective-permute-start.12 = (bf16[32,8192]{1,0:T(8,128)(2,1)S(1)}, bf16[32,8192]{1,0:T(8,128)(2,1)S(1)}, u32[]{:S(2)}, u32[]{:S(2)}) collective-permute-start(bf16[32,8192]{1,0:T(8,128)(2,1)S(1)} %tie.14.refs_0_), channel_id=1, source_target_pairs={{0,1},{1,0},{2,3},{3,2},{4,5},{5,4},{6,7},{7,6},{8,9},{9,8},{10,11... | collective-permute-start | bytes 1572872 | tf_op jit(solution)/shard_map/ppermute | solution.py:141
  44.5 2.2 %collective-permute-start.10 = (bf16[32,4096]{1,0:T(8,128)(2,1)S(1)}, bf16[32,4096]{1,0:T(8,128)(2,1)S(1)}, u32[]{:S(2)}, u32[]{:S(2)}) collective-permute-start(bf16[32,4096]{1,0:T(8,128)(2,1)S(1)} %get-tuple-element.30), channel_id=1, source_target_pairs={{0,1},{1,0},{2,3},{3,2},{4,5},{5,4},{6,7},{7,6},{8,9},{9,8},{10,11... | collective-permute-start | bytes 786440 | tf_op jit(solution)/shard_map/ppermute | solution.py:141
  45.0 3.4 %collective-permute-start.11 = (bf16[32,4096]{1,0:T(8,128)(2,1)S(1)}, bf16[32,4096]{1,0:T(8,128)(2,1)S(1)}, u32[]{:S(2)}, u32[]{:S(2)}) collective-permute-start(bf16[32,4096]{1,0:T(8,128)(2,1)S(1)} %get-tuple-element.29), channel_id=1, source_target_pairs={{0,1},{1,0},{2,3},{3,2},{4,5},{5,4},{6,7},{7,6},{8,9},{9,8},{10,11... | collective-permute-start | bytes 786440 | tf_op jit(solution)/shard_map/ppermute | solution.py:141
  46.7 22.7 %collective-permute-start.7 = (bf16[32,8192]{1,0:T(8,128)(2,1)S(1)}, bf16[32,8192]{1,0:T(8,128)(2,1)S(1)}, u32[]{:S(2)}, u32[]{:S(2)}) collective-permute-start(bf16[32,8192]{1,0:T(8,128)(2,1)S(1)} %tie.14.refs_0_), channel_id=1, source_target_pairs={{0,2},{1,3},{2,0},{3,1},{4,6},{5,7},{6,4},{7,5},{8,10},{9,11},{10,... | collective-permute-start | bytes 1572872 | tf_op jit(solution)/shard_map/ppermute | solution.py:141
  52.9 16.6 %collective-permute-start.19 = (bf16[32,8192]{1,0:T(8,128)(2,1)S(1)}, bf16[32,8192]{1,0:T(8,128)(2,1)S(1)}, u32[]{:S(2)}, u32[]{:S(2)}) collective-permute-start(bf16[32,8192]{1,0:T(8,128)(2,1)S(1)} %apply_layer.10.refs_1_.refs_9_), channel_id=1, source_target_pairs={{0,4},{4,8},{8,12},{12,16},{16,20},{20,24},{24,28},{28,0},{1,5},{5... | collective-permute-start | bytes 1572872 | tf_op jit(solution)/shard_map/ppermute | solution.py:137
  56.7 3.8 %collective-permute-start.16 = (bf16[32,8192]{1,0:T(8,128)(2,1)S(1)}, bf16[32,8192]{1,0:T(8,128)(2,1)S(1)}, u32[]{:S(2)}, u32[]{:S(2)}) collective-permute-start(bf16[32,8192]{1,0:T(8,128)(2,1)S(1)} %tie.17.refs_0_), channel_id=1, source_target_pairs={{0,1},{1,0},{2,3},{3,2},{4,5},{5,4},{6,7},{7,6},{8,9},{9,8},{10,11... | collective-permute-start | bytes 1572872 | tf_op jit(solution)/shard_map/ppermute | solution.py:141
  56.8 2.2 %collective-permute-start.13 = (bf16[32,4096]{1,0:T(8,128)(2,1)S(1)}, bf16[32,4096]{1,0:T(8,128)(2,1)S(1)}, u32[]{:S(2)}, u32[]{:S(2)}) collective-permute-start(bf16[32,4096]{1,0:T(8,128)(2,1)S(1)} %get-tuple-element.28), channel_id=1, source_target_pairs={{0,1},{1,0},{2,3},{3,2},{4,5},{5,4},{6,7},{7,6},{8,9},{9,8},{10,11... | collective-permute-start | bytes 786440 | tf_op jit(solution)/shard_map/ppermute | solution.py:141
  57.3 3.2 %collective-permute-start.14 = (bf16[32,4096]{1,0:T(8,128)(2,1)S(1)}, bf16[32,4096]{1,0:T(8,128)(2,1)S(1)}, u32[]{:S(2)}, u32[]{:S(2)}) collective-permute-start(bf16[32,4096]{1,0:T(8,128)(2,1)S(1)} %get-tuple-element.27), channel_id=1, source_target_pairs={{0,1},{1,0},{2,3},{3,2},{4,5},{5,4},{6,7},{7,6},{8,9},{9,8},{10,11... | collective-permute-start | bytes 786440 | tf_op jit(solution)/shard_map/ppermute | solution.py:141
  59.0 22.4 %collective-permute-start.22 = (bf16[32,8192]{1,0:T(8,128)(2,1)S(1)}, bf16[32,8192]{1,0:T(8,128)(2,1)S(1)}, u32[]{:S(2)}, u32[]{:S(2)}) collective-permute-start(bf16[32,8192]{1,0:T(8,128)(2,1)S(1)} %tie.17.refs_0_), channel_id=1, source_target_pairs={{0,2},{1,3},{2,0},{3,1},{4,6},{5,7},{6,4},{7,5},{8,10},{9,11},{10,... | collective-permute-start | bytes 1572872 | tf_op jit(solution)/shard_map/ppermute | solution.py:141
  64.9 16.4 %collective-permute-start.25 = (bf16[32,8192]{1,0:T(8,128)(2,1)S(1)}, bf16[32,8192]{1,0:T(8,128)(2,1)S(1)}, u32[]{:S(2)}, u32[]{:S(2)}) collective-permute-start(bf16[32,8192]{1,0:T(8,128)(2,1)S(1)} %apply_layer.11.refs_1_.refs_9_), channel_id=1, source_target_pairs={{0,4},{4,8},{8,12},{12,16},{16,20},{20,24},{24,28},{28,0},{1,5},{5... | collective-permute-start | bytes 1572872 | tf_op jit(solution)/shard_map/ppermute | solution.py:137
  69.4 3.0 %collective-permute-start.20 = (bf16[32,8192]{1,0:T(8,128)(2,1)S(1)}, bf16[32,8192]{1,0:T(8,128)(2,1)S(1)}, u32[]{:S(2)}, u32[]{:S(2)}) collective-permute-start(bf16[32,8192]{1,0:T(8,128)(2,1)S(1)} %tie.19.refs_0_), channel_id=1, source_target_pairs={{0,1},{1,0},{2,3},{3,2},{4,5},{5,4},{6,7},{7,6},{8,9},{9,8},{10,11... | collective-permute-start | bytes 1572872 | tf_op jit(solution)/shard_map/ppermute | solution.py:141
  69.5 2.2 %collective-permute-start.17 = (bf16[32,4096]{1,0:T(8,128)(2,1)S(1)}, bf16[32,4096]{1,0:T(8,128)(2,1)S(1)}, u32[]{:S(2)}, u32[]{:S(2)}) collective-permute-start(bf16[32,4096]{1,0:T(8,128)(2,1)S(1)} %get-tuple-element.26), channel_id=1, source_target_pairs={{0,1},{1,0},{2,3},{3,2},{4,5},{5,4},{6,7},{7,6},{8,9},{9,8},{10,11... | collective-permute-start | bytes 786440 | tf_op jit(solution)/shard_map/ppermute | solution.py:141
  70.0 2.3 %collective-permute-start.18 = (bf16[32,4096]{1,0:T(8,128)(2,1)S(1)}, bf16[32,4096]{1,0:T(8,128)(2,1)S(1)}, u32[]{:S(2)}, u32[]{:S(2)}) collective-permute-start(bf16[32,4096]{1,0:T(8,128)(2,1)S(1)} %get-tuple-element.25), channel_id=1, source_target_pairs={{0,1},{1,0},{2,3},{3,2},{4,5},{5,4},{6,7},{7,6},{8,9},{9,8},{10,11... | collective-permute-start | bytes 786440 | tf_op jit(solution)/shard_map/ppermute | solution.py:141
  71.7 17.7 %collective-permute-start.28 = (bf16[32,8192]{1,0:T(8,128)(2,1)S(1)}, bf16[32,8192]{1,0:T(8,128)(2,1)S(1)}, u32[]{:S(2)}, u32[]{:S(2)}) collective-permute-start(bf16[32,8192]{1,0:T(8,128)(2,1)S(1)} %tie.19.refs_0_), channel_id=1, source_target_pairs={{0,2},{1,3},{2,0},{3,1},{4,6},{5,7},{6,4},{7,5},{8,10},{9,11},{10,... | collective-permute-start | bytes 1572872 | tf_op jit(solution)/shard_map/ppermute | solution.py:141
  81.3 2.9 %collective-permute-start.26 = (bf16[32,8192]{1,0:T(8,128)(2,1)S(1)}, bf16[32,8192]{1,0:T(8,128)(2,1)S(1)}, u32[]{:S(2)}, u32[]{:S(2)}) collective-permute-start(bf16[32,8192]{1,0:T(8,128)(2,1)S(1)} %tie.21.refs_0_), channel_id=1, source_target_pairs={{0,1},{1,0},{2,3},{3,2},{4,5},{5,4},{6,7},{7,6},{8,9},{9,8},{10,11... | collective-permute-start | bytes 1572872 | tf_op jit(solution)/shard_map/ppermute | solution.py:141
  81.4 2.2 %collective-permute-start.23 = (bf16[32,4096]{1,0:T(8,128)(2,1)S(1)}, bf16[32,4096]{1,0:T(8,128)(2,1)S(1)}, u32[]{:S(2)}, u32[]{:S(2)}) collective-permute-start(bf16[32,4096]{1,0:T(8,128)(2,1)S(1)} %get-tuple-element.24), channel_id=1, source_target_pairs={{0,1},{1,0},{2,3},{3,2},{4,5},{5,4},{6,7},{7,6},{8,9},{9,8},{10,11... | collective-permute-start | bytes 786440 | tf_op jit(solution)/shard_map/ppermute | solution.py:141
  81.9 2.3 %collective-permute-start.24 = (bf16[32,4096]{1,0:T(8,128)(2,1)S(1)}, bf16[32,4096]{1,0:T(8,128)(2,1)S(1)}, u32[]{:S(2)}, u32[]{:S(2)}) collective-permute-start(bf16[32,4096]{1,0:T(8,128)(2,1)S(1)} %get-tuple-element.23), channel_id=1, source_target_pairs={{0,1},{1,0},{2,3},{3,2},{4,5},{5,4},{6,7},{7,6},{8,9},{9,8},{10,11... | collective-permute-start | bytes 786440 | tf_op jit(solution)/shard_map/ppermute | solution.py:141
  82.0 17.4 %collective-permute-start.21 = (bf16[32,8192]{1,0:T(8,128)(2,1)S(1)}, bf16[32,8192]{1,0:T(8,128)(2,1)S(1)}, u32[]{:S(2)}, u32[]{:S(2)}) collective-permute-start(bf16[32,8192]{1,0:T(8,128)(2,1)S(1)} %apply_layer.12.refs_1_.refs_9_), channel_id=1, source_target_pairs={{0,4},{4,8},{8,12},{12,16},{16,20},{20,24},{24,28},{28,0},{1,5},{5... | collective-permute-start | bytes 1572872 | tf_op jit(solution)/shard_map/ppermute | solution.py:137
  83.6 20.3 %collective-permute-start.32 = (bf16[32,8192]{1,0:T(8,128)(2,1)S(1)}, bf16[32,8192]{1,0:T(8,128)(2,1)S(1)}, u32[]{:S(2)}, u32[]{:S(2)}) collective-permute-start(bf16[32,8192]{1,0:T(8,128)(2,1)S(1)} %tie.21.refs_0_), channel_id=1, source_target_pairs={{0,2},{1,3},{2,0},{3,1},{4,6},{5,7},{6,4},{7,5},{8,10},{9,11},{10,... | collective-permute-start | bytes 1572872 | tf_op jit(solution)/shard_map/ppermute | solution.py:141
  89.4 10.0 %collective-permute-start.29 = (bf16[32,4096]{1,0:T(8,128)(2,1)S(1)}, bf16[32,4096]{1,0:T(8,128)(2,1)S(1)}, u32[]{:S(2)}, u32[]{:S(2)}) collective-permute-start(bf16[32,4096]{1,0:T(8,128)(2,1)S(1)} %get-tuple-element.22), channel_id=1, source_target_pairs={{0,1},{1,0},{2,3},{3,2},{4,5},{5,4},{6,7},{7,6},{8,9},{9,8},{10,11... | collective-permute-start | bytes 786440 | tf_op jit(solution)/shard_map/ppermute | solution.py:141
  89.5 10.0 %collective-permute-start.30 = (bf16[32,4096]{1,0:T(8,128)(2,1)S(1)}, bf16[32,4096]{1,0:T(8,128)(2,1)S(1)}, u32[]{:S(2)}, u32[]{:S(2)}) collective-permute-start(bf16[32,4096]{1,0:T(8,128)(2,1)S(1)} %get-tuple-element.21), channel_id=1, source_target_pairs={{0,1},{1,0},{2,3},{3,2},{4,5},{5,4},{6,7},{7,6},{8,9},{9,8},{10,11... | collective-permute-start | bytes 786440 | tf_op jit(solution)/shard_map/ppermute | solution.py:141
  90.0 20.5 %collective-permute-start.27 = (bf16[32,8192]{1,0:T(8,128)(2,1)S(1)}, bf16[32,8192]{1,0:T(8,128)(2,1)S(1)}, u32[]{:S(2)}, u32[]{:S(2)}) collective-permute-start(bf16[32,8192]{1,0:T(8,128)(2,1)S(1)} %apply_layer.13.refs_1_.refs_9_), channel_id=1, source_target_pairs={{0,4},{4,8},{8,12},{12,16},{16,20},{20,24},{24,28},{28,0},{1,5},{5... | collective-permute-start | bytes 1572872 | tf_op jit(solution)/shard_map/ppermute | solution.py:137
  103.9 6.6 %collective-permute-start.33 = (bf16[32,4096]{1,0:T(8,128)(2,1)S(1)}, bf16[32,4096]{1,0:T(8,128)(2,1)S(1)}, u32[]{:S(2)}, u32[]{:S(2)}) collective-permute-start(bf16[32,4096]{1,0:T(8,128)(2,1)S(1)} %get-tuple-element.20), channel_id=1, source_target_pairs={{0,1},{1,0},{2,3},{3,2},{4,5},{5,4},{6,7},{7,6},{8,9},{9,8},{10,11... | collective-permute-start | bytes 786440 | tf_op jit(solution)/shard_map/ppermute | solution.py:141
  104.0 6.5 %collective-permute-start.34 = (bf16[32,4096]{1,0:T(8,128)(2,1)S(1)}, bf16[32,4096]{1,0:T(8,128)(2,1)S(1)}, u32[]{:S(2)}, u32[]{:S(2)}) collective-permute-start(bf16[32,4096]{1,0:T(8,128)(2,1)S(1)} %get-tuple-element.19), channel_id=1, source_target_pairs={{0,1},{1,0},{2,3},{3,2},{4,5},{5,4},{6,7},{7,6},{8,9},{9,8},{10,11... | collective-permute-start | bytes 786440 | tf_op jit(solution)/shard_map/ppermute | solution.py:141
  104.5 17.5 %collective-permute-start.31 = (bf16[32,8192]{1,0:T(8,128)(2,1)S(1)}, bf16[32,8192]{1,0:T(8,128)(2,1)S(1)}, u32[]{:S(2)}, u32[]{:S(2)}) collective-permute-start(bf16[32,8192]{1,0:T(8,128)(2,1)S(1)} %apply_layer.14.refs_1_.refs_9_), channel_id=1, source_target_pairs={{0,4},{4,8},{8,12},{12,16},{16,20},{20,24},{24,28},{28,0},{1,5},{5... | collective-permute-start | bytes 1572872 | tf_op jit(solution)/shard_map/ppermute | solution.py:137
  114.9 17.8 %collective-permute-start.35 = (bf16[32,8192]{1,0:T(8,128)(2,1)S(1)}, bf16[32,8192]{1,0:T(8,128)(2,1)S(1)}, u32[]{:S(2)}, u32[]{:S(2)}) collective-permute-start(bf16[32,8192]{1,0:T(8,128)(2,1)S(1)} %apply_layer.15), channel_id=1, source_target_pairs={{0,4},{4,8},{8,12},{12,16},{16,20},{20,24},{24,28},{28,0},{1,5},{5... | collective-permute-start | bytes 1572872 | tf_op jit(solution)/shard_map/ppermute | solution.py:137

commit v3 on v2

--- a/solution.py
+++ b/solution.py
@@ -13,10 +13,12 @@
 STREAMS = 4
 CHUNKS = (32, 32, 32, 32)
 PIECES = 2
+TICKS = 2
 TOKEN = (8, LANES)
 MIB = 1 << 20
 ROOMY = 14 * MIB
 TINY = pl.CostEstimate(flops=1, bytes_accessed=1, transcendentals=0)
+SOME = pl.CostEstimate(flops=4 << 30, bytes_accessed=1, transcendentals=0)
 
 
 def arrange_body(*refs):
@@ -162,11 +164,52 @@
     return (tile + jnp.where(inside % 2 == position % 2, 0, size * per_part // 2)).reshape(-1)
 
 
+def copy_body(array_ref, *refs):
+    refs[-1][...] = array_ref[...]
+
+
+def row_block(array, block, rows, earlier):
+    columns = array.shape[1]
+    return pl.pallas_call(
+        copy_body,
+        grid=(1,),
+        in_specs=[pl.BlockSpec((rows, columns), lambda i: (block, 0))] + [pl.BlockSpec(memory_space=pl.ANY)] * len(earlier),
+        out_specs=pl.BlockSpec((rows, columns), lambda i: (0, 0)),
+        out_shape=jax.ShapeDtypeStruct((rows, columns), array.dtype),
+        compiler_params=pltpu.CompilerParams(vmem_limit_bytes=4 * MIB),
+        cost_estimate=TINY,
+        name="row_block",
+    )(array, *earlier)
+
+
+def put_body(start, *refs):
+    chunk_ref, out_ref, sem = refs[0], refs[-2], refs[-1]
+    copy = pltpu.make_async_copy(chunk_ref, out_ref.at[pl.ds(start, chunk_ref.shape[0])], sem)
+    copy.start()
+    copy.wait()
+
+
+def put_rows(chunk, start, total, whole):
+    anywhere = pl.BlockSpec(memory_space=pl.ANY)
+    operands = [chunk] if whole is None else [chunk, whole]
+    return pl.pallas_call(
+        functools.partial(put_body, start),
+        in_specs=[anywhere] * len(operands),
+        out_specs=anywhere,
+        out_shape=jax.ShapeDtypeStruct((total, chunk.shape[1]), chunk.dtype),
+        input_output_aliases={} if whole is None else {1: 0},
+        scratch_shapes=[pltpu.SemaphoreType.DMA],
+        compiler_params=pltpu.CompilerParams(vmem_limit_bytes=MIB),
+        cost_estimate=TINY,
+        name="put_rows",
+    )(*operands)
+
+
 def nothing(*refs):
     del refs
 
 
-def tie(array, *earlier):
+def tie(array, *earlier, cost=TINY):
     anywhere = pl.BlockSpec(memory_space=pl.ANY)
     return pl.pallas_call(
         nothing,
@@ -175,7 +218,7 @@
         out_shape=jax.ShapeDtypeStruct(array.shape, array.dtype),
         input_output_aliases={0: 0},
         compiler_params=pltpu.CompilerParams(vmem_limit_bytes=MIB),
-        cost_estimate=TINY,
+        cost_estimate=cost,
         name="tie",
     )(array, *earlier)
 
@@ -186,44 +229,36 @@
     starts = [sum(CHUNKS[:c]) for c in range(count)]
     size = lax.axis_size("sect")
     top, rest = size // 2, size // 4
-
-    state = [activations[s:s + r] for s, r in zip(starts, CHUNKS)]
-    far = [swapped(chunk, "sect", top) for chunk in state]
-    near = swapped(activations, "sect", rest)
+    calls, moved, own, far, near = [], [], [], [], []
+
+    near_first = swapped(activations, "sect", rest)
     *weights, token = arrange_weights(block_tiles, places)
-    relayed, far_next, near_next, result = {}, {}, {}, {}
-    latest = []
-
-    def layer(c, own, far_part, near_part, pins):
-        far_part = tie(far_part, *(latest[-1:] or [token]))
-        pieces = PIECES if latest else 1
-        wide = far_part.shape[1] // pieces
-        across = [(swapped(far_part[:, p * wide:(p + 1) * wide], "sect", rest), 0) for p in range(pieces)]
-        hidden = apply_layer(CHUNKS[c], [[own], [(far_part, 0)], [near_part], across], weights, places, layer_bias, latest[-1:] + pins)
-        latest.append(hidden)
-        return from_behind(hidden, "phase", 1)
-
-    def first(c, pins):
-        block = starts[c] // CHUNKS[c]
-        relayed[c] = layer(c, (activations, block), far[c], (near, block), pins)
-
-    def spread(c):
-        relayed[c] = tie(relayed[c], latest[-1])
-        far_next[c] = swapped(relayed[c], "sect", top)
-        near_next[c] = swapped(relayed[c], "sect", rest)
-
-    def second(c, pins):
-        result[c] = layer(c, (relayed[c], 0), far_next[c], (near_next[c], 0), pins)
-
-    first(0, [])
-    for c in range(1, count):
-        first(c, [near_next[c - 2]] if c > 1 else [])
-        spread(c - 1)
-    second(0, [near_next[count - 2]])
-    spread(count - 1)
-    for c in range(1, count):
-        second(c, [near_next[count - 1]] if c == 1 else [result[c - 2]])
-    return jnp.concatenate([result[c] for c in range(count)], axis=0)
+
+    def send(n):
+        rows, start = CHUNKS[n % count], starts[n % count]
+        if n < count:
+            chunk = row_block(activations, start // rows, rows, [token] if n == 1 else [])
+            own.append((activations, start // rows))
+            near.append((near_first, start // rows))
+        else:
+            chunk = tie(moved[n - count], calls[n - 2])
+            own.append((chunk, 0))
+            near.append((swapped(chunk, "sect", rest), 0))
+        far.append(swapped(chunk, "sect", top))
+
+    send(0)
+    send(1)
+    for n in range(TICKS * count):
+        here = tie(far[n], *(calls[-1:] or [token]), *moved[max(0, n - 2):max(0, n - 1)])
+        wide = here.shape[1] // PIECES
+        across = [(swapped(here[:, p * wide:(p + 1) * wide], "sect", rest), 0) for p in range(PIECES)]
+        parts = [[own[n]], [(here, 0)], [near[n]], across]
+        calls.append(apply_layer(CHUNKS[n % count], parts, weights, places, layer_bias, calls[-1:]))
+        moved.append(from_behind(calls[n], "phase", 1))
+        if n + 2 < TICKS * count:
+            send(n + 2)
+    moved[-2] = tie(moved[-2], cost=SOME)
+    return jnp.concatenate(moved[-count:], axis=0)
 
 
 def solution(mesh):

time: 134 us -> 125 us (0.933)
  waiting for transfers between devices: 60.4 us -> 55 us
  starting transfers between devices: 22.5 us -> 19.1 us
    ppermute x8, waiting for transfers between devices: 42.6 us -> 28.6 us  [from_behind(): lax.ppermute(array, axis, [(i, (i + by) % size) for i in range(size)])]
    ppermute x28 -> x29, waiting for transfers between devices: 17.8 us -> 26.3 us  [swapped(): lax.ppermute(array, axis, [(i, i ^ bit) for i in range(lax.axis_size(axis...]
    slice x8, local copies, waits for them, and re-layouts: 2.97 us -> 0.28 us  [per_device(): here[:, p * wide:(p + 1) * wide]]
    ppermute x28 -> x29, starting transfers between devices: 15.5 us -> 13.2 us  [swapped(): lax.ppermute(array, axis, [(i, i ^ bit) for i in range(lax.axis_size(axis...]
    unnamed x11 -> x9, local copies, waits for them, and re-layouts: 3.49 us -> 5.08 us
  transfers between devices with their start and end apart: 36 -> 37, of which waited for: 15 -> 28; matrix products, arithmetic and copies ran while one was open for 2% -> 0% of each run, Pallas kernels for 31% -> 34%
where the time goes in v3:
time: 125 us
  waiting for transfers between devices  55 us (44%)
  Pallas kernels  42.8 us (34%)
  starting transfers between devices  19.1 us (15%)
  local copies, waits for them, and re-layouts  5.54 us (4%)
  other arithmetic  1.53 us (1%)
    pallas_call x8, Pallas kernels, apply_layer(): pl.pallas_call(functools.partial(layer_body, [len(part) for part in parts...  35.6 us
    ppermute x8, waiting for transfers between devices, from_behind(): lax.ppermute(array, axis, [(i, (i + by) % size) for i in range(size)])  28.6 us
    ppermute x29, waiting for transfers between devices, swapped(): lax.ppermute(array, axis, [(i, i ^ bit) for i in range(lax.axis_size(axis...  26.3 us
    ppermute x29, starting transfers between devices, swapped(): lax.ppermute(array, axis, [(i, i ^ bit) for i in range(lax.axis_size(axis...  13.2 us
    pallas_call x1, Pallas kernels, arrange_weights(): pl.pallas_call(arrange_body, grid=(steps,), in_specs=[pl.BlockSpec((WIDE,...  6.96 us
    ppermute x8, starting transfers between devices, from_behind(): lax.ppermute(array, axis, [(i, (i + by) % size) for i in range(size)])  5.88 us
    unnamed x9, local copies, waits for them, and re-layouts  5.08 us
  transfers between devices with their start and end apart: 37, of which 28 were waited for; matrix products, arithmetic and copies ran while one was open for 0% of the time, Pallas kernels for 34%

profile of v3, /device:TPU:0, one launch (start us, length us, event | category | flops | bytes accessed | tf_op | source)
XLA Modules:
  0.0 124.9 jit_solution(14280150859574796882)
XLA Ops:
  0.0 0.5 collective-permute-start.1
  0.5 1.6 %copy-done.1 = bf16[128,8192]{1,0:T(8,128)(2,1)S(1)} copy-done((bf16[128,8192]{1,0:T(8,128)(2,1)S(1)}, bf16[128,8192]{1,0:T(8,128)(2,1)}, u32[]{:S(2)}) %copy-start.1) | copy-done | bytes 2097176
  2.1 2.6 %collective-permute-start = (bf16[32,8192]{1,0:T(8,128)(2,1)S(1)}, bf16[32,8192]{1,0:T(8,128)(2,1)S(1)}, u32[]{:S(2)}, u32[]{:S(2)}) collective-permute-start(bf16[32,8192]{1,0:T(8,128)(2,1)S(1)} %row_block.4), channel_id=1, source_target_pairs={{0,2},{1,3},{2,0},{3,1},{4,6},{5,7},{6,4},{7,5},{8,10},{9,11},{10,... | collective-permute-start | bytes 1572872 | tf_op jit(solution)/shard_map/ppermute | solution.py:143
  4.7 0.1 select_n.58
  4.8 0.1 copy.18
  5.0 3.4 %copy-done = bf16[1,128,8,4096]{3,2,1,0:T(8,128)(2,1)S(1)} copy-done((bf16[1,128,8,4096]{3,2,1,0:T(8,128)(2,1)S(1)}, bf16[1,128,8,4096]{3,2,1,0:T(8,128)(2,1)}, u32[]{:S(2)}) %copy-start) | copy-done | bytes 8388632
  8.4 7.0 %arrange_weights.1 = (bf16[8,512,256]{2,1,0:T(8,128)(2,1)S(1)}, bf16[8,512,256]{2,1,0:T(8,128)(2,1)S(1)}, bf16[8,512,256]{2,1,0:T(8,128)(2,1)S(1)}, bf16[8,512,256]{2,1,0:T(8,128)(2,1)S(1)}, f32[8,128]{1,0:T(8,128)S(1)}) custom-call(bf16[128,8,4096]{2,1,0:T(8,128)(2,1)S(1)} %bitcast.1, bf16[128,8,4096]{2,1,0:T(8,128)(2,1)S(1)} %bitcast.2, ...), custom_call_target="tpu_custom_call" | custom-call | flops 1 | bytes 1 | tf_op jit(solution)/shard_map/arrange_weights/pallas_call | solution.py:59
  15.4 0.5 collective-permute-start.6
  15.9 1.3 %collective-permute-done.refs_0_ = bf16[32,8192]{1,0:T(8,128)(2,1)S(1)} collective-permute-done((bf16[32,8192]{1,0:T(8,128)(2,1)S(1)}, bf16[32,8192]{1,0:T(8,128)(2,1)S(1)}, u32[]{:S(2)}, u32[]{:S(2)}) %collective-permute-start) | collective-permute-done | bytes 524320 | tf_op jit(solution)/shard_map/ppermute | solution.py:143
  17.4 0.5 collective-permute-start.3
  17.9 1.8 %collective-permute-start.5 = (bf16[32,8192]{1,0:T(8,128)(2,1)S(1)}, bf16[32,8192]{1,0:T(8,128)(2,1)S(1)}, u32[]{:S(2)}, u32[]{:S(2)}) collective-permute-start(bf16[32,8192]{1,0:T(8,128)(2,1)S(1)} %row_block.5), channel_id=1, source_target_pairs={{0,2},{1,3},{2,0},{3,1},{4,6},{5,7},{6,4},{7,5},{8,10},{9,11},{10,... | collective-permute-start | bytes 1572872 | tf_op jit(solution)/shard_map/ppermute | solution.py:143
  20.4 4.5 %apply_layer.8.refs_1_.refs_9_ = bf16[32,8192]{1,0:T(8,128)(2,1)S(1)} custom-call(s32[1024]{0:T(1024)S(1)} %fusion.2.refs_4_.place_ref, f32[1]{0:T(128)S(6)} %copy.32.bias_ref, bf16[128,8192]{1,0:T(8,128)(2,1)S(1)} %copy-done.2, bf16[32,8192]{1,0:T(8,128)(2,1)S(1)} %tie.13.refs_1_, bf16[128,8192]{1,0:T(8,128)(2,1)S(1)} %collective-permute-done.1.refs_2_, ...), custom_call_target="tpu_custom_call" | custom-call | flops 1 | bytes 1 | tf_op jit(solution)/shard_map/apply_layer/pallas_call | solution.py:124
  24.9 1.6 %collective-permute-start.4 = (bf16[32,8192]{1,0:T(8,128)(2,1)S(1)}, bf16[32,8192]{1,0:T(8,128)(2,1)S(1)}, u32[]{:S(2)}, u32[]{:S(2)}) collective-permute-start(bf16[32,8192]{1,0:T(8,128)(2,1)S(1)} %apply_layer.8.refs_1_.refs_9_), channel_id=1, source_target_pairs={{0,4},{4,8},{8,12},{12,16},{16,20},{20,24},{24,28},{28,0},{1,5},{5... | collective-permute-start | bytes 1572872 | tf_op jit(solution)/shard_map/ppermute | solution.py:139
  26.4 3.8 %collective-permute-done.6.refs_0_ = bf16[32,8192]{1,0:T(8,128)(2,1)S(1)} collective-permute-done((bf16[32,8192]{1,0:T(8,128)(2,1)S(1)}, bf16[32,8192]{1,0:T(8,128)(2,1)S(1)}, u32[]{:S(2)}, u32[]{:S(2)}) %collective-permute-start.6) | collective-permute-done | bytes 524320 | tf_op jit(solution)/shard_map/ppermute | solution.py:143
  30.3 0.5 collective-permute-start.8
  30.9 0.5 collective-permute-start.12
  31.4 0.5 collective-permute-done.7.refs_3_
  31.9 0.4 collective-permute-done.8.refs_4_
  32.2 4.4 %apply_layer.9.refs_1_.refs_9_ = bf16[32,8192]{1,0:T(8,128)(2,1)S(1)} custom-call(s32[1024]{0:T(1024)S(1)} %fusion.2.refs_4_.place_ref, f32[1]{0:T(128)S(6)} %copy.32.bias_ref, bf16[128,8192]{1,0:T(8,128)(2,1)S(1)} %copy-done.2, bf16[32,8192]{1,0:T(8,128)(2,1)S(1)} %tie.14.refs_1_, bf16[128,8192]{1,0:T(8,128)(2,1)S(1)} %collective-permute-done.1.refs_2_, ...), custom_call_target="tpu_custom_call" | custom-call | flops 1 | bytes 1 | tf_op jit(solution)/shard_map/apply_layer/pallas_call | solution.py:124
  36.7 1.6 %collective-permute-start.13 = (bf16[32,8192]{1,0:T(8,128)(2,1)S(1)}, bf16[32,8192]{1,0:T(8,128)(2,1)S(1)}, u32[]{:S(2)}, u32[]{:S(2)}) collective-permute-start(bf16[32,8192]{1,0:T(8,128)(2,1)S(1)} %apply_layer.9.refs_1_.refs_9_), channel_id=1, source_target_pairs={{0,4},{4,8},{8,12},{12,16},{16,20},{20,24},{24,28},{28,0},{1,5},{5... | collective-permute-start | bytes 1572872 | tf_op jit(solution)/shard_map/ppermute | solution.py:139
  38.3 3.2 %collective-permute-done.5.refs_0_ = bf16[32,8192]{1,0:T(8,128)(2,1)S(1)} collective-permute-done((bf16[32,8192]{1,0:T(8,128)(2,1)S(1)}, bf16[32,8192]{1,0:T(8,128)(2,1)S(1)}, u32[]{:S(2)}, u32[]{:S(2)}) %collective-permute-start.5) | collective-permute-done | bytes 524320 | tf_op jit(solution)/shard_map/ppermute | solution.py:143
  41.6 0.5 collective-permute-start.10
  42.1 1.0 collective-permute-done.9.refs_3_
  43.1 0.4 collective-permute-done.10.refs_4_
  43.5 4.5 %apply_layer.10.refs_1_.refs_9_ = bf16[32,8192]{1,0:T(8,128)(2,1)S(1)} custom-call(s32[1024]{0:T(1024)S(1)} %fusion.2.refs_4_.place_ref, f32[1]{0:T(128)S(6)} %copy.32.bias_ref, bf16[128,8192]{1,0:T(8,128)(2,1)S(1)} %copy-done.2, bf16[32,8192]{1,0:T(8,128)(2,1)S(1)} %tie.15.refs_1_, bf16[128,8192]{1,0:T(8,128)(2,1)S(1)} %collective-permute-done.1.refs_2_, ...), custom_call_target="tpu_custom_call" | custom-call | flops 1 | bytes 1 | tf_op jit(solution)/shard_map/apply_layer/pallas_call | solution.py:124
  47.9 1.6 %collective-permute-start.16 = (bf16[32,8192]{1,0:T(8,128)(2,1)S(1)}, bf16[32,8192]{1,0:T(8,128)(2,1)S(1)}, u32[]{:S(2)}, u32[]{:S(2)}) collective-permute-start(bf16[32,8192]{1,0:T(8,128)(2,1)S(1)} %apply_layer.10.refs_1_.refs_9_), channel_id=1, source_target_pairs={{0,4},{4,8},{8,12},{12,16},{16,20},{20,24},{24,28},{28,0},{1,5},{5... | collective-permute-start | bytes 1572872 | tf_op jit(solution)/shard_map/ppermute | solution.py:139
  49.5 0.5 collective-permute-start.11
  50.0 2.0 %collective-permute-done.12.refs_0_ = bf16[32,8192]{1,0:T(8,128)(2,1)S(1)} collective-permute-done((bf16[32,8192]{1,0:T(8,128)(2,1)S(1)}, bf16[32,8192]{1,0:T(8,128)(2,1)S(1)}, u32[]{:S(2)}, u32[]{:S(2)}) %collective-permute-start.12) | collective-permute-done | bytes 524320 | tf_op jit(solution)/shard_map/ppermute | solution.py:143
  52.0 1.5 %collective-permute-done.13.refs_2_.refs_0_ = bf16[32,8192]{1,0:T(8,128)(2,1)S(1)} collective-permute-done((bf16[32,8192]{1,0:T(8,128)(2,1)S(1)}, bf16[32,8192]{1,0:T(8,128)(2,1)S(1)}, u32[]{:S(2)}, u32[]{:S(2)}) %collective-permute-start.13) | collective-permute-done | bytes 524320 | tf_op jit(solution)/shard_map/ppermute | solution.py:139
  53.7 0.5 collective-permute-start.15
  54.2 0.9 collective-permute-done.14.refs_3_
  55.2 0.4 collective-permute-done.15.refs_4_
  55.6 4.4 %apply_layer.11.refs_1_.refs_9_ = bf16[32,8192]{1,0:T(8,128)(2,1)S(1)} custom-call(s32[1024]{0:T(1024)S(1)} %fusion.2.refs_4_.place_ref, f32[1]{0:T(128)S(6)} %copy.32.bias_ref, bf16[128,8192]{1,0:T(8,128)(2,1)S(1)} %copy-done.2, bf16[32,8192]{1,0:T(8,128)(2,1)S(1)} %tie.17.refs_1_, bf16[128,8192]{1,0:T(8,128)(2,1)S(1)} %collective-permute-done.1.refs_2_, ...), custom_call_target="tpu_custom_call" | custom-call | flops 1 | bytes 1 | tf_op jit(solution)/shard_map/apply_layer/pallas_call | solution.py:124
  60.1 0.9 collective-permute-start.21
  61.0 2.5 %collective-permute-done.11.refs_0_ = bf16[32,8192]{1,0:T(8,128)(2,1)S(1)} collective-permute-done((bf16[32,8192]{1,0:T(8,128)(2,1)S(1)}, bf16[32,8192]{1,0:T(8,128)(2,1)S(1)}, u32[]{:S(2)}, u32[]{:S(2)}) %collective-permute-start.11) | collective-permute-done | bytes 524320 | tf_op jit(solution)/shard_map/ppermute | solution.py:143
  63.5 1.3 %collective-permute-done.16.refs_2_.refs_0_ = bf16[32,8192]{1,0:T(8,128)(2,1)S(1)} collective-permute-done((bf16[32,8192]{1,0:T(8,128)(2,1)S(1)}, bf16[32,8192]{1,0:T(8,128)(2,1)S(1)}, u32[]{:S(2)}, u32[]{:S(2)}) %collective-permute-start.16) | collective-permute-done | bytes 524320 | tf_op jit(solution)/shard_map/ppermute | solution.py:139
  64.9 0.5 collective-permute-start.19
  65.5 0.9 collective-permute-done.18.refs_3_
  66.4 0.4 collective-permute-done.19.refs_4_
  66.8 4.5 %apply_layer.12.refs_1_.refs_9_ = bf16[32,8192]{1,0:T(8,128)(2,1)S(1)} custom-call(s32[1024]{0:T(1024)S(1)} %fusion.2.refs_4_.place_ref, f32[1]{0:T(128)S(6)} %copy.32.bias_ref, bf16[32,8192]{1,0:T(8,128)(2,1)S(1)} %tie.16.refs_0_, bf16[32,8192]{1,0:T(8,128)(2,1)S(1)} %tie.18.refs_1_, bf16[32,8192]{1,0:T(8,128)(2,1)S(1)} %collective-permute-done.17.refs_2_, ...), custom_call_target="tpu_custom_call" | custom-call | flops 1 | bytes 1 | tf_op jit(solution)/shard_map/apply_layer/pallas_call | solution.py:124
  71.3 0.7 collective-permute-start.20
  72.0 0.5 collective-permute-start.27
  72.5 4.2 %collective-permute-done.22.refs_2_.refs_0_ = bf16[32,8192]{1,0:T(8,128)(2,1)S(1)} collective-permute-done((bf16[32,8192]{1,0:T(8,128)(2,1)S(1)}, bf16[32,8192]{1,0:T(8,128)(2,1)S(1)}, u32[]{:S(2)}, u32[]{:S(2)}) %collective-permute-start.22) | collective-permute-done | bytes 524320 | tf_op jit(solution)/shard_map/ppermute | solution.py:139
  76.8 0.5 collective-permute-start.25
  77.4 0.9 collective-permute-done.24.refs_3_
  78.4 0.4 collective-permute-done.25.refs_4_
  78.7 4.5 %apply_layer.13.refs_1_.refs_9_ = bf16[32,8192]{1,0:T(8,128)(2,1)S(1)} custom-call(s32[1024]{0:T(1024)S(1)} %fusion.2.refs_4_.place_ref, f32[1]{0:T(128)S(6)} %copy.32.bias_ref, bf16[32,8192]{1,0:T(8,128)(2,1)S(1)} %tie.19.refs_0_, bf16[32,8192]{1,0:T(8,128)(2,1)S(1)} %tie.20.refs_1_, bf16[32,8192]{1,0:T(8,128)(2,1)S(1)} %collective-permute-done.23.refs_2_, ...), custom_call_target="tpu_custom_call" | custom-call | flops 1 | bytes 1 | tf_op jit(solution)/shard_map/apply_layer/pallas_call | solution.py:124
  83.2 0.2 collective-permute-start.26
  83.5 0.6 collective-permute-start.32
  84.0 1.7 %collective-permute-done.27.refs_0_ = bf16[32,8192]{1,0:T(8,128)(2,1)S(1)} collective-permute-done((bf16[32,8192]{1,0:T(8,128)(2,1)S(1)}, bf16[32,8192]{1,0:T(8,128)(2,1)S(1)}, u32[]{:S(2)}, u32[]{:S(2)}) %collective-permute-start.27) | collective-permute-done | bytes 524320 | tf_op jit(solution)/shard_map/ppermute | solution.py:143
  85.7 2.3 %collective-permute-done.20.refs_2_ = bf16[32,8192]{1,0:T(8,128)(2,1)S(1)} collective-permute-done((bf16[32,8192]{1,0:T(8,128)(2,1)S(1)}, bf16[32,8192]{1,0:T(8,128)(2,1)S(1)}, u32[]{:S(2)}, u32[]{:S(2)}) %collective-permute-start.20) | collective-permute-done | bytes 524320 | tf_op jit(solution)/shard_map/ppermute | solution.py:139
  88.1 0.5 collective-permute-start.30
  88.7 0.9 collective-permute-done.29.refs_3_
  89.6 0.4 collective-permute-done.30.refs_4_
  90.0 4.5 %apply_layer.14.refs_1_.refs_9_ = bf16[32,8192]{1,0:T(8,128)(2,1)S(1)} custom-call(s32[1024]{0:T(1024)S(1)} %fusion.2.refs_4_.place_ref, f32[1]{0:T(128)S(6)} %copy.32.bias_ref, bf16[32,8192]{1,0:T(8,128)(2,1)S(1)} %tie.21.refs_0_, bf16[32,8192]{1,0:T(8,128)(2,1)S(1)} %tie.22.refs_1_, bf16[32,8192]{1,0:T(8,128)(2,1)S(1)} %collective-permute-done.28.refs_2_, ...), custom_call_target="tpu_custom_call" | custom-call | flops 1 | bytes 1 | tf_op jit(solution)/shard_map/apply_layer/pallas_call | solution.py:124
  94.5 3.0 %collective-permute-done.32.refs_0_ = bf16[32,8192]{1,0:T(8,128)(2,1)S(1)} collective-permute-done((bf16[32,8192]{1,0:T(8,128)(2,1)S(1)}, bf16[32,8192]{1,0:T(8,128)(2,1)S(1)}, u32[]{:S(2)}, u32[]{:S(2)}) %collective-permute-start.32) | collective-permute-done | bytes 524320 | tf_op jit(solution)/shard_map/ppermute | solution.py:143
  97.5 2.7 %collective-permute-done.26.refs_2_ = bf16[32,8192]{1,0:T(8,128)(2,1)S(1)} collective-permute-done((bf16[32,8192]{1,0:T(8,128)(2,1)S(1)}, bf16[32,8192]{1,0:T(8,128)(2,1)S(1)}, u32[]{:S(2)}, u32[]{:S(2)}) %collective-permute-start.26) | collective-permute-done | bytes 524320 | tf_op jit(solution)/shard_map/ppermute | solution.py:139
  100.3 0.5 collective-permute-start.35
  100.8 1.0 collective-permute-done.34.refs_3_
  101.8 0.4 collective-permute-done.35.refs_4_
  102.2 4.5 %apply_layer.15 = bf16[32,8192]{1,0:T(8,128)(2,1)S(1)} custom-call(s32[1024]{0:T(1024)S(1)} %fusion.2.refs_4_.place_ref, f32[1]{0:T(128)S(6)} %copy.32.bias_ref, bf16[32,8192]{1,0:T(8,128)(2,1)S(1)} %tie.24.refs_0_, bf16[32,8192]{1,0:T(8,128)(2,1)S(1)} %tie.25.refs_1_, bf16[32,8192]{1,0:T(8,128)(2,1)S(1)} %collective-permute-done.33.refs_2_, ...), custom_call_target="tpu_custom_call" | custom-call | flops 1 | bytes 1 | tf_op jit(solution)/shard_map/apply_layer/pallas_call | solution.py:124
  106.7 4.6 %collective-permute-done.31.refs_0_ = bf16[32,8192]{1,0:T(8,128)(2,1)S(1)} collective-permute-done((bf16[32,8192]{1,0:T(8,128)(2,1)S(1)}, bf16[32,8192]{1,0:T(8,128)(2,1)S(1)}, u32[]{:S(2)}, u32[]{:S(2)}) %collective-permute-start.31) | collective-permute-done | bytes 524320 | tf_op jit(solution)/shard_map/ppermute | solution.py:139
  111.3 12.1 %collective-permute-done.36 = bf16[32,8192]{1,0:T(8,128)(2,1)S(1)} collective-permute-done((bf16[32,8192]{1,0:T(8,128)(2,1)S(1)}, bf16[32,8192]{1,0:T(8,128)(2,1)S(1)}, u32[]{:S(2)}, u32[]{:S(2)}) %collective-permute-start.36) | collective-permute-done | bytes 524320 | tf_op jit(solution)/shard_map/ppermute | solution.py:139
  123.4 1.5 %pad_maximum_fusion = bf16[128,8192]{1,0:T(8,128)(2,1)} fusion(bf16[32,8192]{1,0:T(8,128)(2,1)S(1)} %collective-permute-done.36, bf16[32,8192]{1,0:T(8,128)(2,1)S(1)} %tie.23, bf16[32,8192]{1,0:T(8,128)(2,1)S(1)} %collective-permute-done.26.refs_2_, bf16[32,8192]{1,0:T(8,128)(2,1)S(1)} %collective-permute-done.20.refs_2_), kind=kLoop, calls=%fused_computation | loop fusion | flops 8388608 | bytes 4194304 | tf_op jit(solution)/shard_map/concatenate | solution.py:261
  (60 shorter events, 1.7 us)
Async XLA Ops:
  0.0 20.4 %collective-permute-start.1 = (bf16[128,8192]{1,0:T(8,128)(2,1)}, bf16[128,8192]{1,0:T(8,128)(2,1)S(1)}, u32[]{:S(2)}, u32[]{:S(2)}) collective-permute-start(bf16[128,8192]{1,0:T(8,128)(2,1)} %refs_0_.7), channel_id=1, source_target_pairs={{0,1},{1,0},{2,3},{3,2},{4,5},{5,4},{6,7},{7,6},{8,9},{9,8},{10,11... | collective-permute-start | bytes 6291464 | tf_op jit(solution)/shard_map/ppermute | solution.py:143
  0.5 1.6 %copy-start.1 = (bf16[128,8192]{1,0:T(8,128)(2,1)S(1)}, bf16[128,8192]{1,0:T(8,128)(2,1)}, u32[]{:S(2)}) copy-start(bf16[128,8192]{1,0:T(8,128)(2,1)} %refs_0_.7) | copy-start | bytes 6291460
  2.0 2.7 %copy-start.3 = (s32[1,128,8]{1,2,0:T(8,128)S(1)}, s32[1,128,8]{1,2,0:T(8,128)}, u32[]{:S(2)}) copy-start(s32[1,128,8]{1,2,0:T(8,128)} %param.6) | copy-start | bytes 12292
  2.1 15.2 %collective-permute-start = (bf16[32,8192]{1,0:T(8,128)(2,1)S(1)}, bf16[32,8192]{1,0:T(8,128)(2,1)S(1)}, u32[]{:S(2)}, u32[]{:S(2)}) collective-permute-start(bf16[32,8192]{1,0:T(8,128)(2,1)S(1)} %row_block.4), channel_id=1, source_target_pairs={{0,2},{1,3},{2,0},{3,1},{4,6},{5,7},{6,4},{7,5},{8,10},{9,11},{10,... | collective-permute-start | bytes 1572872 | tf_op jit(solution)/shard_map/ppermute | solution.py:143
  5.0 3.4 %copy-start = (bf16[1,128,8,4096]{3,2,1,0:T(8,128)(2,1)S(1)}, bf16[1,128,8,4096]{3,2,1,0:T(8,128)(2,1)}, u32[]{:S(2)}) copy-start(bf16[1,128,8,4096]{3,2,1,0:T(8,128)(2,1)} %param.5) | copy-start | bytes 25165828
  8.4 7.0 %copy-start.2 = (bf16[128,8192]{1,0:T(8,128)(2,1)S(1)}, bf16[128,8192]{1,0:T(8,128)(2,1)}, u32[]{:S(2)}) copy-start(bf16[128,8192]{1,0:T(8,128)(2,1)} %refs_0_.7) | copy-start | bytes 6291460
  15.4 14.8 %collective-permute-start.6 = (bf16[32,8192]{1,0:T(8,128)(2,1)S(1)}, bf16[32,8192]{1,0:T(8,128)(2,1)S(1)}, u32[]{:S(2)}, u32[]{:S(2)}) collective-permute-start(bf16[32,8192]{1,0:T(8,128)(2,1)S(1)} %row_block.6), channel_id=1, source_target_pairs={{0,2},{1,3},{2,0},{3,1},{4,6},{5,7},{6,4},{7,5},{8,10},{9,11},{10,... | collective-permute-start | bytes 1572872 | tf_op jit(solution)/shard_map/ppermute | solution.py:143
  17.3 3.1 %collective-permute-start.2 = (bf16[32,4096]{1,0:T(8,128)(2,1)S(1)}, bf16[32,4096]{1,0:T(8,128)(2,1)S(1)}, u32[]{:S(2)}, u32[]{:S(2)}) collective-permute-start(bf16[32,4096]{1,0:T(8,128)(2,1)S(1)} %get-tuple-element.30), channel_id=1, source_target_pairs={{0,1},{1,0},{2,3},{3,2},{4,5},{5,4},{6,7},{7,6},{8,9},{9,8},{10,11... | collective-permute-start | bytes 786440 | tf_op jit(solution)/shard_map/ppermute | solution.py:143
  17.4 3.0 %collective-permute-start.3 = (bf16[32,4096]{1,0:T(8,128)(2,1)S(1)}, bf16[32,4096]{1,0:T(8,128)(2,1)S(1)}, u32[]{:S(2)}, u32[]{:S(2)}) collective-permute-start(bf16[32,4096]{1,0:T(8,128)(2,1)S(1)} %get-tuple-element.29), channel_id=1, source_target_pairs={{0,1},{1,0},{2,3},{3,2},{4,5},{5,4},{6,7},{7,6},{8,9},{9,8},{10,11... | collective-permute-start | bytes 786440 | tf_op jit(solution)/shard_map/ppermute | solution.py:143
  17.9 23.6 %collective-permute-start.5 = (bf16[32,8192]{1,0:T(8,128)(2,1)S(1)}, bf16[32,8192]{1,0:T(8,128)(2,1)S(1)}, u32[]{:S(2)}, u32[]{:S(2)}) collective-permute-start(bf16[32,8192]{1,0:T(8,128)(2,1)S(1)} %row_block.5), channel_id=1, source_target_pairs={{0,2},{1,3},{2,0},{3,1},{4,6},{5,7},{6,4},{7,5},{8,10},{9,11},{10,... | collective-permute-start | bytes 1572872 | tf_op jit(solution)/shard_map/ppermute | solution.py:143
  24.9 16.6 %collective-permute-start.4 = (bf16[32,8192]{1,0:T(8,128)(2,1)S(1)}, bf16[32,8192]{1,0:T(8,128)(2,1)S(1)}, u32[]{:S(2)}, u32[]{:S(2)}) collective-permute-start(bf16[32,8192]{1,0:T(8,128)(2,1)S(1)} %apply_layer.8.refs_1_.refs_9_), channel_id=1, source_target_pairs={{0,4},{4,8},{8,12},{12,16},{16,20},{20,24},{24,28},{28,0},{1,5},{5... | collective-permute-start | bytes 1572872 | tf_op jit(solution)/shard_map/ppermute | solution.py:139
  30.3 1.6 %collective-permute-start.7 = (bf16[32,4096]{1,0:T(8,128)(2,1)S(1)}, bf16[32,4096]{1,0:T(8,128)(2,1)S(1)}, u32[]{:S(2)}, u32[]{:S(2)}) collective-permute-start(bf16[32,4096]{1,0:T(8,128)(2,1)S(1)} %get-tuple-element.28), channel_id=1, source_target_pairs={{0,1},{1,0},{2,3},{3,2},{4,5},{5,4},{6,7},{7,6},{8,9},{9,8},{10,11... | collective-permute-start | bytes 786440 | tf_op jit(solution)/shard_map/ppermute | solution.py:143
  30.3 1.9 %collective-permute-start.8 = (bf16[32,4096]{1,0:T(8,128)(2,1)S(1)}, bf16[32,4096]{1,0:T(8,128)(2,1)S(1)}, u32[]{:S(2)}, u32[]{:S(2)}) collective-permute-start(bf16[32,4096]{1,0:T(8,128)(2,1)S(1)} %get-tuple-element.27), channel_id=1, source_target_pairs={{0,1},{1,0},{2,3},{3,2},{4,5},{5,4},{6,7},{7,6},{8,9},{9,8},{10,11... | collective-permute-start | bytes 786440 | tf_op jit(solution)/shard_map/ppermute | solution.py:143
  30.9 21.1 %collective-permute-start.12 = (bf16[32,8192]{1,0:T(8,128)(2,1)S(1)}, bf16[32,8192]{1,0:T(8,128)(2,1)S(1)}, u32[]{:S(2)}, u32[]{:S(2)}) collective-permute-start(bf16[32,8192]{1,0:T(8,128)(2,1)S(1)} %row_block.7), channel_id=1, source_target_pairs={{0,2},{1,3},{2,0},{3,1},{4,6},{5,7},{6,4},{7,5},{8,10},{9,11},{10,... | collective-permute-start | bytes 1572872 | tf_op jit(solution)/shard_map/ppermute | solution.py:143
  36.7 16.8 %collective-permute-start.13 = (bf16[32,8192]{1,0:T(8,128)(2,1)S(1)}, bf16[32,8192]{1,0:T(8,128)(2,1)S(1)}, u32[]{:S(2)}, u32[]{:S(2)}) collective-permute-start(bf16[32,8192]{1,0:T(8,128)(2,1)S(1)} %apply_layer.9.refs_1_.refs_9_), channel_id=1, source_target_pairs={{0,4},{4,8},{8,12},{12,16},{16,20},{20,24},{24,28},{28,0},{1,5},{5... | collective-permute-start | bytes 1572872 | tf_op jit(solution)/shard_map/ppermute | solution.py:139
  41.5 1.6 %collective-permute-start.9 = (bf16[32,4096]{1,0:T(8,128)(2,1)S(1)}, bf16[32,4096]{1,0:T(8,128)(2,1)S(1)}, u32[]{:S(2)}, u32[]{:S(2)}) collective-permute-start(bf16[32,4096]{1,0:T(8,128)(2,1)S(1)} %get-tuple-element.26), channel_id=1, source_target_pairs={{0,1},{1,0},{2,3},{3,2},{4,5},{5,4},{6,7},{7,6},{8,9},{9,8},{10,11... | collective-permute-start | bytes 786440 | tf_op jit(solution)/shard_map/ppermute | solution.py:143
  41.6 1.9 %collective-permute-start.10 = (bf16[32,4096]{1,0:T(8,128)(2,1)S(1)}, bf16[32,4096]{1,0:T(8,128)(2,1)S(1)}, u32[]{:S(2)}, u32[]{:S(2)}) collective-permute-start(bf16[32,4096]{1,0:T(8,128)(2,1)S(1)} %get-tuple-element.25), channel_id=1, source_target_pairs={{0,1},{1,0},{2,3},{3,2},{4,5},{5,4},{6,7},{7,6},{8,9},{9,8},{10,11... | collective-permute-start | bytes 786440 | tf_op jit(solution)/shard_map/ppermute | solution.py:143
  47.9 16.8 %collective-permute-start.16 = (bf16[32,8192]{1,0:T(8,128)(2,1)S(1)}, bf16[32,8192]{1,0:T(8,128)(2,1)S(1)}, u32[]{:S(2)}, u32[]{:S(2)}) collective-permute-start(bf16[32,8192]{1,0:T(8,128)(2,1)S(1)} %apply_layer.10.refs_1_.refs_9_), channel_id=1, source_target_pairs={{0,4},{4,8},{8,12},{12,16},{16,20},{20,24},{24,28},{28,0},{1,5},{5... | collective-permute-start | bytes 1572872 | tf_op jit(solution)/shard_map/ppermute | solution.py:139
  49.5 14.0 %collective-permute-start.11 = (bf16[32,8192]{1,0:T(8,128)(2,1)S(1)}, bf16[32,8192]{1,0:T(8,128)(2,1)S(1)}, u32[]{:S(2)}, u32[]{:S(2)}) collective-permute-start(bf16[32,8192]{1,0:T(8,128)(2,1)S(1)} %tie.16.refs_0_), channel_id=1, source_target_pairs={{0,2},{1,3},{2,0},{3,1},{4,6},{5,7},{6,4},{7,5},{8,10},{9,11},{10,... | collective-permute-start | bytes 1572872 | tf_op jit(solution)/shard_map/ppermute | solution.py:143
  53.6 1.6 %collective-permute-start.14 = (bf16[32,4096]{1,0:T(8,128)(2,1)S(1)}, bf16[32,4096]{1,0:T(8,128)(2,1)S(1)}, u32[]{:S(2)}, u32[]{:S(2)}) collective-permute-start(bf16[32,4096]{1,0:T(8,128)(2,1)S(1)} %get-tuple-element.24), channel_id=1, source_target_pairs={{0,1},{1,0},{2,3},{3,2},{4,5},{5,4},{6,7},{7,6},{8,9},{9,8},{10,11... | collective-permute-start | bytes 786440 | tf_op jit(solution)/shard_map/ppermute | solution.py:143
  53.7 1.9 %collective-permute-start.15 = (bf16[32,4096]{1,0:T(8,128)(2,1)S(1)}, bf16[32,4096]{1,0:T(8,128)(2,1)S(1)}, u32[]{:S(2)}, u32[]{:S(2)}) collective-permute-start(bf16[32,4096]{1,0:T(8,128)(2,1)S(1)} %get-tuple-element.23), channel_id=1, source_target_pairs={{0,1},{1,0},{2,3},{3,2},{4,5},{5,4},{6,7},{7,6},{8,9},{9,8},{10,11... | collective-permute-start | bytes 786440 | tf_op jit(solution)/shard_map/ppermute | solution.py:143
  54.2 11.2 %collective-permute-start.17 = (bf16[32,8192]{1,0:T(8,128)(2,1)S(1)}, bf16[32,8192]{1,0:T(8,128)(2,1)S(1)}, u32[]{:S(2)}, u32[]{:S(2)}) collective-permute-start(bf16[32,8192]{1,0:T(8,128)(2,1)S(1)} %tie.16.refs_0_), channel_id=1, source_target_pairs={{0,1},{1,0},{2,3},{3,2},{4,5},{5,4},{6,7},{7,6},{8,9},{9,8},{10,11... | collective-permute-start | bytes 1572872 | tf_op jit(solution)/shard_map/ppermute | solution.py:143
  60.0 16.7 %collective-permute-start.22 = (bf16[32,8192]{1,0:T(8,128)(2,1)S(1)}, bf16[32,8192]{1,0:T(8,128)(2,1)S(1)}, u32[]{:S(2)}, u32[]{:S(2)}) collective-permute-start(bf16[32,8192]{1,0:T(8,128)(2,1)S(1)} %apply_layer.11.refs_1_.refs_9_), channel_id=1, source_target_pairs={{0,4},{4,8},{8,12},{12,16},{16,20},{20,24},{24,28},{28,0},{1,5},{5... | collective-permute-start | bytes 1572872 | tf_op jit(solution)/shard_map/ppermute | solution.py:139
  60.1 16.6 %collective-permute-start.21 = (bf16[32,8192]{1,0:T(8,128)(2,1)S(1)}, bf16[32,8192]{1,0:T(8,128)(2,1)S(1)}, u32[]{:S(2)}, u32[]{:S(2)}) collective-permute-start(bf16[32,8192]{1,0:T(8,128)(2,1)S(1)} %tie.19.refs_0_), channel_id=1, source_target_pairs={{0,2},{1,3},{2,0},{3,1},{4,6},{5,7},{6,4},{7,5},{8,10},{9,11},{10,... | collective-permute-start | bytes 1572872 | tf_op jit(solution)/shard_map/ppermute | solution.py:143
  64.8 1.6 %collective-permute-start.18 = (bf16[32,4096]{1,0:T(8,128)(2,1)S(1)}, bf16[32,4096]{1,0:T(8,128)(2,1)S(1)}, u32[]{:S(2)}, u32[]{:S(2)}) collective-permute-start(bf16[32,4096]{1,0:T(8,128)(2,1)S(1)} %get-tuple-element.22), channel_id=1, source_target_pairs={{0,1},{1,0},{2,3},{3,2},{4,5},{5,4},{6,7},{7,6},{8,9},{9,8},{10,11... | collective-permute-start | bytes 786440 | tf_op jit(solution)/shard_map/ppermute | solution.py:143
  64.9 1.9 %collective-permute-start.19 = (bf16[32,4096]{1,0:T(8,128)(2,1)S(1)}, bf16[32,4096]{1,0:T(8,128)(2,1)S(1)}, u32[]{:S(2)}, u32[]{:S(2)}) collective-permute-start(bf16[32,4096]{1,0:T(8,128)(2,1)S(1)} %get-tuple-element.21), channel_id=1, source_target_pairs={{0,1},{1,0},{2,3},{3,2},{4,5},{5,4},{6,7},{7,6},{8,9},{9,8},{10,11... | collective-permute-start | bytes 786440 | tf_op jit(solution)/shard_map/ppermute | solution.py:143
  65.4 11.9 %collective-permute-start.23 = (bf16[32,8192]{1,0:T(8,128)(2,1)S(1)}, bf16[32,8192]{1,0:T(8,128)(2,1)S(1)}, u32[]{:S(2)}, u32[]{:S(2)}) collective-permute-start(bf16[32,8192]{1,0:T(8,128)(2,1)S(1)} %tie.19.refs_0_), channel_id=1, source_target_pairs={{0,1},{1,0},{2,3},{3,2},{4,5},{5,4},{6,7},{7,6},{8,9},{9,8},{10,11... | collective-permute-start | bytes 1572872 | tf_op jit(solution)/shard_map/ppermute | solution.py:143
  71.3 16.7 %collective-permute-start.20 = (bf16[32,8192]{1,0:T(8,128)(2,1)S(1)}, bf16[32,8192]{1,0:T(8,128)(2,1)S(1)}, u32[]{:S(2)}, u32[]{:S(2)}) collective-permute-start(bf16[32,8192]{1,0:T(8,128)(2,1)S(1)} %apply_layer.12.refs_1_.refs_9_), channel_id=1, source_target_pairs={{0,4},{4,8},{8,12},{12,16},{16,20},{20,24},{24,28},{28,0},{1,5},{5... | collective-permute-start | bytes 1572872 | tf_op jit(solution)/shard_map/ppermute | solution.py:139
  72.0 13.7 %collective-permute-start.27 = (bf16[32,8192]{1,0:T(8,128)(2,1)S(1)}, bf16[32,8192]{1,0:T(8,128)(2,1)S(1)}, u32[]{:S(2)}, u32[]{:S(2)}) collective-permute-start(bf16[32,8192]{1,0:T(8,128)(2,1)S(1)} %tie.21.refs_0_), channel_id=1, source_target_pairs={{0,2},{1,3},{2,0},{3,1},{4,6},{5,7},{6,4},{7,5},{8,10},{9,11},{10,... | collective-permute-start | bytes 1572872 | tf_op jit(solution)/shard_map/ppermute | solution.py:143
  76.8 1.6 %collective-permute-start.24 = (bf16[32,4096]{1,0:T(8,128)(2,1)S(1)}, bf16[32,4096]{1,0:T(8,128)(2,1)S(1)}, u32[]{:S(2)}, u32[]{:S(2)}) collective-permute-start(bf16[32,4096]{1,0:T(8,128)(2,1)S(1)} %get-tuple-element.20), channel_id=1, source_target_pairs={{0,1},{1,0},{2,3},{3,2},{4,5},{5,4},{6,7},{7,6},{8,9},{9,8},{10,11... | collective-permute-start | bytes 786440 | tf_op jit(solution)/shard_map/ppermute | solution.py:143
  76.8 1.9 %collective-permute-start.25 = (bf16[32,4096]{1,0:T(8,128)(2,1)S(1)}, bf16[32,4096]{1,0:T(8,128)(2,1)S(1)}, u32[]{:S(2)}, u32[]{:S(2)}) collective-permute-start(bf16[32,4096]{1,0:T(8,128)(2,1)S(1)} %get-tuple-element.19), channel_id=1, source_target_pairs={{0,1},{1,0},{2,3},{3,2},{4,5},{5,4},{6,7},{7,6},{8,9},{9,8},{10,11... | collective-permute-start | bytes 786440 | tf_op jit(solution)/shard_map/ppermute | solution.py:143
  77.3 11.3 %collective-permute-start.28 = (bf16[32,8192]{1,0:T(8,128)(2,1)S(1)}, bf16[32,8192]{1,0:T(8,128)(2,1)S(1)}, u32[]{:S(2)}, u32[]{:S(2)}) collective-permute-start(bf16[32,8192]{1,0:T(8,128)(2,1)S(1)} %tie.21.refs_0_), channel_id=1, source_target_pairs={{0,1},{1,0},{2,3},{3,2},{4,5},{5,4},{6,7},{7,6},{8,9},{9,8},{10,11... | collective-permute-start | bytes 1572872 | tf_op jit(solution)/shard_map/ppermute | solution.py:143
  83.2 17.0 %collective-permute-start.26 = (bf16[32,8192]{1,0:T(8,128)(2,1)S(1)}, bf16[32,8192]{1,0:T(8,128)(2,1)S(1)}, u32[]{:S(2)}, u32[]{:S(2)}) collective-permute-start(bf16[32,8192]{1,0:T(8,128)(2,1)S(1)} %apply_layer.13.refs_1_.refs_9_), channel_id=1, source_target_pairs={{0,4},{4,8},{8,12},{12,16},{16,20},{20,24},{24,28},{28,0},{1,5},{5... | collective-permute-start | bytes 1572872 | tf_op jit(solution)/shard_map/ppermute | solution.py:139
  83.5 14.0 %collective-permute-start.32 = (bf16[32,8192]{1,0:T(8,128)(2,1)S(1)}, bf16[32,8192]{1,0:T(8,128)(2,1)S(1)}, u32[]{:S(2)}, u32[]{:S(2)}) collective-permute-start(bf16[32,8192]{1,0:T(8,128)(2,1)S(1)} %tie.24.refs_0_), channel_id=1, source_target_pairs={{0,2},{1,3},{2,0},{3,1},{4,6},{5,7},{6,4},{7,5},{8,10},{9,11},{10,... | collective-permute-start | bytes 1572872 | tf_op jit(solution)/shard_map/ppermute | solution.py:143
  88.0 1.6 %collective-permute-start.29 = (bf16[32,4096]{1,0:T(8,128)(2,1)S(1)}, bf16[32,4096]{1,0:T(8,128)(2,1)S(1)}, u32[]{:S(2)}, u32[]{:S(2)}) collective-permute-start(bf16[32,4096]{1,0:T(8,128)(2,1)S(1)} %get-tuple-element.18), channel_id=1, source_target_pairs={{0,1},{1,0},{2,3},{3,2},{4,5},{5,4},{6,7},{7,6},{8,9},{9,8},{10,11... | collective-permute-start | bytes 786440 | tf_op jit(solution)/shard_map/ppermute | solution.py:143
  88.1 1.9 %collective-permute-start.30 = (bf16[32,4096]{1,0:T(8,128)(2,1)S(1)}, bf16[32,4096]{1,0:T(8,128)(2,1)S(1)}, u32[]{:S(2)}, u32[]{:S(2)}) collective-permute-start(bf16[32,4096]{1,0:T(8,128)(2,1)S(1)} %get-tuple-element.17), channel_id=1, source_target_pairs={{0,1},{1,0},{2,3},{3,2},{4,5},{5,4},{6,7},{7,6},{8,9},{9,8},{10,11... | collective-permute-start | bytes 786440 | tf_op jit(solution)/shard_map/ppermute | solution.py:143
  88.6 12.2 %collective-permute-start.33 = (bf16[32,8192]{1,0:T(8,128)(2,1)S(1)}, bf16[32,8192]{1,0:T(8,128)(2,1)S(1)}, u32[]{:S(2)}, u32[]{:S(2)}) collective-permute-start(bf16[32,8192]{1,0:T(8,128)(2,1)S(1)} %tie.24.refs_0_), channel_id=1, source_target_pairs={{0,1},{1,0},{2,3},{3,2},{4,5},{5,4},{6,7},{7,6},{8,9},{9,8},{10,11... | collective-permute-start | bytes 1572872 | tf_op jit(solution)/shard_map/ppermute | solution.py:143
  94.5 16.9 %collective-permute-start.31 = (bf16[32,8192]{1,0:T(8,128)(2,1)S(1)}, bf16[32,8192]{1,0:T(8,128)(2,1)S(1)}, u32[]{:S(2)}, u32[]{:S(2)}) collective-permute-start(bf16[32,8192]{1,0:T(8,128)(2,1)S(1)} %apply_layer.14.refs_1_.refs_9_), channel_id=1, source_target_pairs={{0,4},{4,8},{8,12},{12,16},{16,20},{20,24},{24,28},{28,0},{1,5},{5... | collective-permute-start | bytes 1572872 | tf_op jit(solution)/shard_map/ppermute | solution.py:139
  100.2 1.6 %collective-permute-start.34 = (bf16[32,4096]{1,0:T(8,128)(2,1)S(1)}, bf16[32,4096]{1,0:T(8,128)(2,1)S(1)}, u32[]{:S(2)}, u32[]{:S(2)}) collective-permute-start(bf16[32,4096]{1,0:T(8,128)(2,1)S(1)} %get-tuple-element.16), channel_id=1, source_target_pairs={{0,1},{1,0},{2,3},{3,2},{4,5},{5,4},{6,7},{7,6},{8,9},{9,8},{10,11... | collective-permute-start | bytes 786440 | tf_op jit(solution)/shard_map/ppermute | solution.py:143
  100.3 1.9 %collective-permute-start.35 = (bf16[32,4096]{1,0:T(8,128)(2,1)S(1)}, bf16[32,4096]{1,0:T(8,128)(2,1)S(1)}, u32[]{:S(2)}, u32[]{:S(2)}) collective-permute-start(bf16[32,4096]{1,0:T(8,128)(2,1)S(1)} %get-tuple-element.15), channel_id=1, source_target_pairs={{0,1},{1,0},{2,3},{3,2},{4,5},{5,4},{6,7},{7,6},{8,9},{9,8},{10,11... | collective-permute-start | bytes 786440 | tf_op jit(solution)/shard_map/ppermute | solution.py:143
  106.7 16.7 %collective-permute-start.36 = (bf16[32,8192]{1,0:T(8,128)(2,1)S(1)}, bf16[32,8192]{1,0:T(8,128)(2,1)S(1)}, u32[]{:S(2)}, u32[]{:S(2)}) collective-permute-start(bf16[32,8192]{1,0:T(8,128)(2,1)S(1)} %apply_layer.15), channel_id=1, source_target_pairs={{0,4},{4,8},{8,12},{12,16},{16,20},{20,24},{24,28},{28,0},{1,5},{5... | collective-permute-start | bytes 1572872 | tf_op jit(solution)/shard_map/ppermute | solution.py:139

commit v4 on v3

--- a/solution.py
+++ b/solution.py
@@ -70,46 +70,46 @@
     )(*[tiles] * STREAMS, earlier)
 
 
-def layer_body(parts, waited, place_ref, bias_ref, *refs):
-    pieces = sum(parts)
+def layer_body(pieces, waited, place_ref, bias_ref, *refs):
     piece_refs, weight_refs = refs[:pieces], refs[pieces:pieces + STREAMS]
     out_ref, tile_ref = refs[pieces + STREAMS + waited:]
     rows = out_ref.shape[0]
     turned = tile_ref.shape[0] // 2
-    step = pl.program_id(0)
-    fanin = weight_refs[0].shape[1] // BLK
-
-    @pl.when(step == 0)
-    def _():
-        place = 0
-        for ref in piece_refs:
-            for t in range(ref.shape[1] // LANES):
-                tile = ref[:, t * LANES:(t + 1) * LANES]
-                tile_ref[place] = tile
-                tile_ref[turned + place] = jnp.concatenate([tile[:, BLK:], tile[:, :BLK]], axis=1)
-                place += 1
+    steps, depth, width = weight_refs[0].shape
+    fanin = depth // BLK
+
+    place = 0
+    for ref in piece_refs:
+        for t in range(ref.shape[1] // LANES):
+            tile = ref[:, t * LANES:(t + 1) * LANES]
+            tile_ref[place] = tile
+            tile_ref[turned + place] = jnp.concatenate([tile[:, BLK:], tile[:, :BLK]], axis=1)
+            place += 1
 
     low = lax.broadcasted_iota(jnp.int32, (rows, LANES), 1) < BLK
     bias = bias_ref[0]
-    for q, weight_ref in enumerate(weight_refs):
-        stacked = []
-        for member in range(WIDE):
-            base = ((step * STREAMS + q) * WIDE + member) * fanin
-            picked = []
-            for k in range(0, fanin, 2):
-                left = tile_ref[place_ref[base + k]]
-                right = tile_ref[place_ref[base + k + 1]]
-                picked.append(jnp.where(low, left, right))
-            stacked.append(jnp.concatenate(picked, axis=1))
-        lhs = jnp.concatenate(stacked, axis=0)
-        sums = jnp.dot(lhs, weight_ref[0], preferred_element_type=jnp.float32)
-        for pair in range(WIDE // 2):
-            lanes = slice(pair * LANES, (pair + 1) * LANES)
-            first = sums[2 * pair * rows:(2 * pair + 1) * rows, lanes]
-            second = sums[(2 * pair + 1) * rows:(2 * pair + 2) * rows, lanes]
-            result = jnp.maximum(jnp.where(low, first, second) + bias, 0.0)
-            start = (q * (WIDE // 2) + pair) * LANES
-            out_ref[:, start:start + LANES] = result.astype(jnp.bfloat16)
+
+    @pl.loop(0, steps, unroll=steps)
+    def _(step):
+        for q, weight_ref in enumerate(weight_refs):
+            stacked = []
+            for member in range(WIDE):
+                base = ((step * STREAMS + q) * WIDE + member) * fanin
+                picked = []
+                for k in range(0, fanin, 2):
+                    left = tile_ref[place_ref[base + k]]
+                    right = tile_ref[place_ref[base + k + 1]]
+                    picked.append(jnp.where(low, left, right))
+                stacked.append(jnp.concatenate(picked, axis=1))
+            lhs = jnp.concatenate(stacked, axis=0)
+            sums = jnp.dot(lhs, weight_ref[step], preferred_element_type=jnp.float32)
+            for pair in range(WIDE // 2):
+                lanes = slice(pair * LANES, (pair + 1) * LANES)
+                first = sums[2 * pair * rows:(2 * pair + 1) * rows, lanes]
+                second = sums[(2 * pair + 1) * rows:(2 * pair + 2) * rows, lanes]
+                result = jnp.maximum(jnp.where(low, first, second) + bias, 0.0)
+                start = pl.multiple_of((step * STREAMS + q) * width + pair * LANES, LANES)
+                out_ref[:, pl.ds(start, LANES)] = result.astype(jnp.bfloat16)
 
 
 def apply_layer(rows, parts, weights, places, layer_bias, earlier):
@@ -118,17 +118,20 @@
     steps, depth, width = weights[0].shape
     in_specs = [pl.BlockSpec(memory_space=pltpu.SMEM), pl.BlockSpec(memory_space=pltpu.SMEM)]
     for array, block in pieces:
-        in_specs.append(pl.BlockSpec((rows, array.shape[1]), lambda i, block=block: (block, 0), pipeline_mode=pl.Buffered(1)))
-    in_specs += [pl.BlockSpec((1, depth, width), lambda i: (i, 0, 0))] * STREAMS
+        if array.shape[0] == rows:
+            in_specs.append(pl.BlockSpec(memory_space=pltpu.VMEM))
+        else:
+            in_specs.append(pl.BlockSpec((rows, array.shape[1]), lambda i, block=block: (block, 0), pipeline_mode=pl.Buffered(1)))
+    in_specs += [pl.BlockSpec(memory_space=pltpu.VMEM)] * STREAMS
     in_specs += [pl.BlockSpec(memory_space=pl.ANY)] * len(earlier)
     return pl.pallas_call(
-        functools.partial(layer_body, [len(part) for part in parts], len(earlier)),
-        grid=(steps,),
+        functools.partial(layer_body, len(pieces), len(earlier)),
+        grid=(1,),
         in_specs=in_specs,
-        out_specs=pl.BlockSpec((rows, STREAMS * width), lambda i: (0, i)),
+        out_specs=pl.BlockSpec(memory_space=pltpu.VMEM),
         out_shape=jax.ShapeDtypeStruct((rows, steps * STREAMS * width), jnp.bfloat16),
         scratch_shapes=[pltpu.VMEM((2 * columns // LANES, rows, LANES), jnp.bfloat16)],
-        compiler_params=pltpu.CompilerParams(vmem_limit_bytes=ROOMY),
+        compiler_params=pltpu.CompilerParams(vmem_limit_bytes=24 * MIB),
         cost_estimate=TINY,
         name="apply_layer",
     )(places, layer_bias, *[array for array, _ in pieces], *weights, *earlier)
@@ -238,7 +241,7 @@
         rows, start = CHUNKS[n % count], starts[n % count]
         if n < count:
             chunk = row_block(activations, start // rows, rows, [token] if n == 1 else [])
-            own.append((activations, start // rows))
+            own.append((chunk, 0))
             near.append((near_first, start // rows))
         else:
             chunk = tie(moved[n - count], calls[n - 2])
@@ -258,7 +261,10 @@
         if n + 2 < TICKS * count:
             send(n + 2)
     moved[-2] = tie(moved[-2], cost=SOME)
-    return jnp.concatenate(moved[-count:], axis=0)
+    whole = None
+    for c in range(count):
+        whole = put_rows(moved[c - count], starts[c], activations.shape[0], whole)
+    return whole
 
 
 def solution(mesh):

time: 125 us -> 121 us (0.968)
  Pallas kernels: 42.8 us -> 35.2 us
  starting transfers between devices: 19.1 us -> 25.3 us
  other arithmetic: 1.53 us -> 0.04 us
  waiting for transfers between devices: 55 us -> 53.6 us
    ppermute x8, waiting for transfers between devices: 28.6 us -> 14.2 us  [from_behind(): lax.ppermute(array, axis, [(i, (i + by) % size) for i in range(size)])]
    ppermute x29, waiting for transfers between devices: 26.3 us -> 39.4 us  [swapped(): lax.ppermute(array, axis, [(i, i ^ bit) for i in range(lax.axis_size(axis...]
    pallas_call x8 -> x12, Pallas kernels: 35.6 us -> 28 us  [the longest x8 24.8 us: apply_layer(): pl.pallas_call(functools.partial(layer_body, len(pieces), len(earlier)),...]
    ppermute x8, starting transfers between devices: 5.88 us -> 12.6 us  [from_behind(): lax.ppermute(array, axis, [(i, (i + by) % size) for i in range(size)])]
    concatenate x1 -> x0, other arithmetic: 1.49 us -> none  [per_device(): return jnp.concatenate(moved[-count:], axis=0)]
  transfers between devices with their start and end apart: 37 -> 37, of which waited for: 28 -> 25; matrix products, arithmetic and copies ran while one was open for 0% -> 0% of each run, Pallas kernels for 34% -> 28%
where the time goes in v4:
time: 121 us
  waiting for transfers between devices  53.6 us (44%)
  Pallas kernels  35.2 us (29%)
  starting transfers between devices  25.3 us (21%)
  local copies, waits for them, and re-layouts  5.54 us (5%)
    ppermute x29, waiting for transfers between devices, swapped(): lax.ppermute(array, axis, [(i, i ^ bit) for i in range(lax.axis_size(axis...  39.4 us
    pallas_call x8, Pallas kernels, apply_layer(): pl.pallas_call(functools.partial(layer_body, len(pieces), len(earlier)),...  24.8 us
    ppermute x8, waiting for transfers between devices, from_behind(): lax.ppermute(array, axis, [(i, (i + by) % size) for i in range(size)])  14.2 us
    ppermute x29, starting transfers between devices, swapped(): lax.ppermute(array, axis, [(i, i ^ bit) for i in range(lax.axis_size(axis...  12.7 us
    ppermute x8, starting transfers between devices, from_behind(): lax.ppermute(array, axis, [(i, (i + by) % size) for i in range(size)])  12.6 us
    pallas_call x1, Pallas kernels, arrange_weights(): pl.pallas_call(arrange_body, grid=(steps,), in_specs=[pl.BlockSpec((WIDE,...  6.97 us
    unnamed x9, local copies, waits for them, and re-layouts  5.08 us
    pallas_call x4, Pallas kernels, put_rows(): pl.pallas_call(functools.partial(put_body, start), in_specs=[anywhere] *...  3.21 us
  transfers between devices with their start and end apart: 37, of which 25 were waited for; matrix products, arithmetic and copies ran while one was open for 0% of the time, Pallas kernels for 28%

profile of v4, /device:TPU:0, one launch (start us, length us, event | category | flops | bytes accessed | tf_op | source)
XLA Modules:
  0.0 120.8 jit_solution(5220544358754641000)
XLA Ops:
  0.0 0.5 collective-permute-start.4
  0.5 1.6 %copy-done.1 = bf16[128,8192]{1,0:T(8,128)(2,1)S(1)} copy-done((bf16[128,8192]{1,0:T(8,128)(2,1)S(1)}, bf16[128,8192]{1,0:T(8,128)(2,1)}, u32[]{:S(2)}) %copy-start.1) | copy-done | bytes 2097176
  2.1 2.6 %collective-permute-start.3 = (bf16[32,8192]{1,0:T(8,128)(2,1)S(1)}, bf16[32,8192]{1,0:T(8,128)(2,1)S(1)}, u32[]{:S(2)}, u32[]{:S(2)}) collective-permute-start(bf16[32,8192]{1,0:T(8,128)(2,1)S(1)} %row_block.7.refs_0_), channel_id=1, source_target_pairs={{0,2},{1,3},{2,0},{3,1},{4,6},{5,7},{6,4},{7,5},{8,10},{9,11},{10,... | collective-permute-start | bytes 1572872 | tf_op jit(solution)/shard_map/ppermute | solution.py:146
  5.0 3.4 %copy-done = bf16[1,128,8,4096]{3,2,1,0:T(8,128)(2,1)S(1)} copy-done((bf16[1,128,8,4096]{3,2,1,0:T(8,128)(2,1)S(1)}, bf16[1,128,8,4096]{3,2,1,0:T(8,128)(2,1)}, u32[]{:S(2)}) %copy-start) | copy-done | bytes 8388632
  8.4 7.0 %arrange_weights.1 = (bf16[8,512,256]{2,1,0:T(8,128)(2,1)S(1)}, bf16[8,512,256]{2,1,0:T(8,128)(2,1)S(1)}, bf16[8,512,256]{2,1,0:T(8,128)(2,1)S(1)}, bf16[8,512,256]{2,1,0:T(8,128)(2,1)S(1)}, f32[8,128]{1,0:T(8,128)S(1)}) custom-call(bf16[128,8,4096]{2,1,0:T(8,128)(2,1)S(1)} %bitcast.1, bf16[128,8,4096]{2,1,0:T(8,128)(2,1)S(1)} %bitcast.2, ...), custom_call_target="tpu_custom_call" | custom-call | flops 1 | bytes 1 | tf_op jit(solution)/shard_map/arrange_weights/pallas_call | solution.py:59
  15.4 0.5 collective-permute-start.2
  15.9 1.3 %collective-permute-done.3.refs_0_ = bf16[32,8192]{1,0:T(8,128)(2,1)S(1)} collective-permute-done((bf16[32,8192]{1,0:T(8,128)(2,1)S(1)}, bf16[32,8192]{1,0:T(8,128)(2,1)S(1)}, u32[]{:S(2)}, u32[]{:S(2)}) %collective-permute-start.3) | collective-permute-done | bytes 524320 | tf_op jit(solution)/shard_map/ppermute | solution.py:146
  17.4 0.5 collective-permute-start.5
  17.9 1.8 %collective-permute-start.1 = (bf16[32,8192]{1,0:T(8,128)(2,1)S(1)}, bf16[32,8192]{1,0:T(8,128)(2,1)S(1)}, u32[]{:S(2)}, u32[]{:S(2)}) collective-permute-start(bf16[32,8192]{1,0:T(8,128)(2,1)S(1)} %row_block.5.refs_0_), channel_id=1, source_target_pairs={{0,2},{1,3},{2,0},{3,1},{4,6},{5,7},{6,4},{7,5},{8,10},{9,11},{10,... | collective-permute-start | bytes 1572872 | tf_op jit(solution)/shard_map/ppermute | solution.py:146
  20.4 3.1 %apply_layer.8.refs_1_.refs_9_ = bf16[32,8192]{1,0:T(8,128)(2,1)S(1)} custom-call(s32[1024]{0:T(1024)S(1)} %fusion.2.refs_4_.place_ref, f32[1]{0:T(128)S(6)} %copy.38.bias_ref, bf16[32,8192]{1,0:T(8,128)(2,1)S(1)} %row_block.7.refs_0_, bf16[32,8192]{1,0:T(8,128)(2,1)S(1)} %tie.13.refs_1_, bf16[128,8192]{1,0:T(8,128)(2,1)S(1)} %collective-permute-done.4.refs_2_, ...), custom_call_target="tpu_custom_call" | custom-call | flops 1 | bytes 1 | tf_op jit(solution)/shard_map/apply_layer/pallas_call | solution.py:127
  23.5 1.6 %collective-permute-start.9 = (bf16[32,8192]{1,0:T(8,128)(2,1)S(1)}, bf16[32,8192]{1,0:T(8,128)(2,1)S(1)}, u32[]{:S(2)}, u32[]{:S(2)}) collective-permute-start(bf16[32,8192]{1,0:T(8,128)(2,1)S(1)} %apply_layer.8.refs_1_.refs_9_), channel_id=1, source_target_pairs={{0,4},{4,8},{8,12},{12,16},{16,20},{20,24},{24,28},{28,0},{1,5},{5... | collective-permute-start | bytes 1572872 | tf_op jit(solution)/shard_map/ppermute | solution.py:142
  25.1 5.2 %collective-permute-done.2.refs_0_ = bf16[32,8192]{1,0:T(8,128)(2,1)S(1)} collective-permute-done((bf16[32,8192]{1,0:T(8,128)(2,1)S(1)}, bf16[32,8192]{1,0:T(8,128)(2,1)S(1)}, u32[]{:S(2)}, u32[]{:S(2)}) %collective-permute-start.2) | collective-permute-done | bytes 524320 | tf_op jit(solution)/shard_map/ppermute | solution.py:146
  30.3 0.5 collective-permute-start.7
  30.9 0.5 collective-permute-start
  31.4 0.5 collective-permute-done.8.refs_4_
  31.9 0.4 collective-permute-done.7.refs_3_
  32.2 3.1 %apply_layer.9.refs_1_.refs_9_ = bf16[32,8192]{1,0:T(8,128)(2,1)S(1)} custom-call(s32[1024]{0:T(1024)S(1)} %fusion.2.refs_4_.place_ref, f32[1]{0:T(128)S(6)} %copy.38.bias_ref, bf16[32,8192]{1,0:T(8,128)(2,1)S(1)} %row_block.6.refs_0_, bf16[32,8192]{1,0:T(8,128)(2,1)S(1)} %tie.14.refs_1_, bf16[128,8192]{1,0:T(8,128)(2,1)S(1)} %collective-permute-done.4.refs_2_, ...), custom_call_target="tpu_custom_call" | custom-call | flops 1 | bytes 1 | tf_op jit(solution)/shard_map/apply_layer/pallas_call | solution.py:127
  35.3 1.6 %collective-permute-start.12 = (bf16[32,8192]{1,0:T(8,128)(2,1)S(1)}, bf16[32,8192]{1,0:T(8,128)(2,1)S(1)}, u32[]{:S(2)}, u32[]{:S(2)}) collective-permute-start(bf16[32,8192]{1,0:T(8,128)(2,1)S(1)} %apply_layer.9.refs_1_.refs_9_), channel_id=1, source_target_pairs={{0,4},{4,8},{8,12},{12,16},{16,20},{20,24},{24,28},{28,0},{1,5},{5... | collective-permute-start | bytes 1572872 | tf_op jit(solution)/shard_map/ppermute | solution.py:142
  36.9 4.5 %collective-permute-done.1.refs_0_ = bf16[32,8192]{1,0:T(8,128)(2,1)S(1)} collective-permute-done((bf16[32,8192]{1,0:T(8,128)(2,1)S(1)}, bf16[32,8192]{1,0:T(8,128)(2,1)S(1)}, u32[]{:S(2)}, u32[]{:S(2)}) %collective-permute-start.1) | collective-permute-done | bytes 524320 | tf_op jit(solution)/shard_map/ppermute | solution.py:146
  41.6 0.5 collective-permute-start.10
  42.1 1.0 collective-permute-done.11.refs_4_
  43.1 0.4 collective-permute-done.10.refs_3_
  43.5 3.1 %apply_layer.10.refs_1_.refs_9_ = bf16[32,8192]{1,0:T(8,128)(2,1)S(1)} custom-call(s32[1024]{0:T(1024)S(1)} %fusion.2.refs_4_.place_ref, f32[1]{0:T(128)S(6)} %copy.38.bias_ref, bf16[32,8192]{1,0:T(8,128)(2,1)S(1)} %row_block.5.refs_0_, bf16[32,8192]{1,0:T(8,128)(2,1)S(1)} %tie.15.refs_1_, bf16[128,8192]{1,0:T(8,128)(2,1)S(1)} %collective-permute-done.4.refs_2_, ...), custom_call_target="tpu_custom_call" | custom-call | flops 1 | bytes 1 | tf_op jit(solution)/shard_map/apply_layer/pallas_call | solution.py:127
  46.6 1.8 %collective-permute-start.18 = (bf16[32,8192]{1,0:T(8,128)(2,1)S(1)}, bf16[32,8192]{1,0:T(8,128)(2,1)S(1)}, u32[]{:S(2)}, u32[]{:S(2)}) collective-permute-start(bf16[32,8192]{1,0:T(8,128)(2,1)S(1)} %apply_layer.10.refs_1_.refs_9_), channel_id=1, source_target_pairs={{0,4},{4,8},{8,12},{12,16},{16,20},{20,24},{24,28},{28,0},{1,5},{5... | collective-permute-start | bytes 1572872 | tf_op jit(solution)/shard_map/ppermute | solution.py:142
  48.3 0.5 collective-permute-start.17
  48.9 3.8 %collective-permute-done.refs_0_ = bf16[32,8192]{1,0:T(8,128)(2,1)S(1)} collective-permute-done((bf16[32,8192]{1,0:T(8,128)(2,1)S(1)}, bf16[32,8192]{1,0:T(8,128)(2,1)S(1)}, u32[]{:S(2)}, u32[]{:S(2)}) %collective-permute-start) | collective-permute-done | bytes 524320 | tf_op jit(solution)/shard_map/ppermute | solution.py:146
  52.8 0.5 collective-permute-start.13
  53.4 0.9 collective-permute-done.14.refs_4_
  54.3 0.4 collective-permute-done.13.refs_3_
  54.7 3.1 %apply_layer.11.refs_1_.refs_9_ = bf16[32,8192]{1,0:T(8,128)(2,1)S(1)} custom-call(s32[1024]{0:T(1024)S(1)} %fusion.2.refs_4_.place_ref, f32[1]{0:T(128)S(6)} %copy.38.bias_ref, bf16[32,8192]{1,0:T(8,128)(2,1)S(1)} %row_block.4.refs_0_, bf16[32,8192]{1,0:T(8,128)(2,1)S(1)} %tie.16.refs_1_, bf16[128,8192]{1,0:T(8,128)(2,1)S(1)} %collective-permute-done.4.refs_2_, ...), custom_call_target="tpu_custom_call" | custom-call | flops 1 | bytes 1 | tf_op jit(solution)/shard_map/apply_layer/pallas_call | solution.py:127
  57.8 1.6 %collective-permute-start.15 = (bf16[32,8192]{1,0:T(8,128)(2,1)S(1)}, bf16[32,8192]{1,0:T(8,128)(2,1)S(1)}, u32[]{:S(2)}, u32[]{:S(2)}) collective-permute-start(bf16[32,8192]{1,0:T(8,128)(2,1)S(1)} %apply_layer.11.refs_1_.refs_9_), channel_id=1, source_target_pairs={{0,4},{4,8},{8,12},{12,16},{16,20},{20,24},{24,28},{28,0},{1,5},{5... | collective-permute-start | bytes 1572872 | tf_op jit(solution)/shard_map/ppermute | solution.py:142
  59.4 0.5 collective-permute-start.16
  59.9 4.0 %collective-permute-done.17.refs_0_ = bf16[32,8192]{1,0:T(8,128)(2,1)S(1)} collective-permute-done((bf16[32,8192]{1,0:T(8,128)(2,1)S(1)}, bf16[32,8192]{1,0:T(8,128)(2,1)S(1)}, u32[]{:S(2)}, u32[]{:S(2)}) %collective-permute-start.17) | collective-permute-done | bytes 524320 | tf_op jit(solution)/shard_map/ppermute | solution.py:146
  64.1 0.5 collective-permute-start.20
  64.6 0.9 collective-permute-done.21.refs_4_
  65.9 3.1 %apply_layer.12.refs_1_.refs_9_ = bf16[32,8192]{1,0:T(8,128)(2,1)S(1)} custom-call(s32[1024]{0:T(1024)S(1)} %fusion.2.refs_4_.place_ref, f32[1]{0:T(128)S(6)} %copy.38.bias_ref, bf16[32,8192]{1,0:T(8,128)(2,1)S(1)} %tie.18.refs_0_, bf16[32,8192]{1,0:T(8,128)(2,1)S(1)} %tie.19.refs_1_, bf16[32,8192]{1,0:T(8,128)(2,1)S(1)} %collective-permute-done.19.refs_2_, ...), custom_call_target="tpu_custom_call" | custom-call | flops 1 | bytes 1 | tf_op jit(solution)/shard_map/apply_layer/pallas_call | solution.py:127
  69.1 1.6 %collective-permute-start.27 = (bf16[32,8192]{1,0:T(8,128)(2,1)S(1)}, bf16[32,8192]{1,0:T(8,128)(2,1)S(1)}, u32[]{:S(2)}, u32[]{:S(2)}) collective-permute-start(bf16[32,8192]{1,0:T(8,128)(2,1)S(1)} %apply_layer.12.refs_1_.refs_9_), channel_id=1, source_target_pairs={{0,4},{4,8},{8,12},{12,16},{16,20},{20,24},{24,28},{28,0},{1,5},{5... | collective-permute-start | bytes 1572872 | tf_op jit(solution)/shard_map/ppermute | solution.py:142
  70.6 0.5 collective-permute-start.26
  71.2 4.0 %collective-permute-done.16.refs_0_ = bf16[32,8192]{1,0:T(8,128)(2,1)S(1)} collective-permute-done((bf16[32,8192]{1,0:T(8,128)(2,1)S(1)}, bf16[32,8192]{1,0:T(8,128)(2,1)S(1)}, u32[]{:S(2)}, u32[]{:S(2)}) %collective-permute-start.16) | collective-permute-done | bytes 524320 | tf_op jit(solution)/shard_map/ppermute | solution.py:146
  75.3 0.5 collective-permute-start.23
  75.9 0.9 collective-permute-done.24.refs_4_
  76.8 0.4 collective-permute-done.23.refs_3_
  77.2 3.1 %apply_layer.13.refs_1_.refs_9_ = bf16[32,8192]{1,0:T(8,128)(2,1)S(1)} custom-call(s32[1024]{0:T(1024)S(1)} %fusion.2.refs_4_.place_ref, f32[1]{0:T(128)S(6)} %copy.38.bias_ref, bf16[32,8192]{1,0:T(8,128)(2,1)S(1)} %tie.17.refs_0_, bf16[32,8192]{1,0:T(8,128)(2,1)S(1)} %tie.20.refs_1_, bf16[32,8192]{1,0:T(8,128)(2,1)S(1)} %collective-permute-done.22.refs_2_, ...), custom_call_target="tpu_custom_call" | custom-call | flops 1 | bytes 1 | tf_op jit(solution)/shard_map/apply_layer/pallas_call | solution.py:127
  80.3 1.6 %collective-permute-start.31 = (bf16[32,8192]{1,0:T(8,128)(2,1)S(1)}, bf16[32,8192]{1,0:T(8,128)(2,1)S(1)}, u32[]{:S(2)}, u32[]{:S(2)}) collective-permute-start(bf16[32,8192]{1,0:T(8,128)(2,1)S(1)} %apply_layer.13.refs_1_.refs_9_), channel_id=1, source_target_pairs={{0,4},{4,8},{8,12},{12,16},{16,20},{20,24},{24,28},{28,0},{1,5},{5... | collective-permute-start | bytes 1572872 | tf_op jit(solution)/shard_map/ppermute | solution.py:142
  81.9 0.5 collective-permute-start.25
  82.4 4.0 %collective-permute-done.26.refs_0_ = bf16[32,8192]{1,0:T(8,128)(2,1)S(1)} collective-permute-done((bf16[32,8192]{1,0:T(8,128)(2,1)S(1)}, bf16[32,8192]{1,0:T(8,128)(2,1)S(1)}, u32[]{:S(2)}, u32[]{:S(2)}) %collective-permute-start.26) | collective-permute-done | bytes 524320 | tf_op jit(solution)/shard_map/ppermute | solution.py:146
  86.5 0.5 collective-permute-start.29
  87.1 0.9 collective-permute-done.30.refs_4_
  88.0 0.4 collective-permute-done.29.refs_3_
  88.4 3.1 %apply_layer.14.refs_1_.refs_9_ = bf16[32,8192]{1,0:T(8,128)(2,1)S(1)} custom-call(s32[1024]{0:T(1024)S(1)} %fusion.2.refs_4_.place_ref, f32[1]{0:T(128)S(6)} %copy.38.bias_ref, bf16[32,8192]{1,0:T(8,128)(2,1)S(1)} %tie.22.refs_0_, bf16[32,8192]{1,0:T(8,128)(2,1)S(1)} %tie.23.refs_1_, bf16[32,8192]{1,0:T(8,128)(2,1)S(1)} %collective-permute-done.28.refs_2_, ...), custom_call_target="tpu_custom_call" | custom-call | flops 1 | bytes 1 | tf_op jit(solution)/shard_map/apply_layer/pallas_call | solution.py:127
  91.5 1.8 %collective-permute-start.36 = (bf16[32,8192]{1,0:T(8,128)(2,1)S(1)}, bf16[32,8192]{1,0:T(8,128)(2,1)S(1)}, u32[]{:S(2)}, u32[]{:S(2)}) collective-permute-start(bf16[32,8192]{1,0:T(8,128)(2,1)S(1)} %apply_layer.14.refs_1_.refs_9_), channel_id=1, source_target_pairs={{0,4},{4,8},{8,12},{12,16},{16,20},{20,24},{24,28},{28,0},{1,5},{5... | collective-permute-start | bytes 1572872 | tf_op jit(solution)/shard_map/ppermute | solution.py:142
  93.3 3.6 %collective-permute-done.25.refs_0_ = bf16[32,8192]{1,0:T(8,128)(2,1)S(1)} collective-permute-done((bf16[32,8192]{1,0:T(8,128)(2,1)S(1)}, bf16[32,8192]{1,0:T(8,128)(2,1)S(1)}, u32[]{:S(2)}, u32[]{:S(2)}) %collective-permute-start.25) | collective-permute-done | bytes 524320 | tf_op jit(solution)/shard_map/ppermute | solution.py:146
  96.9 0.4 collective-permute-done.31.refs_2_.refs_0_
  97.4 0.5 collective-permute-start.33
  97.9 1.0 collective-permute-done.34.refs_4_
  99.0 0.4 collective-permute-done.33.refs_3_
  99.3 3.1 %apply_layer.15 = bf16[32,8192]{1,0:T(8,128)(2,1)S(1)} custom-call(s32[1024]{0:T(1024)S(1)} %fusion.2.refs_4_.place_ref, f32[1]{0:T(128)S(6)} %copy.38.bias_ref, bf16[32,8192]{1,0:T(8,128)(2,1)S(1)} %tie.21.refs_0_, bf16[32,8192]{1,0:T(8,128)(2,1)S(1)} %tie.24.refs_1_, bf16[32,8192]{1,0:T(8,128)(2,1)S(1)} %collective-permute-done.32.refs_2_, ...), custom_call_target="tpu_custom_call" | custom-call | flops 1 | bytes 1 | tf_op jit(solution)/shard_map/apply_layer/pallas_call | solution.py:127
  102.4 1.2 collective-permute-start.35
  103.6 0.8 put_rows.4.refs_1_
  104.4 0.8 put_rows.5.refs_1_
  105.3 4.0 %collective-permute-done.36.refs_0_ = bf16[32,8192]{1,0:T(8,128)(2,1)S(1)} collective-permute-done((bf16[32,8192]{1,0:T(8,128)(2,1)S(1)}, bf16[32,8192]{1,0:T(8,128)(2,1)S(1)}, u32[]{:S(2)}, u32[]{:S(2)}) %collective-permute-start.36) | collective-permute-done | bytes 524320 | tf_op jit(solution)/shard_map/ppermute | solution.py:142
  109.3 0.8 put_rows.6.refs_1_
  110.1 9.8 %collective-permute-done.35.refs_0_ = bf16[32,8192]{1,0:T(8,128)(2,1)S(1)} collective-permute-done((bf16[32,8192]{1,0:T(8,128)(2,1)S(1)}, bf16[32,8192]{1,0:T(8,128)(2,1)S(1)}, u32[]{:S(2)}, u32[]{:S(2)}) %collective-permute-start.35) | collective-permute-done | bytes 524320 | tf_op jit(solution)/shard_map/ppermute | solution.py:142
  119.8 0.8 put_rows.7
  (63 shorter events, 2.1 us)
Async XLA Ops:
  0.0 20.4 %collective-permute-start.4 = (bf16[128,8192]{1,0:T(8,128)(2,1)}, bf16[128,8192]{1,0:T(8,128)(2,1)S(1)}, u32[]{:S(2)}, u32[]{:S(2)}) collective-permute-start(bf16[128,8192]{1,0:T(8,128)(2,1)} %array_ref.7), channel_id=1, source_target_pairs={{0,1},{1,0},{2,3},{3,2},{4,5},{5,4},{6,7},{7,6},{8,9},{9,8},{10,11... | collective-permute-start | bytes 6291464 | tf_op jit(solution)/shard_map/ppermute | solution.py:146
  0.5 1.6 %copy-start.1 = (bf16[128,8192]{1,0:T(8,128)(2,1)S(1)}, bf16[128,8192]{1,0:T(8,128)(2,1)}, u32[]{:S(2)}) copy-start(bf16[128,8192]{1,0:T(8,128)(2,1)} %array_ref.7) | copy-start | bytes 6291460
  2.0 2.7 %copy-start.3 = (s32[1,128,8]{1,2,0:T(8,128)S(1)}, s32[1,128,8]{1,2,0:T(8,128)}, u32[]{:S(2)}) copy-start(s32[1,128,8]{1,2,0:T(8,128)} %param.6) | copy-start | bytes 12292
  2.1 15.2 %collective-permute-start.3 = (bf16[32,8192]{1,0:T(8,128)(2,1)S(1)}, bf16[32,8192]{1,0:T(8,128)(2,1)S(1)}, u32[]{:S(2)}, u32[]{:S(2)}) collective-permute-start(bf16[32,8192]{1,0:T(8,128)(2,1)S(1)} %row_block.7.refs_0_), channel_id=1, source_target_pairs={{0,2},{1,3},{2,0},{3,1},{4,6},{5,7},{6,4},{7,5},{8,10},{9,11},{10,... | collective-permute-start | bytes 1572872 | tf_op jit(solution)/shard_map/ppermute | solution.py:146
  5.0 3.4 %copy-start = (bf16[1,128,8,4096]{3,2,1,0:T(8,128)(2,1)S(1)}, bf16[1,128,8,4096]{3,2,1,0:T(8,128)(2,1)}, u32[]{:S(2)}) copy-start(bf16[1,128,8,4096]{3,2,1,0:T(8,128)(2,1)} %param.5) | copy-start | bytes 25165828
  8.4 7.0 %copy-start.2 = (bf16[128,8192]{1,0:T(8,128)(2,1)S(1)}, bf16[128,8192]{1,0:T(8,128)(2,1)}, u32[]{:S(2)}) copy-start(bf16[128,8192]{1,0:T(8,128)(2,1)} %array_ref.7) | copy-start | bytes 6291460
  15.4 14.8 %collective-permute-start.2 = (bf16[32,8192]{1,0:T(8,128)(2,1)S(1)}, bf16[32,8192]{1,0:T(8,128)(2,1)S(1)}, u32[]{:S(2)}, u32[]{:S(2)}) collective-permute-start(bf16[32,8192]{1,0:T(8,128)(2,1)S(1)} %row_block.6.refs_0_), channel_id=1, source_target_pairs={{0,2},{1,3},{2,0},{3,1},{4,6},{5,7},{6,4},{7,5},{8,10},{9,11},{10,... | collective-permute-start | bytes 1572872 | tf_op jit(solution)/shard_map/ppermute | solution.py:146
  17.3 3.1 %collective-permute-start.6 = (bf16[32,4096]{1,0:T(8,128)(2,1)S(1)}, bf16[32,4096]{1,0:T(8,128)(2,1)S(1)}, u32[]{:S(2)}, u32[]{:S(2)}) collective-permute-start(bf16[32,4096]{1,0:T(8,128)(2,1)S(1)} %get-tuple-element.29), channel_id=1, source_target_pairs={{0,1},{1,0},{2,3},{3,2},{4,5},{5,4},{6,7},{7,6},{8,9},{9,8},{10,11... | collective-permute-start | bytes 786440 | tf_op jit(solution)/shard_map/ppermute | solution.py:146
  17.4 3.0 %collective-permute-start.5 = (bf16[32,4096]{1,0:T(8,128)(2,1)S(1)}, bf16[32,4096]{1,0:T(8,128)(2,1)S(1)}, u32[]{:S(2)}, u32[]{:S(2)}) collective-permute-start(bf16[32,4096]{1,0:T(8,128)(2,1)S(1)} %get-tuple-element.30), channel_id=1, source_target_pairs={{0,1},{1,0},{2,3},{3,2},{4,5},{5,4},{6,7},{7,6},{8,9},{9,8},{10,11... | collective-permute-start | bytes 786440 | tf_op jit(solution)/shard_map/ppermute | solution.py:146
  17.9 23.6 %collective-permute-start.1 = (bf16[32,8192]{1,0:T(8,128)(2,1)S(1)}, bf16[32,8192]{1,0:T(8,128)(2,1)S(1)}, u32[]{:S(2)}, u32[]{:S(2)}) collective-permute-start(bf16[32,8192]{1,0:T(8,128)(2,1)S(1)} %row_block.5.refs_0_), channel_id=1, source_target_pairs={{0,2},{1,3},{2,0},{3,1},{4,6},{5,7},{6,4},{7,5},{8,10},{9,11},{10,... | collective-permute-start | bytes 1572872 | tf_op jit(solution)/shard_map/ppermute | solution.py:146
  23.5 18.0 %collective-permute-start.9 = (bf16[32,8192]{1,0:T(8,128)(2,1)S(1)}, bf16[32,8192]{1,0:T(8,128)(2,1)S(1)}, u32[]{:S(2)}, u32[]{:S(2)}) collective-permute-start(bf16[32,8192]{1,0:T(8,128)(2,1)S(1)} %apply_layer.8.refs_1_.refs_9_), channel_id=1, source_target_pairs={{0,4},{4,8},{8,12},{12,16},{16,20},{20,24},{24,28},{28,0},{1,5},{5... | collective-permute-start | bytes 1572872 | tf_op jit(solution)/shard_map/ppermute | solution.py:142
  30.3 1.6 %collective-permute-start.8 = (bf16[32,4096]{1,0:T(8,128)(2,1)S(1)}, bf16[32,4096]{1,0:T(8,128)(2,1)S(1)}, u32[]{:S(2)}, u32[]{:S(2)}) collective-permute-start(bf16[32,4096]{1,0:T(8,128)(2,1)S(1)} %get-tuple-element.27), channel_id=1, source_target_pairs={{0,1},{1,0},{2,3},{3,2},{4,5},{5,4},{6,7},{7,6},{8,9},{9,8},{10,11... | collective-permute-start | bytes 786440 | tf_op jit(solution)/shard_map/ppermute | solution.py:146
  30.3 1.9 %collective-permute-start.7 = (bf16[32,4096]{1,0:T(8,128)(2,1)S(1)}, bf16[32,4096]{1,0:T(8,128)(2,1)S(1)}, u32[]{:S(2)}, u32[]{:S(2)}) collective-permute-start(bf16[32,4096]{1,0:T(8,128)(2,1)S(1)} %get-tuple-element.28), channel_id=1, source_target_pairs={{0,1},{1,0},{2,3},{3,2},{4,5},{5,4},{6,7},{7,6},{8,9},{9,8},{10,11... | collective-permute-start | bytes 786440 | tf_op jit(solution)/shard_map/ppermute | solution.py:146
  30.9 21.8 %collective-permute-start = (bf16[32,8192]{1,0:T(8,128)(2,1)S(1)}, bf16[32,8192]{1,0:T(8,128)(2,1)S(1)}, u32[]{:S(2)}, u32[]{:S(2)}) collective-permute-start(bf16[32,8192]{1,0:T(8,128)(2,1)S(1)} %row_block.4.refs_0_), channel_id=1, source_target_pairs={{0,2},{1,3},{2,0},{3,1},{4,6},{5,7},{6,4},{7,5},{8,10},{9,11},{10,... | collective-permute-start | bytes 1572872 | tf_op jit(solution)/shard_map/ppermute | solution.py:146
  35.3 17.4 %collective-permute-start.12 = (bf16[32,8192]{1,0:T(8,128)(2,1)S(1)}, bf16[32,8192]{1,0:T(8,128)(2,1)S(1)}, u32[]{:S(2)}, u32[]{:S(2)}) collective-permute-start(bf16[32,8192]{1,0:T(8,128)(2,1)S(1)} %apply_layer.9.refs_1_.refs_9_), channel_id=1, source_target_pairs={{0,4},{4,8},{8,12},{12,16},{16,20},{20,24},{24,28},{28,0},{1,5},{5... | collective-permute-start | bytes 1572872 | tf_op jit(solution)/shard_map/ppermute | solution.py:142
  41.5 1.6 %collective-permute-start.11 = (bf16[32,4096]{1,0:T(8,128)(2,1)S(1)}, bf16[32,4096]{1,0:T(8,128)(2,1)S(1)}, u32[]{:S(2)}, u32[]{:S(2)}) collective-permute-start(bf16[32,4096]{1,0:T(8,128)(2,1)S(1)} %get-tuple-element.25), channel_id=1, source_target_pairs={{0,1},{1,0},{2,3},{3,2},{4,5},{5,4},{6,7},{7,6},{8,9},{9,8},{10,11... | collective-permute-start | bytes 786440 | tf_op jit(solution)/shard_map/ppermute | solution.py:146
  41.6 1.9 %collective-permute-start.10 = (bf16[32,4096]{1,0:T(8,128)(2,1)S(1)}, bf16[32,4096]{1,0:T(8,128)(2,1)S(1)}, u32[]{:S(2)}, u32[]{:S(2)}) collective-permute-start(bf16[32,4096]{1,0:T(8,128)(2,1)S(1)} %get-tuple-element.26), channel_id=1, source_target_pairs={{0,1},{1,0},{2,3},{3,2},{4,5},{5,4},{6,7},{7,6},{8,9},{9,8},{10,11... | collective-permute-start | bytes 786440 | tf_op jit(solution)/shard_map/ppermute | solution.py:146
  46.6 17.3 %collective-permute-start.18 = (bf16[32,8192]{1,0:T(8,128)(2,1)S(1)}, bf16[32,8192]{1,0:T(8,128)(2,1)S(1)}, u32[]{:S(2)}, u32[]{:S(2)}) collective-permute-start(bf16[32,8192]{1,0:T(8,128)(2,1)S(1)} %apply_layer.10.refs_1_.refs_9_), channel_id=1, source_target_pairs={{0,4},{4,8},{8,12},{12,16},{16,20},{20,24},{24,28},{28,0},{1,5},{5... | collective-permute-start | bytes 1572872 | tf_op jit(solution)/shard_map/ppermute | solution.py:142
  48.3 15.6 %collective-permute-start.17 = (bf16[32,8192]{1,0:T(8,128)(2,1)S(1)}, bf16[32,8192]{1,0:T(8,128)(2,1)S(1)}, u32[]{:S(2)}, u32[]{:S(2)}) collective-permute-start(bf16[32,8192]{1,0:T(8,128)(2,1)S(1)} %tie.18.refs_0_), channel_id=1, source_target_pairs={{0,2},{1,3},{2,0},{3,1},{4,6},{5,7},{6,4},{7,5},{8,10},{9,11},{10,... | collective-permute-start | bytes 1572872 | tf_op jit(solution)/shard_map/ppermute | solution.py:146
  52.7 1.6 %collective-permute-start.14 = (bf16[32,4096]{1,0:T(8,128)(2,1)S(1)}, bf16[32,4096]{1,0:T(8,128)(2,1)S(1)}, u32[]{:S(2)}, u32[]{:S(2)}) collective-permute-start(bf16[32,4096]{1,0:T(8,128)(2,1)S(1)} %get-tuple-element.23), channel_id=1, source_target_pairs={{0,1},{1,0},{2,3},{3,2},{4,5},{5,4},{6,7},{7,6},{8,9},{9,8},{10,11... | collective-permute-start | bytes 786440 | tf_op jit(solution)/shard_map/ppermute | solution.py:146
  52.8 1.9 %collective-permute-start.13 = (bf16[32,4096]{1,0:T(8,128)(2,1)S(1)}, bf16[32,4096]{1,0:T(8,128)(2,1)S(1)}, u32[]{:S(2)}, u32[]{:S(2)}) collective-permute-start(bf16[32,4096]{1,0:T(8,128)(2,1)S(1)} %get-tuple-element.24), channel_id=1, source_target_pairs={{0,1},{1,0},{2,3},{3,2},{4,5},{5,4},{6,7},{7,6},{8,9},{9,8},{10,11... | collective-permute-start | bytes 786440 | tf_op jit(solution)/shard_map/ppermute | solution.py:146
  53.3 11.2 %collective-permute-start.19 = (bf16[32,8192]{1,0:T(8,128)(2,1)S(1)}, bf16[32,8192]{1,0:T(8,128)(2,1)S(1)}, u32[]{:S(2)}, u32[]{:S(2)}) collective-permute-start(bf16[32,8192]{1,0:T(8,128)(2,1)S(1)} %tie.18.refs_0_), channel_id=1, source_target_pairs={{0,1},{1,0},{2,3},{3,2},{4,5},{5,4},{6,7},{7,6},{8,9},{9,8},{10,11... | collective-permute-start | bytes 1572872 | tf_op jit(solution)/shard_map/ppermute | solution.py:146
  57.8 17.3 %collective-permute-start.15 = (bf16[32,8192]{1,0:T(8,128)(2,1)S(1)}, bf16[32,8192]{1,0:T(8,128)(2,1)S(1)}, u32[]{:S(2)}, u32[]{:S(2)}) collective-permute-start(bf16[32,8192]{1,0:T(8,128)(2,1)S(1)} %apply_layer.11.refs_1_.refs_9_), channel_id=1, source_target_pairs={{0,4},{4,8},{8,12},{12,16},{16,20},{20,24},{24,28},{28,0},{1,5},{5... | collective-permute-start | bytes 1572872 | tf_op jit(solution)/shard_map/ppermute | solution.py:142
  59.4 15.8 %collective-permute-start.16 = (bf16[32,8192]{1,0:T(8,128)(2,1)S(1)}, bf16[32,8192]{1,0:T(8,128)(2,1)S(1)}, u32[]{:S(2)}, u32[]{:S(2)}) collective-permute-start(bf16[32,8192]{1,0:T(8,128)(2,1)S(1)} %tie.17.refs_0_), channel_id=1, source_target_pairs={{0,2},{1,3},{2,0},{3,1},{4,6},{5,7},{6,4},{7,5},{8,10},{9,11},{10,... | collective-permute-start | bytes 1572872 | tf_op jit(solution)/shard_map/ppermute | solution.py:146
  64.0 1.6 %collective-permute-start.21 = (bf16[32,4096]{1,0:T(8,128)(2,1)S(1)}, bf16[32,4096]{1,0:T(8,128)(2,1)S(1)}, u32[]{:S(2)}, u32[]{:S(2)}) collective-permute-start(bf16[32,4096]{1,0:T(8,128)(2,1)S(1)} %get-tuple-element.21), channel_id=1, source_target_pairs={{0,1},{1,0},{2,3},{3,2},{4,5},{5,4},{6,7},{7,6},{8,9},{9,8},{10,11... | collective-permute-start | bytes 786440 | tf_op jit(solution)/shard_map/ppermute | solution.py:146
  64.1 1.9 %collective-permute-start.20 = (bf16[32,4096]{1,0:T(8,128)(2,1)S(1)}, bf16[32,4096]{1,0:T(8,128)(2,1)S(1)}, u32[]{:S(2)}, u32[]{:S(2)}) collective-permute-start(bf16[32,4096]{1,0:T(8,128)(2,1)S(1)} %get-tuple-element.22), channel_id=1, source_target_pairs={{0,1},{1,0},{2,3},{3,2},{4,5},{5,4},{6,7},{7,6},{8,9},{9,8},{10,11... | collective-permute-start | bytes 786440 | tf_op jit(solution)/shard_map/ppermute | solution.py:146
  64.6 11.2 %collective-permute-start.22 = (bf16[32,8192]{1,0:T(8,128)(2,1)S(1)}, bf16[32,8192]{1,0:T(8,128)(2,1)S(1)}, u32[]{:S(2)}, u32[]{:S(2)}) collective-permute-start(bf16[32,8192]{1,0:T(8,128)(2,1)S(1)} %tie.17.refs_0_), channel_id=1, source_target_pairs={{0,1},{1,0},{2,3},{3,2},{4,5},{5,4},{6,7},{7,6},{8,9},{9,8},{10,11... | collective-permute-start | bytes 1572872 | tf_op jit(solution)/shard_map/ppermute | solution.py:146
  69.1 17.3 %collective-permute-start.27 = (bf16[32,8192]{1,0:T(8,128)(2,1)S(1)}, bf16[32,8192]{1,0:T(8,128)(2,1)S(1)}, u32[]{:S(2)}, u32[]{:S(2)}) collective-permute-start(bf16[32,8192]{1,0:T(8,128)(2,1)S(1)} %apply_layer.12.refs_1_.refs_9_), channel_id=1, source_target_pairs={{0,4},{4,8},{8,12},{12,16},{16,20},{20,24},{24,28},{28,0},{1,5},{5... | collective-permute-start | bytes 1572872 | tf_op jit(solution)/shard_map/ppermute | solution.py:142
  70.6 15.8 %collective-permute-start.26 = (bf16[32,8192]{1,0:T(8,128)(2,1)S(1)}, bf16[32,8192]{1,0:T(8,128)(2,1)S(1)}, u32[]{:S(2)}, u32[]{:S(2)}) collective-permute-start(bf16[32,8192]{1,0:T(8,128)(2,1)S(1)} %tie.22.refs_0_), channel_id=1, source_target_pairs={{0,2},{1,3},{2,0},{3,1},{4,6},{5,7},{6,4},{7,5},{8,10},{9,11},{10,... | collective-permute-start | bytes 1572872 | tf_op jit(solution)/shard_map/ppermute | solution.py:146
  75.2 1.6 %collective-permute-start.24 = (bf16[32,4096]{1,0:T(8,128)(2,1)S(1)}, bf16[32,4096]{1,0:T(8,128)(2,1)S(1)}, u32[]{:S(2)}, u32[]{:S(2)}) collective-permute-start(bf16[32,4096]{1,0:T(8,128)(2,1)S(1)} %get-tuple-element.19), channel_id=1, source_target_pairs={{0,1},{1,0},{2,3},{3,2},{4,5},{5,4},{6,7},{7,6},{8,9},{9,8},{10,11... | collective-permute-start | bytes 786440 | tf_op jit(solution)/shard_map/ppermute | solution.py:146
  75.3 1.9 %collective-permute-start.23 = (bf16[32,4096]{1,0:T(8,128)(2,1)S(1)}, bf16[32,4096]{1,0:T(8,128)(2,1)S(1)}, u32[]{:S(2)}, u32[]{:S(2)}) collective-permute-start(bf16[32,4096]{1,0:T(8,128)(2,1)S(1)} %get-tuple-element.20), channel_id=1, source_target_pairs={{0,1},{1,0},{2,3},{3,2},{4,5},{5,4},{6,7},{7,6},{8,9},{9,8},{10,11... | collective-permute-start | bytes 786440 | tf_op jit(solution)/shard_map/ppermute | solution.py:146
  75.8 11.2 %collective-permute-start.28 = (bf16[32,8192]{1,0:T(8,128)(2,1)S(1)}, bf16[32,8192]{1,0:T(8,128)(2,1)S(1)}, u32[]{:S(2)}, u32[]{:S(2)}) collective-permute-start(bf16[32,8192]{1,0:T(8,128)(2,1)S(1)} %tie.22.refs_0_), channel_id=1, source_target_pairs={{0,1},{1,0},{2,3},{3,2},{4,5},{5,4},{6,7},{7,6},{8,9},{9,8},{10,11... | collective-permute-start | bytes 1572872 | tf_op jit(solution)/shard_map/ppermute | solution.py:146
  80.3 17.0 %collective-permute-start.31 = (bf16[32,8192]{1,0:T(8,128)(2,1)S(1)}, bf16[32,8192]{1,0:T(8,128)(2,1)S(1)}, u32[]{:S(2)}, u32[]{:S(2)}) collective-permute-start(bf16[32,8192]{1,0:T(8,128)(2,1)S(1)} %apply_layer.13.refs_1_.refs_9_), channel_id=1, source_target_pairs={{0,4},{4,8},{8,12},{12,16},{16,20},{20,24},{24,28},{28,0},{1,5},{5... | collective-permute-start | bytes 1572872 | tf_op jit(solution)/shard_map/ppermute | solution.py:142
  81.9 15.1 %collective-permute-start.25 = (bf16[32,8192]{1,0:T(8,128)(2,1)S(1)}, bf16[32,8192]{1,0:T(8,128)(2,1)S(1)}, u32[]{:S(2)}, u32[]{:S(2)}) collective-permute-start(bf16[32,8192]{1,0:T(8,128)(2,1)S(1)} %tie.21.refs_0_), channel_id=1, source_target_pairs={{0,2},{1,3},{2,0},{3,1},{4,6},{5,7},{6,4},{7,5},{8,10},{9,11},{10,... | collective-permute-start | bytes 1572872 | tf_op jit(solution)/shard_map/ppermute | solution.py:146
  86.4 1.6 %collective-permute-start.30 = (bf16[32,4096]{1,0:T(8,128)(2,1)S(1)}, bf16[32,4096]{1,0:T(8,128)(2,1)S(1)}, u32[]{:S(2)}, u32[]{:S(2)}) collective-permute-start(bf16[32,4096]{1,0:T(8,128)(2,1)S(1)} %get-tuple-element.17), channel_id=1, source_target_pairs={{0,1},{1,0},{2,3},{3,2},{4,5},{5,4},{6,7},{7,6},{8,9},{9,8},{10,11... | collective-permute-start | bytes 786440 | tf_op jit(solution)/shard_map/ppermute | solution.py:146
  86.5 1.9 %collective-permute-start.29 = (bf16[32,4096]{1,0:T(8,128)(2,1)S(1)}, bf16[32,4096]{1,0:T(8,128)(2,1)S(1)}, u32[]{:S(2)}, u32[]{:S(2)}) collective-permute-start(bf16[32,4096]{1,0:T(8,128)(2,1)S(1)} %get-tuple-element.18), channel_id=1, source_target_pairs={{0,1},{1,0},{2,3},{3,2},{4,5},{5,4},{6,7},{7,6},{8,9},{9,8},{10,11... | collective-permute-start | bytes 786440 | tf_op jit(solution)/shard_map/ppermute | solution.py:146
  87.0 10.9 %collective-permute-start.32 = (bf16[32,8192]{1,0:T(8,128)(2,1)S(1)}, bf16[32,8192]{1,0:T(8,128)(2,1)S(1)}, u32[]{:S(2)}, u32[]{:S(2)}) collective-permute-start(bf16[32,8192]{1,0:T(8,128)(2,1)S(1)} %tie.21.refs_0_), channel_id=1, source_target_pairs={{0,1},{1,0},{2,3},{3,2},{4,5},{5,4},{6,7},{7,6},{8,9},{9,8},{10,11... | collective-permute-start | bytes 1572872 | tf_op jit(solution)/shard_map/ppermute | solution.py:146
  91.5 17.7 %collective-permute-start.36 = (bf16[32,8192]{1,0:T(8,128)(2,1)S(1)}, bf16[32,8192]{1,0:T(8,128)(2,1)S(1)}, u32[]{:S(2)}, u32[]{:S(2)}) collective-permute-start(bf16[32,8192]{1,0:T(8,128)(2,1)S(1)} %apply_layer.14.refs_1_.refs_9_), channel_id=1, source_target_pairs={{0,4},{4,8},{8,12},{12,16},{16,20},{20,24},{24,28},{28,0},{1,5},{5... | collective-permute-start | bytes 1572872 | tf_op jit(solution)/shard_map/ppermute | solution.py:142
  97.4 1.6 %collective-permute-start.34 = (bf16[32,4096]{1,0:T(8,128)(2,1)S(1)}, bf16[32,4096]{1,0:T(8,128)(2,1)S(1)}, u32[]{:S(2)}, u32[]{:S(2)}) collective-permute-start(bf16[32,4096]{1,0:T(8,128)(2,1)S(1)} %get-tuple-element.15), channel_id=1, source_target_pairs={{0,1},{1,0},{2,3},{3,2},{4,5},{5,4},{6,7},{7,6},{8,9},{9,8},{10,11... | collective-permute-start | bytes 786440 | tf_op jit(solution)/shard_map/ppermute | solution.py:146
  97.4 1.9 %collective-permute-start.33 = (bf16[32,4096]{1,0:T(8,128)(2,1)S(1)}, bf16[32,4096]{1,0:T(8,128)(2,1)S(1)}, u32[]{:S(2)}, u32[]{:S(2)}) collective-permute-start(bf16[32,4096]{1,0:T(8,128)(2,1)S(1)} %get-tuple-element.16), channel_id=1, source_target_pairs={{0,1},{1,0},{2,3},{3,2},{4,5},{5,4},{6,7},{7,6},{8,9},{9,8},{10,11... | collective-permute-start | bytes 786440 | tf_op jit(solution)/shard_map/ppermute | solution.py:146
  102.4 17.4 %collective-permute-start.35 = (bf16[32,8192]{1,0:T(8,128)(2,1)S(1)}, bf16[32,8192]{1,0:T(8,128)(2,1)S(1)}, u32[]{:S(2)}, u32[]{:S(2)}) collective-permute-start(bf16[32,8192]{1,0:T(8,128)(2,1)S(1)} %apply_layer.15), channel_id=1, source_target_pairs={{0,4},{4,8},{8,12},{12,16},{16,20},{20,24},{24,28},{28,0},{1,5},{5... | collective-permute-start | bytes 1572872 | tf_op jit(solution)/shard_map/ppermute | solution.py:142
